TPU v7x, 32 devices: a whole 2x2x4 slice. The times are simulated.
32 devices in a mesh: grp: 4 (over y, core), row: 8 (over z, x).
Axes of the slice: x: 2, y: 2, z: 4, core: 2. Of those that a mesh axis runs over, the one named last changes fastest.
Arguments:
- features: bfloat16 [65536, 256], P(('grp', 'row')), may hold values from -6 to 6
- cotangent: bfloat16 [65536, 256], P(('grp', 'row')), may hold values from -6 to 6
- self_weight: bfloat16 [256, 256], replicated, may hold values from -0.375 to 0.375
- neighbor_weight: bfloat16 [256, 256], replicated, may hold values from -0.375 to 0.375
- tile_values: bfloat16 [32, 64, 128, 128], P(('grp', 'row')), may hold values from 0 to 1
- tile_index: int32 [32, 64, 2], P(('grp', 'row')), may hold values from 0 to 15
- hub_adjacency: bfloat16 [65536, 1024], P(('grp', 'row')), may hold values from 0 to 1
- hub_owner: int32 [4, 8], P('grp'), may hold values from 0 to 7
- send_rows: int32 [32, 4, 64], P(('grp', 'row')), may hold values from 0 to 2047
- cut_adjacency: bfloat16 [65536, 256], P(('grp', 'row')), may hold values from 0 to 1
- degrees: int32 [65536], P(('grp', 'row')), may hold values from 896 to 1791
Outputs:
- hidden: bfloat16 [65536, 256], P(('grp', 'row'))
- grad_features: bfloat16 [65536, 256], P(('grp', 'row'))
- grad_self: float32 [256, 256], replicated
- grad_neighbor: float32 [256, 256], replicated
Inputs may be any that keep to these rules, and one draw needn't show every extreme that they name: `send_rows`: rows may repeat.
All inputs are finite; a program needn't handle non-finite values.
Results may differ from a plain program's by a relative error of at most 0.014.
Values may be sent and summed in bfloat16 or wider, within the bound.
No kernel may reach another device: no remote copies, remote signals or barrier semaphores. Data moves between devices by JAX's collectives and lax.ppermute only.
A program may use at most 128 MiB of HBM per device.

v0:
```python
import jax
import jax.numpy as jnp
from jax import lax
from jax.sharding import PartitionSpec as P

TILE = 128
HUB = 128


def spread(value, axis, root):
    mine = lax.axis_index(axis) == root
    return lax.psum(jnp.where(mine, value, jnp.zeros_like(value)), axis)


def on_device(
    features,
    cotangent,
    self_weight,
    neighbor_weight,
    tile_values,
    tile_index,
    hub_adjacency,
    hub_owner,
    send_rows,
    cut_adjacency,
    degrees,
):
    node_count, width = features.shape
    tile_total = node_count // TILE
    group_count = lax.axis_size("grp")
    section_count = hub_owner.shape[1]
    values = tile_values[0]
    index = tile_index[0]
    owners = hub_owner[0]
    blocks = features.reshape(tile_total, TILE, width)
    row_select = (index[:, 0][None, :] == jnp.arange(tile_total)[:, None]).astype(jnp.float32)
    col_select = (index[:, 1][None, :] == jnp.arange(tile_total)[:, None]).astype(jnp.float32)
    picked = blocks[index[:, 1]]
    product = jnp.einsum("lab,lbf->laf", values, picked, preferred_element_type=jnp.float32)
    local_sum = jnp.einsum(
        "nl,laf->naf", row_select, product, precision=lax.Precision.HIGHEST
    ).reshape(node_count, width)
    heads = features[:HUB]
    hub_sum = jnp.zeros((node_count, width), jnp.float32)
    for section in range(section_count):
        panel = spread(heads, "row", owners[section])
        hub_sum = hub_sum + jnp.dot(
            hub_adjacency[:, section * HUB : (section + 1) * HUB],
            panel,
            preferred_element_type=jnp.float32,
        )
    outgoing = features[send_rows[0]]
    arrived = lax.all_to_all(outgoing, "grp", split_axis=0, concat_axis=0, tiled=True)
    cut_sum = jnp.dot(
        cut_adjacency,
        arrived.reshape(group_count * outgoing.shape[1], width),
        preferred_element_type=jnp.float32,
    )
    scaling = lax.rsqrt(degrees.astype(jnp.float32))[:, None]
    aggregated = ((local_sum + hub_sum + cut_sum) * scaling).astype(jnp.bfloat16)
    before = jnp.dot(features, self_weight, preferred_element_type=jnp.float32) + jnp.dot(
        aggregated, neighbor_weight, preferred_element_type=jnp.float32
    )
    activated, pullback = jax.vjp(jax.nn.gelu, before)
    hidden = activated.astype(jnp.bfloat16)
    grad_before = pullback(cotangent.astype(jnp.float32))[0].astype(jnp.bfloat16)
    rows_dims = (((0,), (0,)), ((), ()))
    cols_dims = (((1,), (1,)), ((), ()))
    self_part = lax.dot_general(
        features, grad_before, rows_dims, preferred_element_type=jnp.float32
    )
    neighbor_part = lax.dot_general(
        aggregated, grad_before, rows_dims, preferred_element_type=jnp.float32
    )
    grad_self, grad_neighbor = lax.psum((self_part, neighbor_part), ("grp", "row"))
    grad_aggregate = (
        lax.dot_general(grad_before, neighbor_weight, cols_dims, preferred_element_type=jnp.float32)
        * scaling
    ).astype(jnp.bfloat16)
    grad_total = lax.dot_general(
        grad_before, self_weight, cols_dims, preferred_element_type=jnp.float32
    )
    agg_blocks = grad_aggregate.reshape(tile_total, TILE, width)[index[:, 0]]
    returned = jnp.einsum("lab,laf->lbf", values, agg_blocks, preferred_element_type=jnp.float32)
    grad_total = grad_total + jnp.einsum(
        "nl,lbf->nbf", col_select, returned, precision=lax.Precision.HIGHEST
    ).reshape(node_count, width)
    hub_terms = lax.dot_general(
        hub_adjacency, grad_aggregate, rows_dims, preferred_element_type=jnp.float32
    ).reshape(section_count, HUB, width)
    totals = lax.psum(hub_terms.astype(jnp.bfloat16), "row").astype(jnp.float32)
    owned = (owners == lax.axis_index("row")).astype(jnp.float32)
    hub_grad = jnp.einsum("s,shf->hf", owned, totals, precision=lax.Precision.HIGHEST)
    grad_total = grad_total.at[:HUB].add(hub_grad)
    back_rows = lax.dot_general(
        cut_adjacency, grad_aggregate, rows_dims, preferred_element_type=jnp.float32
    ).astype(jnp.bfloat16)
    back_rows = back_rows.reshape(group_count, -1, width)
    returned_rows = lax.all_to_all(back_rows, "grp", split_axis=0, concat_axis=0, tiled=True)
    scatter_table = (send_rows[0].reshape(-1)[None, :] == jnp.arange(node_count)[:, None]).astype(
        jnp.bfloat16
    )
    grad_total = grad_total + jnp.dot(
        scatter_table, returned_rows.reshape(-1, width), preferred_element_type=jnp.float32
    )
    return (hidden, grad_total.astype(jnp.bfloat16), grad_self, grad_neighbor)


def solution(mesh):
    in_specs = (
        P(("grp", "row"), None),
        P(("grp", "row"), None),
        P(),
        P(),
        P(("grp", "row"), None, None, None),
        P(("grp", "row"), None, None),
        P(("grp", "row"), None),
        P("grp", None),
        P(("grp", "row"), None, None),
        P(("grp", "row"), None),
        P(("grp", "row")),
    )
    out_specs = (P(("grp", "row"), None), P(("grp", "row"), None), P(), P())
    return jax.shard_map(
        on_device, mesh=mesh, in_specs=in_specs, out_specs=out_specs, check_vma=False
    )
```

profile of v0, /device:TPU:0, one launch (start us, length us, event | category | flops | bytes accessed | tf_op | source)
XLA Modules:
  0.0 366.1 jit_solution(6832768031318857833)
XLA Ops:
  7.2 0.8 compare_select_fusion
  8.1 3.0 gather_fusion.1
  11.2 4.2 %all-to-all-start = ((bf16[4,64,256]{2,1,0:T(8,128)(2,1)}), bf16[4,64,256]{2,1,0:T(8,128)(2,1)S(1)}, u32[]{:S(2)}, u32[]{:S(2)}) async-start(bf16[4,64,256]{2,1,0:T(8,128)(2,1)} %bitcast.18), calls=%async_computation | async-start | bytes 262144 | tf_op jit(solution)/shard_map/all_to_all | solution.py:53
  15.4 1.6 fusion.49
  22.1 1.6 broadcast_select_fusion
  23.9 0.6 slice_bitcast_fusion
  24.5 2.8 gather_fusion
  27.3 6.8 %fusion.23 = f32[64,256,128]{2,1,0:T(8,128)} fusion(bf16[64,128,256]{2,1,0:T(8,128)(2,1)} %gather_fusion, bf16[1,64,128,128]{3,2,1,0:T(8,128)(2,1)S(1)} %copy-done), kind=kOutput, calls=%fused_computation.42 | convolution fusion | flops 536870912 | bytes 14680064 | tf_op jit(solution)/shard_map/lab,lbf->laf/dot_general | solution.py:39
  34.0 9.2 %copy.24 = f32[64,256,128]{1,0,2:T(8,128)} copy(f32[64,256,128]{2,1,0:T(8,128)} %fusion.23) | data formatting | bytes 16777216 | tf_op jit(solution)/shard_map/lab,lbf->laf/dot_general | solution.py:39
  43.3 5.2 %fusion.2 = f32[16,128,256]{2,0,1:T(8,128)S(1)} fusion(f32[64,256,128]{1,0,2:T(8,128)} %copy.24, s32[64]{0:T(128)S(1)} %get-tuple-element.47), kind=kOutput, calls=%fused_computation.5 | convolution fusion | flops 402654208 | bytes 10486016 | tf_op jit(solution)/shard_map/nl,laf->naf/dot_general | solution.py:40
  48.4 2.6 copy.18
  51.0 2.9 copy.19
  54.0 1.8 fusion.50
  55.8 44.9 %all-reduce.10.cloned.1.call-done = (bf16[128,256]{1,0:T(8,128)(2,1)}, bf16[128,256]{1,0:T(8,128)(2,1)}, bf16[128,256]{1,0:T(8,128)(2,1)}, bf16[128,256]{1,0:T(8...) async-done(((bf16[128,256]{1,0:T(8,128)(2,1)}, bf16[128,256]{1,0:T(8,128)(2,1)}, ...) | async-done | bytes 524304 | tf_op jit(solution)/shard_map/psum | solution.py:12
  100.6 1.6 fusion.34
  102.2 1.6 convolution_add_fusion.9
  103.9 0.7 copy-done.6
  104.6 0.5 convolution_add_fusion.8
  105.4 0.5 convolution_add_fusion.7
  105.9 0.4 copy-done.14
  106.3 0.5 convolution_add_fusion.6
  107.1 0.5 convolution_add_fusion.5
  107.9 0.5 convolution_add_fusion.4
  108.4 1.1 copy-done.5
  109.5 1.8 fusion.7
  111.4 2.5 fusion.8
  114.2 3.0 fusion.13
  117.2 1.1 fusion.51
  118.3 1.2 convolution_bitcast_fusion.1
  119.5 2.7 fusion.9
  122.2 1.7 copy.28
  123.9 2.8 gather_fusion.2
  126.7 6.8 %fusion.21 = f32[64,256,128]{2,1,0:T(8,128)} fusion(bf16[64,128,256]{2,1,0:T(8,128)(2,1)} %gather_fusion.2, bf16[1,64,128,128]{3,2,1,0:T(8,128)(2,1)S(1)} %copy-done), kind=kOutput, calls=%fused_computation.40 | convolution fusion | flops 536870912 | bytes 14680064 | tf_op jit(solution)/shard_map/lab,laf->lbf/dot_general | solution.py:84
  133.5 9.2 %copy.26 = f32[64,256,128]{1,0,2:T(8,128)} copy(f32[64,256,128]{2,1,0:T(8,128)} %fusion.21) | data formatting | bytes 16777216 | tf_op jit(solution)/shard_map/lab,laf->lbf/dot_general | solution.py:84
  142.6 5.2 %fusion = f32[16,128,256]{2,0,1:T(8,128)S(1)} fusion(f32[64,256,128]{1,0,2:T(8,128)} %copy.26, s32[64]{0:T(128)S(1)} %copy-done.21), kind=kOutput, calls=%fused_computation.3 | convolution fusion | flops 402654208 | bytes 10486016 | tf_op jit(solution)/shard_map/nl,lbf->nbf/dot_general | solution.py:85
  147.8 2.6 copy.22
  150.5 3.4 fusion.25
  153.9 0.9 copy.29
  154.9 2.7 convolution_convert_fusion.1
  157.6 3.3 all-to-all-start.1
  161.0 3.4 convolution_add_fusion.1
  164.4 113.5 %all-reduce.8.cloned.1.call-done = (f32[256,256]{0,1:T(8,128)}, f32[256,256]{1,0:T(8,128)}) async-done(((f32[256,256]{0,1:T(8,128)}, f32[256,256]{1,0:T(8,128)}), (f32[256,256]{0,1:T(8,128)}, f32[256,256]{1,0:T(8,128)})) %all-reduce.8.cloned.1.call-update) | async-done | bytes 524304 | tf_op jit(solution)/shard_map/psum | solution.py:75
  277.9 1.8 copy.23
  279.7 73.1 %all-reduce.6.cloned.1.call-done = bf16[8,128,256]{1,0,2:T(8,128)(2,1)} async-done(((bf16[8,128,256]{1,0,2:T(8,128)(2,1)}), bf16[8,128,256]{1,0,2:T(8,128)(2,1)}) %all-reduce.6.cloned.1.call-update) | async-done | bytes 524304 | tf_op jit(solution)/shard_map/psum | solution.py:91
  352.7 1.3 fusion.43
  354.2 1.6 fusion.36
  355.8 3.1 fusion.10
  358.9 0.7 copy.42
  (59 shorter events, 1.9 us)
Async XLA Ops:
  7.2 20.1 %copy-start = (bf16[1,64,128,128]{3,2,1,0:T(8,128)(2,1)S(1)}, bf16[1,64,128,128]{3,2,1,0:T(8,128)(2,1)}, u32[]{:S(2)}) copy-start(bf16[1,64,128,128]{3,2,1,0:T(8,128)(2,1)} %param.17) | copy-start | bytes 6291460
  7.2 16.6 %copy-start.20 = (s32[1,4,64]{2,1,0:T(4,128)S(1)}, s32[1,4,64]{2,1,0:T(4,128)}, u32[]{:S(2)}) copy-start(s32[1,4,64]{2,1,0:T(4,128)} %param.21) | copy-start | bytes 3076
  7.2 17.3 %copy-start.1 = (bf16[2048,256]{1,0:T(8,128)(2,1)S(1)}, bf16[2048,256]{1,0:T(8,128)(2,1)}, u32[]{:S(2)}) copy-start(bf16[2048,256]{1,0:T(8,128)(2,1)} %param.13) | copy-start | bytes 3145732
  7.2 16.7 %copy-start.22 = (s32[1,64,2]{1,2,0:T(2,128)S(1)}, s32[1,64,2]{1,2,0:T(2,128)}, u32[]{:S(2)}) copy-start(s32[1,64,2]{1,2,0:T(2,128)} %param.18) | copy-start | bytes 1540
  11.2 100.2 %all-to-all-start = ((bf16[4,64,256]{2,1,0:T(8,128)(2,1)}), bf16[4,64,256]{2,1,0:T(8,128)(2,1)S(1)}, u32[]{:S(2)}, u32[]{:S(2)}) async-start(bf16[4,64,256]{2,1,0:T(8,128)(2,1)} %bitcast.18), calls=%async_computation | async-start | bytes 262144 | tf_op jit(solution)/shard_map/all_to_all | solution.py:53
  15.4 85.2 %all-reduce.10.cloned.1.call-start = ((), (), s32[]{:S(2)}) async-start(), calls=%async_computation.4 | async-start | bytes 1048576 | tf_op jit(solution)/shard_map/psum | solution.py:12
  23.7 254.2 %all-reduce.8.cloned.1.call-start = ((), (), s32[]{:S(2)}) async-start(), calls=%async_computation.3 | async-start | bytes 1048576 | tf_op jit(solution)/shard_map/psum | solution.py:75
  51.0 2.9 copy-start.19
  51.0 3.0 copy-start.8
  100.6 1.6 copy-start.17
  102.2 2.4 copy-start.6
  102.2 2.4 copy-start.16
  104.6 0.8 copy-start.15
  105.4 0.8 copy-start.14
  106.3 0.8 copy-start.13
  107.1 0.8 copy-start.12
  107.9 1.6 copy-start.5
  107.9 1.6 copy-start.11
  111.3 2.6 copy-start.7
  111.3 2.6 copy-start.10
  111.3 2.8 copy-start.23
  117.2 1.1 copy-start.2
  133.5 9.2 %copy-start.21 = (s32[64]{0:T(128)S(1)}, s32[64]{0:T(128)}, u32[]{:S(2)}) copy-start(s32[64]{0:T(128)} %get-tuple-element.44) | copy-start | bytes 772
  147.8 2.7 copy-start.4
  150.4 202.3 %all-reduce.6.cloned.1.call-start = ((), (), s32[]{:S(2)}) async-start(), calls=%async_computation.2 | async-start | bytes 1048576 | tf_op jit(solution)/shard_map/psum | solution.py:91
  153.9 7.0 %copy-start.3 = (bf16[2048,256]{1,0:T(8,128)(2,1)S(1)}, bf16[2048,256]{1,0:T(8,128)(2,1)}, u32[]{:S(2)}) copy-start(bf16[2048,256]{1,0:T(8,128)(2,1)} %copy-done.2) | copy-start | bytes 3145732
  157.6 198.2 %all-to-all-start.1 = ((bf16[4,64,256]{2,1,0:T(8,128)(2,1)}), bf16[4,64,256]{2,1,0:T(8,128)(2,1)S(1)}, u32[]{:S(2)}, u32[]{:S(2)}) async-start(bf16[4,64,256]{2,1,0:T(8,128)(2,1)} %bitcast.32), calls=%async_computation.1 | async-start | bytes 262144 | tf_op jit(solution)/shard_map/all_to_all | solution.py:99
  161.0 191.8 %copy-start.18 = (s32[1,8]{1,0:T(1,128)S(1)}, s32[1,8]{1,0:T(1,128)}, u32[]{:S(2)}) copy-start(s32[1,8]{1,0:T(1,128)} %param.20) | copy-start | bytes 100
  354.1 4.8 %copy-start.9 = (f32[256,256]{1,0:T(8,128)S(1)}, f32[256,256]{1,0:T(8,128)}, u32[]{:S(2)}) copy-start(f32[256,256]{1,0:T(8,128)} %get-tuple-element.61) | copy-start | bytes 786436
Sparse Core Ops, SparseCore 0:
  23.9 76.7 all-reduce.9
  150.5 127.3 all-reduce.7
  281.3 71.3 all-reduce.5
where the time goes:
time: 367 us; the launch traced here: 366 us
  waiting for transfers between devices  232 us (63%)
  matrix products  57.5 us (16%)
  local copies, waits for them, and re-layouts  45.7 us (12%)
  between operations  19.1 us (5%)
  starting transfers between devices  7.64 us (2%)
  other arithmetic  4.64 us (1%)
    psum x1, waiting for transfers between devices, on_device(): lax.psum((self_part, neighbor_part), ('grp', 'row'))  114 us
    psum x1, waiting for transfers between devices, on_device(): totals = lax.psum(hub_terms.astype(jnp.bfloat16), 'row').astype(jnp.float32)  73.1 us
    psum x1, waiting for transfers between devices, spread(): return lax.psum(jnp.where(mine, value, jnp.zeros_like(value)), axis)  44.9 us
    dot_general x1, local copies, waits for them, and re-layouts, on_device(): jnp.einsum('lab,lbf->laf', values, picked, preferred_element_type=jnp.flo...  9.21 us
    dot_general x1, local copies, waits for them, and re-layouts, on_device(): jnp.einsum('lab,laf->lbf', values, agg_blocks, preferred_element_type=jnp...  9.18 us
    dot_general x8, matrix products, on_device(): jnp.dot(hub_adjacency[:, section * HUB:(section + 1) * HUB], panel, prefe...  7.36 us
  transfers between devices with their start and end apart: 5, of which 3 were waited for; matrix products, arithmetic and copies ran while one was open for 16% of the time, Pallas kernels for 0%

commit v1 on v0

v1 whole, which is shorter than its diff:
```python
import jax
import jax.numpy as jnp
from jax import lax
from jax.experimental import pallas as pl
from jax.experimental.pallas import tpu as pltpu
from jax.sharding import PartitionSpec as P

TILE = 128
HUB = 128
CHUNK = 256
TILE_STEP = 8
VMEM_LIMIT = 48 * 2**20
ROWS = (((0,), (0,)), ((), ()))
COLS = (((1,), (1,)), ((), ()))
F32 = jnp.float32
BF16 = jnp.bfloat16


def params():
    return pltpu.CompilerParams(
        dimension_semantics=("arbitrary",), vmem_limit_bytes=VMEM_LIMIT
    )


def cost(flops, bytes_accessed):
    return pl.CostEstimate(flops=flops, bytes_accessed=bytes_accessed, transcendentals=0)


def dot(a, b, dims=(((1,), (0,)), ((), ()))):
    return lax.dot_general(a, b, dims, preferred_element_type=F32)


def whole(shape):
    return pl.BlockSpec(shape, lambda i, *_: (0,) * len(shape))


def rows_of(step, width):
    return pl.BlockSpec((step, width), lambda i, *_: (i, 0))


def pick_kernel(rows_ref, features_ref, out_ref):
    count = features_ref.shape[0]
    where = lax.broadcasted_iota(jnp.int32, (rows_ref.shape[0], count), 1)
    table = jnp.where(where == rows_ref[...], 1.0, 0.0).astype(BF16)
    out_ref[...] = dot(table, features_ref[...]).astype(BF16)


def pick_rows(rows, features):
    picks = rows.shape[0]
    count, width = features.shape
    step = 128
    return pl.pallas_call(
        pick_kernel,
        grid=(picks // step,),
        in_specs=[rows_of(step, 1), whole((count, width))],
        out_specs=rows_of(step, width),
        out_shape=jax.ShapeDtypeStruct((picks, width), BF16),
        compiler_params=params(),
        cost_estimate=cost(2 * picks * count * width, 2 * count * width),
        name="pick_rows",
    )(rows, features)


def local_kernel(index_ref, values_ref, features_ref, out_ref):
    step = pl.program_id(0)

    @pl.when(step == 0)
    def _():
        out_ref[...] = jnp.zeros_like(out_ref)

    for t in range(TILE_STEP):
        at = step * TILE_STEP + t
        row = pl.ds(pl.multiple_of(index_ref[at, 0] * TILE, TILE), TILE)
        col = pl.ds(pl.multiple_of(index_ref[at, 1] * TILE, TILE), TILE)
        out_ref[row, :] += dot(values_ref[t], features_ref[col, :])


def local_forward(index, values, features):
    tiles = values.shape[0]
    count, width = features.shape
    return pl.pallas_call(
        local_kernel,
        grid_spec=pltpu.PrefetchScalarGridSpec(
            num_scalar_prefetch=1,
            grid=(tiles // TILE_STEP,),
            in_specs=[
                pl.BlockSpec((TILE_STEP, TILE, TILE), lambda i, *_: (i, 0, 0)),
                whole((count, width)),
            ],
            out_specs=whole((count, width)),
        ),
        out_shape=jax.ShapeDtypeStruct((count, width), F32),
        compiler_params=params(),
        cost_estimate=cost(2 * tiles * TILE * TILE * width, 2 * values.size + 6 * features.size),
        name="local_forward",
    )(index, values, features)


def forward_kernel(
    owner_ref,
    hub_ref,
    heads_ref,
    cut_ref,
    arrived_ref,
    local_ref,
    scale_ref,
    features_ref,
    cotangent_ref,
    self_ref,
    neighbor_ref,
    hidden_ref,
    grad_ref,
    weights_ref,
    panels,
    total,
):
    step = pl.program_id(0)
    sections = panels.shape[0] // HUB
    width = features_ref.shape[1]

    @pl.when(step == 0)
    def _():
        total[...] = jnp.zeros_like(total)
        for s in range(sections):
            panels[s * HUB : (s + 1) * HUB, :] = heads_ref[owner_ref[s]]

    summed = dot(hub_ref[...], panels[...]) + dot(cut_ref[...], arrived_ref[...]) + local_ref[...]
    aggregated = (summed * scale_ref[...]).astype(BF16)
    features = features_ref[...]
    before = dot(features, self_ref[...]) + dot(aggregated, neighbor_ref[...])
    root = 0.7978845608028654
    square = before * before
    bend = jnp.tanh(root * before * (1.0 + 0.044715 * square))
    half = 0.5 + 0.5 * bend
    hidden_ref[...] = (before * half).astype(BF16)
    slope = half + (0.5 * root) * before * (1.0 - bend * bend) * (1.0 + (3 * 0.044715) * square)
    grad = (cotangent_ref[...].astype(F32) * slope).astype(BF16)
    grad_ref[...] = grad
    total[:width, :] += dot(features, grad, ROWS)
    total[width:, :] += dot(aggregated, grad, ROWS)

    @pl.when(step == pl.num_programs(0) - 1)
    def _():
        weights_ref[...] = total[...].astype(BF16)


def forward(owners, hub, heads, cut, arrived, local, scale, features, cotangent, self_weight, neighbor_weight):
    count, width = features.shape
    sections = hub.shape[1] // HUB
    flops = 2 * count * width * (hub.shape[1] + cut.shape[1] + 4 * width)
    return pl.pallas_call(
        forward_kernel,
        grid_spec=pltpu.PrefetchScalarGridSpec(
            num_scalar_prefetch=1,
            grid=(count // CHUNK,),
            in_specs=[
                rows_of(CHUNK, hub.shape[1]),
                whole(heads.shape),
                rows_of(CHUNK, cut.shape[1]),
                whole(arrived.shape),
                rows_of(CHUNK, width),
                rows_of(CHUNK, 1),
                rows_of(CHUNK, width),
                rows_of(CHUNK, width),
                whole((width, width)),
                whole((width, width)),
            ],
            out_specs=[rows_of(CHUNK, width), rows_of(CHUNK, width), whole((2 * width, width))],
            scratch_shapes=[
                pltpu.VMEM((sections * HUB, width), BF16),
                pltpu.VMEM((2 * width, width), F32),
            ],
        ),
        out_shape=[
            jax.ShapeDtypeStruct((count, width), BF16),
            jax.ShapeDtypeStruct((count, width), BF16),
            jax.ShapeDtypeStruct((2 * width, width), BF16),
        ],
        compiler_params=params(),
        cost_estimate=cost(flops, 2 * hub.size + 2 * cut.size + 14 * features.size),
        name="forward",
    )(owners, hub, heads, cut, arrived, local, scale, features, cotangent, self_weight, neighbor_weight)


def backward_kernel(
    owner_ref, hub_ref, cut_ref, scale_ref, grad_ref, neighbor_ref, aggregate_ref, heads_ref, back_ref, hub_total, cut_total
):
    step = pl.program_id(0)
    sections = hub_ref.shape[1] // HUB

    @pl.when(step == 0)
    def _():
        hub_total[...] = jnp.zeros_like(hub_total)
        cut_total[...] = jnp.zeros_like(cut_total)

    aggregate = (dot(grad_ref[...], neighbor_ref[...], COLS) * scale_ref[...]).astype(BF16)
    aggregate_ref[...] = aggregate
    hub_total[...] += dot(hub_ref[...], aggregate, ROWS)
    cut_total[...] += dot(cut_ref[...], aggregate, ROWS)

    @pl.when(step == pl.num_programs(0) - 1)
    def _():
        back_ref[...] = cut_total[...].astype(BF16)
        for r in range(heads_ref.shape[0]):
            piece = jnp.zeros(heads_ref.shape[1:], F32)
            for s in range(sections):
                mine = jnp.where(owner_ref[s] == r, 1.0, 0.0).astype(F32)
                piece = piece + mine * hub_total[s * HUB : (s + 1) * HUB, :]
            heads_ref[r] = piece.astype(BF16)


def backward(owners, hub, cut, scale, grad, neighbor_weight, row_count):
    count, width = grad.shape
    flops = 2 * count * width * (hub.shape[1] + cut.shape[1] + width)
    return pl.pallas_call(
        backward_kernel,
        grid_spec=pltpu.PrefetchScalarGridSpec(
            num_scalar_prefetch=1,
            grid=(count // CHUNK,),
            in_specs=[
                rows_of(CHUNK, hub.shape[1]),
                rows_of(CHUNK, cut.shape[1]),
                rows_of(CHUNK, 1),
                rows_of(CHUNK, width),
                whole((width, width)),
            ],
            out_specs=[
                rows_of(CHUNK, width),
                whole((row_count, HUB, width)),
                whole((cut.shape[1], width)),
            ],
            scratch_shapes=[
                pltpu.VMEM((hub.shape[1], width), F32),
                pltpu.VMEM((cut.shape[1], width), F32),
            ],
        ),
        out_shape=[
            jax.ShapeDtypeStruct((count, width), BF16),
            jax.ShapeDtypeStruct((row_count, HUB, width), BF16),
            jax.ShapeDtypeStruct((cut.shape[1], width), BF16),
        ],
        compiler_params=params(),
        cost_estimate=cost(flops, 2 * hub.size + 2 * cut.size + 4 * grad.size),
        name="backward",
    )(owners, hub, cut, scale, grad, neighbor_weight)


def local_back_kernel(index_ref, values_ref, aggregate_ref, grad_ref, self_ref, out_ref):
    step = pl.program_id(0)

    @pl.when(step == 0)
    def _():
        out_ref[...] = dot(grad_ref[...], self_ref[...], COLS)

    for t in range(TILE_STEP):
        at = step * TILE_STEP + t
        row = pl.ds(pl.multiple_of(index_ref[at, 0] * TILE, TILE), TILE)
        col = pl.ds(pl.multiple_of(index_ref[at, 1] * TILE, TILE), TILE)
        out_ref[col, :] += dot(values_ref[t], aggregate_ref[row, :], ROWS)


def local_backward(index, values, aggregate, grad, self_weight):
    tiles = values.shape[0]
    count, width = grad.shape
    return pl.pallas_call(
        local_back_kernel,
        grid_spec=pltpu.PrefetchScalarGridSpec(
            num_scalar_prefetch=1,
            grid=(tiles // TILE_STEP,),
            in_specs=[
                pl.BlockSpec((TILE_STEP, TILE, TILE), lambda i, *_: (i, 0, 0)),
                whole((count, width)),
                whole((count, width)),
                whole((width, width)),
            ],
            out_specs=whole((count, width)),
        ),
        out_shape=jax.ShapeDtypeStruct((count, width), F32),
        compiler_params=params(),
        cost_estimate=cost(
            2 * tiles * TILE * TILE * width + 2 * count * width * width,
            2 * values.size + 8 * grad.size,
        ),
        name="local_backward",
    )(index, values, aggregate, grad, self_weight)


def finish_kernel(rows_ref, returned_ref, heads_ref, local_ref, out_ref):
    step = pl.program_id(0)
    picks = returned_ref.shape[0]
    where = lax.broadcasted_iota(jnp.int32, (CHUNK, picks), 0) + step * CHUNK
    table = jnp.where(where == rows_ref[...], 1.0, 0.0).astype(BF16)
    total = local_ref[...] + dot(table, returned_ref[...])
    out_ref[...] = total.astype(BF16)

    @pl.when(step == 0)
    def _():
        heads = jnp.sum(heads_ref[...].astype(F32), axis=0)
        out_ref[:HUB, :] = (total[:HUB, :] + heads).astype(BF16)


def finish(rows, returned, heads, local):
    count, width = local.shape
    picks = returned.shape[0]
    return pl.pallas_call(
        finish_kernel,
        grid=(count // CHUNK,),
        in_specs=[
            whole((1, picks)),
            whole((picks, width)),
            whole(heads.shape),
            rows_of(CHUNK, width),
        ],
        out_specs=rows_of(CHUNK, width),
        out_shape=jax.ShapeDtypeStruct((count, width), BF16),
        compiler_params=params(),
        cost_estimate=cost(2 * count * picks * width, 6 * local.size),
        name="finish",
    )(rows, returned, heads, local)


def on_device(
    features,
    cotangent,
    self_weight,
    neighbor_weight,
    tile_values,
    tile_index,
    hub_adjacency,
    hub_owner,
    send_rows,
    cut_adjacency,
    degrees,
):
    count, width = features.shape
    groups = lax.axis_size("grp")
    row_count = lax.axis_size("row")
    everyone = ("grp", "row")
    device_count = groups * row_count
    values = tile_values[0]
    index = tile_index[0]
    owners = hub_owner[0]
    rows = send_rows[0].reshape(-1)

    heads = jnp.broadcast_to(features[:HUB][None], (row_count, HUB, width))
    heads = lax.all_to_all(heads, "row", split_axis=0, concat_axis=0, tiled=True)
    outgoing = pick_rows(rows[:, None], features)
    arrived = lax.all_to_all(outgoing, "grp", split_axis=0, concat_axis=0, tiled=True)
    scale = lax.rsqrt(degrees.astype(F32))[:, None]
    local = local_forward(index, values, features)
    hidden, grad, weights = forward(
        owners, hub_adjacency, heads, cut_adjacency, arrived, local, scale,
        features, cotangent, self_weight, neighbor_weight,
    )
    parts = lax.all_to_all(weights, everyone, split_axis=0, concat_axis=0, tiled=True)
    aggregate, head_parts, back_rows = backward(
        owners, hub_adjacency, cut_adjacency, scale, grad, neighbor_weight, row_count
    )
    head_parts = lax.all_to_all(head_parts, "row", split_axis=0, concat_axis=0, tiled=True)
    returned = lax.all_to_all(back_rows, "grp", split_axis=0, concat_axis=0, tiled=True)
    local_grad = local_backward(index, values, aggregate, grad, self_weight)
    summed = jnp.sum(parts.reshape(device_count, -1, width).astype(F32), axis=0).astype(BF16)
    spread = jnp.broadcast_to(summed[None], (device_count, *summed.shape))
    spread = lax.all_to_all(spread, everyone, split_axis=0, concat_axis=0, tiled=True)
    weight_grads = spread.reshape(2 * width, width).astype(F32)
    grad_features = finish(rows[None, :], returned, head_parts, local_grad)
    return hidden, grad_features, weight_grads[:width], weight_grads[width:]


def solution(mesh):
    nodes = P(("grp", "row"), None)
    in_specs = (
        nodes,
        nodes,
        P(),
        P(),
        P(("grp", "row"), None, None, None),
        P(("grp", "row"), None, None),
        nodes,
        P("grp", None),
        P(("grp", "row"), None, None),
        nodes,
        P(("grp", "row")),
    )
    out_specs = (nodes, nodes, P(), P())
    return jax.shard_map(
        on_device, mesh=mesh, in_specs=in_specs, out_specs=out_specs, check_vma=False
    )
```

time: 367 us -> 111 us (0.30)
  waiting for transfers between devices: 232 us -> 24.1 us
  matrix products: 57.5 us -> 0 us
  Pallas kernels: 0 us -> 36 us
  local copies, waits for them, and re-layouts: 45.7 us -> 11.1 us
  blocking collectives: 0 us -> 20.4 us
  between operations: 19.1 us -> 0.81 us
  starting transfers between devices: 7.64 us -> 17.4 us
  other arithmetic: 4.64 us -> 0.06 us
    psum x3 -> x0, waiting for transfers between devices: 231 us -> none  [the longest x1 114 us: on_device(): lax.psum((self_part, neighbor_part), ('grp', 'row'))]
    dot_general x23 -> x0, matrix products: 57.5 us -> none  [the longest x8 7.36 us: on_device(): jnp.dot(hub_adjacency[:, section * HUB:(section + 1) * HUB], panel, prefe...]
    pallas_call x0 -> x6, Pallas kernels: none -> 36 us  [the longest x1 11.5 us: forward(): pl.pallas_call(forward_kernel, grid_spec=pltpu.PrefetchScalarGridSpec(num...]
    dot_general x5 -> x0, local copies, waits for them, and re-layouts: 23.6 us -> none  [the longest x1 9.21 us: on_device(): jnp.einsum('lab,lbf->laf', values, picked, preferred_element_type=jnp.flo...]
    all_to_all x0 -> x2, blocking collectives: none -> 20.4 us  [the longest x1 13.2 us: on_device(): lax.all_to_all(weights, everyone, split_axis=0, concat_axis=0, tiled=True)]
    all_to_all x1 -> x3, waiting for transfers between devices: 0.01 us -> 20.3 us  [the longest x1 14.5 us: on_device(): lax.all_to_all(head_parts, 'row', split_axis=0, concat_axis=0, tiled=True)]
    all_to_all x1 -> x3, starting transfers between devices: 3.32 us -> 13.2 us  [the longest x1 6.31 us: on_device(): lax.all_to_all(heads, 'row', split_axis=0, concat_axis=0, tiled=True)]
    gather x3 -> x0, local copies, waits for them, and re-layouts: 8.64 us -> none  [the longest x1 3.01 us: on_device(): outgoing = features[send_rows[0]]]
  transfers between devices with their start and end apart: 5 -> 4, of which waited for: 3 -> 3; matrix products, arithmetic and copies ran while one was open for 16% -> 2% of each run, Pallas kernels for 0% -> 13%
where the time goes in v1:
time: 111 us; the launch traced here: 110 us
  Pallas kernels  36 us (32%)
  waiting for transfers between devices  24.1 us (22%)
  blocking collectives  20.4 us (18%)
  starting transfers between devices  17.4 us (16%)
  local copies, waits for them, and re-layouts  11.1 us (10%)
    all_to_all x1, waiting for transfers between devices, on_device(): lax.all_to_all(head_parts, 'row', split_axis=0, concat_axis=0, tiled=True)  14.5 us
    all_to_all x1, blocking collectives, on_device(): lax.all_to_all(weights, everyone, split_axis=0, concat_axis=0, tiled=True)  13.2 us
    pallas_call x1, Pallas kernels, forward(): pl.pallas_call(forward_kernel, grid_spec=pltpu.PrefetchScalarGridSpec(num...  11.5 us
    pallas_call x1, Pallas kernels, backward(): pl.pallas_call(backward_kernel, grid_spec=pltpu.PrefetchScalarGridSpec(nu...  8.54 us
    all_to_all x1, blocking collectives, on_device(): lax.all_to_all(back_rows, 'grp', split_axis=0, concat_axis=0, tiled=True)  7.28 us
    pallas_call x1, Pallas kernels, local_backward(): pl.pallas_call(local_back_kernel, grid_spec=pltpu.PrefetchScalarGridSpec(...  7.13 us
    all_to_all x1, starting transfers between devices, on_device(): lax.all_to_all(heads, 'row', split_axis=0, concat_axis=0, tiled=True)  6.31 us
    unnamed x36, local copies, waits for them, and re-layouts  5.9 us
  transfers between devices with their start and end apart: 4, of which 3 were waited for; matrix products, arithmetic and copies ran while one was open for 2% of the time, Pallas kernels for 13%

profile of v1, /device:TPU:0, one launch (start us, length us, event | category | flops | bytes accessed | tf_op | source)
XLA Modules:
  0.0 110.0 jit_solution(10813391388540296483)
XLA Ops:
  0.6 0.0 copy-start.17
  0.6 0.0 copy-start.16
  0.7 0.8 broadcast_in_dim_reshape_squeeze.8.rows_ref
  1.5 0.0 copy-start
  1.5 1.2 %copy-done = bf16[2048,256]{1,0:T(8,128)(2,1)S(1)} copy-done((bf16[2048,256]{1,0:T(8,128)(2,1)S(1)}, bf16[2048,256]{1,0:T(8,128)(2,1)}, u32[]{:S(2)}) %copy-start) | copy-done | bytes 1048600
  2.7 1.4 %pick_rows.1 = bf16[256,256]{1,0:T(8,128)(2,1)} custom-call(s32[256,1]{1,0:T(8,128)S(1)} %broadcast_in_dim_reshape_squeeze.8.rows_ref, bf16[2048,256]{1,0:T(8,128)(2,1)S(1)} %copy-done), custom_call_target="tpu_custom_call" | custom-call | flops 268435456 | bytes 1048576 | tf_op jit(solution)/shard_map/pick_rows/pallas_call | solution.py:52
  4.1 4.2 %all-to-all-start.1 = ((bf16[4,64,256]{2,1,0:T(8,128)(2,1)}), bf16[4,64,256]{2,1,0:T(8,128)(2,1)S(1)}, u32[]{:S(2)}, u32[]{:S(2)}) async-start(bf16[4,64,256]{2,1,0:T(8,128)(2,1)} %bitcast.1), calls=%async_computation.1 | async-start | bytes 262144 | tf_op jit(solution)/shard_map/all_to_all | solution.py:348
  8.4 0.8 slice.15
  9.2 3.8 %all-to-all-done.1 = bf16[4,64,256]{2,1,0:T(8,128)(2,1)S(1)} async-done(((bf16[4,64,256]{2,1,0:T(8,128)(2,1)}), bf16[4,64,256]{2,1,0:T(8,128)(2,1)S(1)}, u32[]{:S(2)}, u32[]{:S(2)}) %all-to-all-start.1) | async-done | bytes 131104 | tf_op jit(solution)/shard_map/all_to_all | solution.py:348
  13.0 0.8 broadcast_in_dim.6
  13.8 6.3 %all-to-all-start = ((bf16[8,128,256]{2,1,0:T(8,128)(2,1)}), bf16[8,128,256]{2,1,0:T(8,128)(2,1)}, u32[]{:S(2)}, u32[]{:S(2)}) async-start(bf16[8,128,256]{2,1,0:T(8,128)(2,1)} %broadcast_in_dim.6), calls=%async_computation | async-start | bytes 1048576 | tf_op jit(solution)/shard_map/all_to_all | solution.py:346
  20.2 0.0 copy-done.17
  20.2 0.7 copy.18.index_ref
  20.9 0.0 copy-done.16
  20.9 0.4 copy.19.scale_ref
  21.3 0.0 copy-done.1
  21.3 0.0 copy-start.2
  21.3 1.6 %copy-done.2 = bf16[1,64,128,128]{3,2,1,0:T(8,128)(2,1)S(1)} copy-done((bf16[1,64,128,128]{3,2,1,0:T(8,128)(2,1)S(1)}, bf16[1,64,128,128]{3,2,1,0:T(8,128)(2,1)}, u32[]{:S(2)}) %copy-start.2) | copy-done | bytes 2097176
  22.9 0.8 copy-done.12
  23.6 3.7 %local_forward.1.local_ref = f32[2048,256]{1,0:T(8,128)S(1)} custom-call(s32[64,2]{1,0:T(8,128)S(1)} %copy-done.12, bf16[64,128,128]{2,1,0:T(8,128)(2,1)S(1)} %bitcast.12, bf16[2048,256]{1,0:T(8,128)(2,1)S(1)} %copy-done.1), custom_call_target="tpu_custom_call" | custom-call | flops 536870912 | bytes 5242880 | tf_op jit(solution)/shard_map/local_forward/pallas_call | solution.py:81
  27.3 0.0 copy-start.3
  27.4 1.3 %copy-done.3 = f32[2048,256]{1,0:T(8,128)} copy-done((f32[2048,256]{1,0:T(8,128)}, f32[2048,256]{1,0:T(8,128)S(1)}, u32[]{:S(2)}) %copy-start.3) | copy-done | bytes 2097176
  28.7 5.8 %all-to-all-done.heads_ref = bf16[8,128,256]{2,1,0:T(8,128)(2,1)} async-done(((bf16[8,128,256]{2,1,0:T(8,128)(2,1)}), bf16[8,128,256]{2,1,0:T(8,128)(2,1)}, u32[]{:S(2)}, u32[]{:S(2)}) %all-to-all-start) | async-done | bytes 524320 | tf_op jit(solution)/shard_map/all_to_all | solution.py:346
  34.4 0.0 copy-done.4
  34.4 0.0 copy-done.9
  34.4 0.0 copy-done.10
  34.4 0.0 copy-done.14
  34.5 11.5 %forward.1 = (bf16[2048,256]{1,0:T(8,128)(2,1)}, bf16[2048,256]{1,0:T(8,128)(2,1)S(1)}, bf16[512,256]{1,0:T(8,128)(2,1)S(1)}) custom-call(s32[8]{0:T(128)S(1)} %bitcast.17, bf16[2048,1024]{1,0:T(8,128)(2,1)} %hub_ref.3, bf16[8,128,256]{2,1,0:T(8,128)(2,1)} %all-to-all-done.heads_ref, bf16[2048,256]{1,0:T(8,128)(2,1)S(1)} %copy-done.4, ...), custom_call_target="tpu_custom_call" | custom-call | flops 2415919104 | bytes 12582912 | tf_op jit(solution)/shard_map/forward/pallas_call | solution.py:151
  46.0 8.5 %backward.1 = (bf16[2048,256]{1,0:T(8,128)(2,1)S(1)}, bf16[8,128,256]{2,1,0:T(8,128)(2,1)S(1)}, bf16[256,256]{1,0:T(8,128)(2,1)S(1)}) custom-call(s32[8]{0:T(128)S(1)} %bitcast.18, bf16[2048,1024]{1,0:T(8,128)(2,1)} %hub_ref.3, bf16[2048,256]{1,0:T(8,128)(2,1)S(1)} %copy-done.4, f32[2048,1]{1,0:T(8,128)S(1)} %copy.19.scale_ref, ...), custom_call_target="tpu_custom_call" | custom-call | flops 1610612736 | bytes 7340032 | tf_op jit(solution)/shard_map/backward/pallas_call | solution.py:215
  54.5 0.0 copy-done.5
  54.5 0.0 copy-start.7
  54.5 1.0 copy-done.7
  55.5 0.0 copy-start.8
  55.5 7.3 %all_to_all.46 = bf16[4,64,256]{2,1,0:T(8,128)(2,1)S(1)} all-to-all(bf16[4,64,256]{2,1,0:T(8,128)(2,1)S(1)} %bitcast.16), channel_id=1, replica_groups=mesh['grp'=4,'row'=8] {'grp'}, dimensions={0} | all-to-all | bytes 262144 | tf_op jit(solution)/shard_map/all_to_all | solution.py:360
  62.8 13.2 %all_to_all.47 = bf16[32,16,256]{2,1,0:T(8,128)(2,1)S(1)} all-to-all(bf16[32,16,256]{2,1,0:T(8,128)(2,1)S(1)} %bitcast.15), channel_id=1, replica_groups=mesh['grp'=4,'row'=8] {'grp','row'}, dimensions={0} | all-to-all | bytes 524288 | tf_op jit(solution)/shard_map/all_to_all | solution.py:355
  76.0 0.0 copy-done.11
  76.0 3.5 %all-to-all-start.3 = ((bf16[8,128,256]{2,1,0:T(8,128)(2,1)}), bf16[8,128,256]{2,1,0:T(8,128)(2,1)S(1)}, u32[]{:S(2)}, u32[]{:S(2)}) async-start(bf16[8,128,256]{2,1,0:T(8,128)(2,1)} %copy-done.11), calls=%async_computation.3 | async-start | bytes 1048576 | tf_op jit(solution)/shard_map/all_to_all | solution.py:359
  79.5 0.1 reduce_sum.12
  79.5 14.5 %all-to-all-done.3.heads_ref = bf16[8,128,256]{2,1,0:T(8,128)(2,1)S(1)} async-done(((bf16[8,128,256]{2,1,0:T(8,128)(2,1)}), bf16[8,128,256]{2,1,0:T(8,128)(2,1)S(1)}, u32[]{:S(2)}, u32[]{:S(2)}) %all-to-all-start.3) | async-done | bytes 524320 | tf_op jit(solution)/shard_map/all_to_all | solution.py:359
  94.1 0.7 broadcast_in_dim.8
  94.8 3.4 %all-to-all-start.5 = ((bf16[32,16,256]{2,1,0:T(8,128)(2,1)}), bf16[32,16,256]{2,1,0:T(8,128)(2,1)S(1)}, u32[]{:S(2)}, u32[]{:S(2)}) async-start(bf16[32,16,256]{2,1,0:T(8,128)(2,1)} %broadcast_in_dim.8), calls=%async_computation.5 | async-start | bytes 524288 | tf_op jit(solution)/shard_map/all_to_all | solution.py:364
  98.2 0.0 copy-done.15
  98.2 0.1 broadcast_in_dim_reshape_squeeze.7.rows_ref
  98.3 0.0 copy-done.8
  98.3 7.1 %local_backward.1.local_ref = f32[2048,256]{1,0:T(8,128)S(1)} custom-call(s32[64,2]{1,0:T(8,128)S(1)} %copy-done.13, bf16[64,128,128]{2,1,0:T(8,128)(2,1)} %bitcast.11, bf16[2048,256]{1,0:T(8,128)(2,1)S(1)} %copy-done.8, bf16[2048,256]{1,0:T(8,128)(2,1)S(1)} %copy-done.6, bf16[256,256]{1,0:T(8,128)(2,1)S(1)} %copy-done.10), custom_call_target="tpu_custom_call" | custom-call | flops 805306368 | bytes 6291456 | tf_op jit(solution)/shard_map/local_backward/pallas_call | solution.py:265
  105.4 3.7 %finish.1 = bf16[2048,256]{1,0:T(8,128)(2,1)} custom-call(s32[1,256]{1,0:T(1,128)S(1)} %broadcast_in_dim_reshape_squeeze.7.rows_ref, bf16[256,256]{1,0:T(8,128)(2,1)S(1)} %bitcast.14, bf16[8,128,256]{2,1,0:T(8,128)(2,1)S(1)} %all-to-all-done.3.heads_ref, f32[2048,256]{1,0:T(8,128)S(1)} %local_backward.1.local_ref), custom_call_target="tpu_custom_call" | custom-call | flops 268435456 | bytes 3145728 | tf_op jit(solution)/shard_map/finish/pallas_call | solution.py:305
  109.1 0.0 all-to-all-done.5
  109.1 0.8 fusion
  (14 shorter events, 0.0 us)
Async XLA Ops:
  0.6 19.5 %copy-start.17 = (s32[1,64,2]{1,2,0:T(2,128)S(1)}, s32[1,64,2]{1,2,0:T(2,128)}, u32[]{:S(2)}) copy-start(s32[1,64,2]{1,2,0:T(2,128)} %param.16) | copy-start | bytes 1540
  0.6 20.2 %copy-start.16 = (s32[2048]{0:T(1024)S(1)}, s32[2048]{0:T(1024)}, u32[]{:S(2)}) copy-start(s32[2048]{0:T(1024)} %param.21) | copy-start | bytes 24580
  1.5 1.2 %copy-start = (bf16[2048,256]{1,0:T(8,128)(2,1)S(1)}, bf16[2048,256]{1,0:T(8,128)(2,1)}, u32[]{:S(2)}) copy-start(bf16[2048,256]{1,0:T(8,128)(2,1)} %features_ref.5) | copy-start | bytes 3145732
  2.7 18.5 %copy-start.1 = (bf16[2048,256]{1,0:T(8,128)(2,1)S(1)}, bf16[2048,256]{1,0:T(8,128)(2,1)}, u32[]{:S(2)}) copy-start(bf16[2048,256]{1,0:T(8,128)(2,1)} %features_ref.5) | copy-start | bytes 3145732
  4.1 8.9 %all-to-all-start.1 = ((bf16[4,64,256]{2,1,0:T(8,128)(2,1)}), bf16[4,64,256]{2,1,0:T(8,128)(2,1)S(1)}, u32[]{:S(2)}, u32[]{:S(2)}) async-start(bf16[4,64,256]{2,1,0:T(8,128)(2,1)} %bitcast.1), calls=%async_computation.1 | async-start | bytes 262144 | tf_op jit(solution)/shard_map/all_to_all | solution.py:348
  13.8 20.6 %all-to-all-start = ((bf16[8,128,256]{2,1,0:T(8,128)(2,1)}), bf16[8,128,256]{2,1,0:T(8,128)(2,1)}, u32[]{:S(2)}, u32[]{:S(2)}) async-start(bf16[8,128,256]{2,1,0:T(8,128)(2,1)} %broadcast_in_dim.6), calls=%async_computation | async-start | bytes 1048576 | tf_op jit(solution)/shard_map/all_to_all | solution.py:346
  21.3 1.6 %copy-start.2 = (bf16[1,64,128,128]{3,2,1,0:T(8,128)(2,1)S(1)}, bf16[1,64,128,128]{3,2,1,0:T(8,128)(2,1)}, u32[]{:S(2)}) copy-start(bf16[1,64,128,128]{3,2,1,0:T(8,128)(2,1)} %param.15) | copy-start | bytes 6291460
  22.9 0.8 copy-start.12
  23.6 10.8 %copy-start.4 = (bf16[2048,256]{1,0:T(8,128)(2,1)S(1)}, bf16[2048,256]{1,0:T(8,128)(2,1)}, u32[]{:S(2)}) copy-start(bf16[2048,256]{1,0:T(8,128)(2,1)} %cut_ref.3) | copy-start | bytes 3145732
  23.6 10.8 %copy-start.9 = (bf16[256,256]{1,0:T(8,128)(2,1)S(1)}, bf16[256,256]{1,0:T(8,128)(2,1)}, u32[]{:S(2)}) copy-start(bf16[256,256]{1,0:T(8,128)(2,1)} %neighbor_ref.3) | copy-start | bytes 393220
  23.6 10.8 %copy-start.10 = (bf16[256,256]{1,0:T(8,128)(2,1)S(1)}, bf16[256,256]{1,0:T(8,128)(2,1)}, u32[]{:S(2)}) copy-start(bf16[256,256]{1,0:T(8,128)(2,1)} %self_ref.3) | copy-start | bytes 393220
  23.6 10.8 %copy-start.14 = (s32[1,8]{1,0:T(1,128)S(1)}, s32[1,8]{1,0:T(1,128)}, u32[]{:S(2)}) copy-start(s32[1,8]{1,0:T(1,128)} %param.18) | copy-start | bytes 100
  27.3 1.3 %copy-start.3 = (f32[2048,256]{1,0:T(8,128)}, f32[2048,256]{1,0:T(8,128)S(1)}, u32[]{:S(2)}) copy-start(f32[2048,256]{1,0:T(8,128)S(1)} %local_forward.1.local_ref) | copy-start | bytes 6291460
  46.0 8.6 %copy-start.5 = (bf16[2048,256]{1,0:T(8,128)(2,1)}, bf16[2048,256]{1,0:T(8,128)(2,1)S(1)}, u32[]{:S(2)}) copy-start(bf16[2048,256]{1,0:T(8,128)(2,1)S(1)} %get-tuple-element.11.grad_ref) | copy-start | bytes 3145732
  54.5 1.0 copy-start.7
  55.5 20.5 %copy-start.11 = (bf16[8,128,256]{2,1,0:T(8,128)(2,1)}, bf16[8,128,256]{2,1,0:T(8,128)(2,1)S(1)}, u32[]{:S(2)}) copy-start(bf16[8,128,256]{2,1,0:T(8,128)(2,1)S(1)} %get-tuple-element.13) | copy-start | bytes 1572868
  55.5 42.7 %copy-start.15 = (s32[1,4,64]{2,1,0:T(4,128)S(1)}, s32[1,4,64]{2,1,0:T(4,128)}, u32[]{:S(2)}) copy-start(s32[1,4,64]{2,1,0:T(4,128)} %param.19) | copy-start | bytes 3076
  55.5 42.8 %copy-start.13 = (s32[64,2]{1,0:T(8,128)S(1)}, s32[64,2]{1,0:T(8,128)}, u32[]{:S(2)}) copy-start(s32[64,2]{1,0:T(8,128)} %copy.18.index_ref) | copy-start | bytes 1540
  55.5 42.8 %copy-start.6 = (bf16[2048,256]{1,0:T(8,128)(2,1)S(1)}, bf16[2048,256]{1,0:T(8,128)(2,1)}, u32[]{:S(2)}) copy-start(bf16[2048,256]{1,0:T(8,128)(2,1)} %copy-done.5) | copy-start | bytes 3145732
  55.5 42.8 %copy-start.8 = (bf16[2048,256]{1,0:T(8,128)(2,1)S(1)}, bf16[2048,256]{1,0:T(8,128)(2,1)}, u32[]{:S(2)}) copy-start(bf16[2048,256]{1,0:T(8,128)(2,1)} %copy-done.7) | copy-start | bytes 3145732
  76.0 18.1 %all-to-all-start.3 = ((bf16[8,128,256]{2,1,0:T(8,128)(2,1)}), bf16[8,128,256]{2,1,0:T(8,128)(2,1)S(1)}, u32[]{:S(2)}, u32[]{:S(2)}) async-start(bf16[8,128,256]{2,1,0:T(8,128)(2,1)} %copy-done.11), calls=%async_computation.3 | async-start | bytes 1048576 | tf_op jit(solution)/shard_map/all_to_all | solution.py:359
  94.8 14.3 %all-to-all-start.5 = ((bf16[32,16,256]{2,1,0:T(8,128)(2,1)}), bf16[32,16,256]{2,1,0:T(8,128)(2,1)S(1)}, u32[]{:S(2)}, u32[]{:S(2)}) async-start(bf16[32,16,256]{2,1,0:T(8,128)(2,1)} %broadcast_in_dim.8), calls=%async_computation.5 | async-start | bytes 524288 | tf_op jit(solution)/shard_map/all_to_all | solution.py:364

commit v2 on v1

--- a/solution.py
+++ b/solution.py
@@ -1,3 +1,5 @@
+import functools
+
 import jax
 import jax.numpy as jnp
 from jax import lax
@@ -38,27 +40,52 @@
     return pl.BlockSpec((step, width), lambda i, *_: (i, 0))
 
 
-def pick_kernel(rows_ref, features_ref, out_ref):
+def pick_kernel(place_ref, rows_ref, features_ref, own_ref, odd_ref, *rest):
+    even_refs, picked = rest[:-1], rest[-1]
     count = features_ref.shape[0]
-    where = lax.broadcasted_iota(jnp.int32, (rows_ref.shape[0], count), 1)
-    table = jnp.where(where == rows_ref[...], 1.0, 0.0).astype(BF16)
-    out_ref[...] = dot(table, features_ref[...]).astype(BF16)
-
-
-def pick_rows(rows, features):
-    picks = rows.shape[0]
+    lanes = rows_ref.shape[1]
+    across = lax.broadcasted_iota(jnp.int32, (lanes, lanes), 0)
+    along = lax.broadcasted_iota(jnp.int32, (lanes, lanes), 1)
+    where = lax.broadcasted_iota(jnp.int32, (lanes, count), 1)
+    for j in range(rows_ref.shape[0]):
+        line = jnp.broadcast_to(rows_ref[j : j + 1, :].astype(F32), (lanes, lanes))
+        column = jnp.sum(jnp.where(across == along, line, 0.0), axis=1, keepdims=True)
+        table = jnp.where(where == column.astype(jnp.int32), 1.0, 0.0).astype(BF16)
+        picked[j * lanes : (j + 1) * lanes, :] = dot(table, features_ref[...]).astype(BF16)
+    cut = own_ref.shape[0]
+
+    def piece(k):
+        return picked[pl.ds(pl.multiple_of((place_ref[0] ^ k) * cut, cut), cut), :]
+
+    own_ref[...] = piece(0)
+    for j in range(odd_ref.shape[0]):
+        odd_ref[j] = piece(2 * j + 1)
+    for j, ref in enumerate(even_refs):
+        ref[...] = piece(2 * j + 2)
+
+
+def pick_rows(place, rows, features):
+    groups, cut = rows.shape
+    picks = groups * cut
     count, width = features.shape
-    step = 128
-    return pl.pallas_call(
+    evens = groups // 2 - 1
+    piece = jax.ShapeDtypeStruct((cut, width), BF16)
+    out = pl.pallas_call(
         pick_kernel,
-        grid=(picks // step,),
-        in_specs=[rows_of(step, 1), whole((count, width))],
-        out_specs=rows_of(step, width),
-        out_shape=jax.ShapeDtypeStruct((picks, width), BF16),
+        grid_spec=pltpu.PrefetchScalarGridSpec(
+            num_scalar_prefetch=1,
+            grid=(1,),
+            in_specs=[whole((picks // 128, 128)), whole((count, width))],
+            out_specs=[whole((cut, width)), whole((groups // 2, cut, width))]
+            + [whole((cut, width))] * evens,
+            scratch_shapes=[pltpu.VMEM((picks, width), BF16)],
+        ),
+        out_shape=[piece, jax.ShapeDtypeStruct((groups // 2, cut, width), BF16)] + [piece] * evens,
         compiler_params=params(),
         cost_estimate=cost(2 * picks * count * width, 2 * count * width),
         name="pick_rows",
-    )(rows, features)
+    )(place, rows.reshape(picks // 128, 128), features)
+    return out[0], out[1], out[2:]
 
 
 def local_kernel(index_ref, values_ref, features_ref, out_ref):
@@ -97,34 +124,44 @@
 
 
 def forward_kernel(
-    owner_ref,
+    head_count,
+    place_ref,
     hub_ref,
-    heads_ref,
     cut_ref,
-    arrived_ref,
     local_ref,
     scale_ref,
     features_ref,
     cotangent_ref,
     self_ref,
     neighbor_ref,
-    hidden_ref,
-    grad_ref,
-    weights_ref,
-    panels,
-    total,
+    *rest,
 ):
+    hidden_ref, grad_ref, weights_ref, heads, panels, arrived, total = rest[-7:]
+    head_refs, own_ref, side_ref = rest[:head_count], rest[head_count], rest[head_count + 1]
+    far_refs = rest[head_count + 2 : -7]
     step = pl.program_id(0)
     sections = panels.shape[0] // HUB
     width = features_ref.shape[1]
+    cut = own_ref.shape[0]
 
     @pl.when(step == 0)
     def _():
         total[...] = jnp.zeros_like(total)
+        for k, ref in enumerate(head_refs):
+            heads[k] = ref[...]
         for s in range(sections):
-            panels[s * HUB : (s + 1) * HUB, :] = heads_ref[owner_ref[s]]
-
-    summed = dot(hub_ref[...], panels[...]) + dot(cut_ref[...], arrived_ref[...]) + local_ref[...]
+            panels[s * HUB : (s + 1) * HUB, :] = heads[place_ref[1 + s]]
+
+        def put(k, piece):
+            arrived[pl.ds(pl.multiple_of((place_ref[0] ^ k) * cut, cut), cut), :] = piece
+
+        put(0, own_ref[...])
+        put(1, side_ref[0])
+        for j, ref in enumerate(far_refs):
+            put(2 * j + 2, ref[0])
+            put(2 * j + 3, ref[1])
+
+    summed = dot(hub_ref[...], panels[...]) + dot(cut_ref[...], arrived[...]) + local_ref[...]
     aggregated = (summed * scale_ref[...]).astype(BF16)
     features = features_ref[...]
     before = dot(features, self_ref[...]) + dot(aggregated, neighbor_ref[...])
@@ -144,30 +181,31 @@
         weights_ref[...] = total[...].astype(BF16)
 
 
-def forward(owners, hub, heads, cut, arrived, local, scale, features, cotangent, self_weight, neighbor_weight):
+def forward(place, hub, cut, local, scale, features, cotangent, self_weight, neighbor_weight, heads, pieces):
     count, width = features.shape
     sections = hub.shape[1] // HUB
     flops = 2 * count * width * (hub.shape[1] + cut.shape[1] + 4 * width)
     return pl.pallas_call(
-        forward_kernel,
+        functools.partial(forward_kernel, len(heads)),
         grid_spec=pltpu.PrefetchScalarGridSpec(
             num_scalar_prefetch=1,
             grid=(count // CHUNK,),
             in_specs=[
                 rows_of(CHUNK, hub.shape[1]),
-                whole(heads.shape),
                 rows_of(CHUNK, cut.shape[1]),
-                whole(arrived.shape),
                 rows_of(CHUNK, width),
                 rows_of(CHUNK, 1),
                 rows_of(CHUNK, width),
                 rows_of(CHUNK, width),
                 whole((width, width)),
                 whole((width, width)),
-            ],
+            ]
+            + [whole(x.shape) for x in (*heads, *pieces)],
             out_specs=[rows_of(CHUNK, width), rows_of(CHUNK, width), whole((2 * width, width))],
             scratch_shapes=[
+                pltpu.VMEM((len(heads), HUB, width), BF16),
                 pltpu.VMEM((sections * HUB, width), BF16),
+                pltpu.VMEM((cut.shape[1], width), BF16),
                 pltpu.VMEM((2 * width, width), F32),
             ],
         ),
@@ -179,14 +217,27 @@
         compiler_params=params(),
         cost_estimate=cost(flops, 2 * hub.size + 2 * cut.size + 14 * features.size),
         name="forward",
-    )(owners, hub, heads, cut, arrived, local, scale, features, cotangent, self_weight, neighbor_weight)
+    )(place, hub, cut, local, scale, features, cotangent, self_weight, neighbor_weight, *heads, *pieces)
 
 
 def backward_kernel(
-    owner_ref, hub_ref, cut_ref, scale_ref, grad_ref, neighbor_ref, aggregate_ref, heads_ref, back_ref, hub_total, cut_total
+    place_ref,
+    hub_ref,
+    cut_ref,
+    scale_ref,
+    grad_ref,
+    neighbor_ref,
+    aggregate_ref,
+    low_ref,
+    high_ref,
+    own_ref,
+    side_ref,
+    *rest,
 ):
+    even_refs, far_refs, (hub_total, cut_total, heads) = split_refs(rest, 2 * low_ref.shape[0])
     step = pl.program_id(0)
     sections = hub_ref.shape[1] // HUB
+    cut = own_ref.shape[0]
 
     @pl.when(step == 0)
     def _():
@@ -200,19 +251,45 @@
 
     @pl.when(step == pl.num_programs(0) - 1)
     def _():
-        back_ref[...] = cut_total[...].astype(BF16)
-        for r in range(heads_ref.shape[0]):
-            piece = jnp.zeros(heads_ref.shape[1:], F32)
-            for s in range(sections):
-                mine = jnp.where(owner_ref[s] == r, 1.0, 0.0).astype(F32)
-                piece = piece + mine * hub_total[s * HUB : (s + 1) * HUB, :]
-            heads_ref[r] = piece.astype(BF16)
-
-
-def backward(owners, hub, cut, scale, grad, neighbor_weight, row_count):
+        heads[...] = jnp.zeros_like(heads)
+        for s in range(sections):
+            heads[place_ref[1 + s]] += hub_total[s * HUB : (s + 1) * HUB, :]
+        half = low_ref.shape[0]
+        for j in range(half):
+            low_ref[j] = heads[2 * j + 1].astype(BF16)
+            high_ref[j] = heads[2 * (half + j) + 1].astype(BF16)
+        for j, ref in enumerate(even_refs):
+            ref[...] = heads[2 * j].astype(BF16)
+
+        def piece(k):
+            at = pl.multiple_of((place_ref[0] ^ k) * cut, cut)
+            return cut_total[pl.ds(at, cut), :].astype(BF16)
+
+        own_ref[...] = piece(0)
+        for j in range(side_ref.shape[0]):
+            side_ref[j] = piece(2 * j + 1)
+        for j, ref in enumerate(far_refs):
+            ref[...] = piece(2 * j + 2)
+
+
+def split_refs(refs, first):
+    return refs[:first], refs[first:-3], refs[-3:]
+
+
+def backward(place, hub, cut, scale, grad, neighbor_weight, groups, row_count):
     count, width = grad.shape
     flops = 2 * count * width * (hub.shape[1] + cut.shape[1] + width)
-    return pl.pallas_call(
+    half = row_count // 4
+    width_cut = cut.shape[1] // groups
+    outs = [
+        (half, HUB, width),
+        (half, HUB, width),
+        (width_cut, width),
+        (groups // 2, width_cut, width),
+        *[(HUB, width)] * (row_count // 2),
+        *[(width_cut, width)] * (groups // 2 - 1),
+    ]
+    out = pl.pallas_call(
         backward_kernel,
         grid_spec=pltpu.PrefetchScalarGridSpec(
             num_scalar_prefetch=1,
@@ -224,25 +301,20 @@
                 rows_of(CHUNK, width),
                 whole((width, width)),
             ],
-            out_specs=[
-                rows_of(CHUNK, width),
-                whole((row_count, HUB, width)),
-                whole((cut.shape[1], width)),
-            ],
+            out_specs=[rows_of(CHUNK, width)] + [whole(x) for x in outs],
             scratch_shapes=[
                 pltpu.VMEM((hub.shape[1], width), F32),
                 pltpu.VMEM((cut.shape[1], width), F32),
+                pltpu.VMEM((row_count, HUB, width), F32),
             ],
         ),
-        out_shape=[
-            jax.ShapeDtypeStruct((count, width), BF16),
-            jax.ShapeDtypeStruct((row_count, HUB, width), BF16),
-            jax.ShapeDtypeStruct((cut.shape[1], width), BF16),
-        ],
+        out_shape=[jax.ShapeDtypeStruct(x, BF16) for x in ((count, width), *outs)],
         compiler_params=params(),
         cost_estimate=cost(flops, 2 * hub.size + 2 * cut.size + 4 * grad.size),
         name="backward",
-    )(owners, hub, cut, scale, grad, neighbor_weight)
+    )(place, hub, cut, scale, grad, neighbor_weight)
+    aggregate, low, high, own, side = out[:5]
+    return aggregate, low, high, out[5 : 5 + row_count // 2], own, side, out[5 + row_count // 2 :]
 
 
 def local_back_kernel(index_ref, values_ref, aggregate_ref, grad_ref, self_ref, out_ref):
@@ -285,38 +357,67 @@
     )(index, values, aggregate, grad, self_weight)
 
 
-def finish_kernel(rows_ref, returned_ref, heads_ref, local_ref, out_ref):
+def finish_kernel(piece_count, place_ref, rows_ref, local_ref, low_ref, own_ref, side_ref, *rest):
+    out_ref, returned = rest[-2:]
+    far_refs, head_refs = rest[:piece_count], rest[piece_count:-2]
     step = pl.program_id(0)
-    picks = returned_ref.shape[0]
+    cut = own_ref.shape[0]
+    picks = returned.shape[0]
+
+    @pl.when(step == 0)
+    def _():
+        def put(k, piece):
+            returned[pl.ds(pl.multiple_of((place_ref[0] ^ k) * cut, cut), cut), :] = piece
+
+        put(0, own_ref[...])
+        put(1, side_ref[0])
+        for j, ref in enumerate(far_refs):
+            put(2 * j + 2, ref[0])
+            put(2 * j + 3, ref[1])
+
     where = lax.broadcasted_iota(jnp.int32, (CHUNK, picks), 0) + step * CHUNK
     table = jnp.where(where == rows_ref[...], 1.0, 0.0).astype(BF16)
-    total = local_ref[...] + dot(table, returned_ref[...])
+    total = local_ref[...] + dot(table, returned[...])
     out_ref[...] = total.astype(BF16)
 
     @pl.when(step == 0)
     def _():
-        heads = jnp.sum(heads_ref[...].astype(F32), axis=0)
+        heads = low_ref[0].astype(F32)
+        for ref in head_refs:
+            heads = heads + ref[...].astype(F32)
         out_ref[:HUB, :] = (total[:HUB, :] + heads).astype(BF16)
 
 
-def finish(rows, returned, heads, local):
+def finish(place, rows, local, low, own, side, far, heads):
     count, width = local.shape
-    picks = returned.shape[0]
+    picks = rows.shape[1]
     return pl.pallas_call(
-        finish_kernel,
-        grid=(count // CHUNK,),
-        in_specs=[
-            whole((1, picks)),
-            whole((picks, width)),
-            whole(heads.shape),
-            rows_of(CHUNK, width),
-        ],
-        out_specs=rows_of(CHUNK, width),
+        functools.partial(finish_kernel, len(far)),
+        grid_spec=pltpu.PrefetchScalarGridSpec(
+            num_scalar_prefetch=1,
+            grid=(count // CHUNK,),
+            in_specs=[whole((1, picks)), rows_of(CHUNK, width)]
+            + [whole(x.shape) for x in (low, own, side, *far, *heads)],
+            out_specs=rows_of(CHUNK, width),
+            scratch_shapes=[pltpu.VMEM((picks, width), BF16)],
+        ),
         out_shape=jax.ShapeDtypeStruct((count, width), BF16),
         compiler_params=params(),
         cost_estimate=cost(2 * count * picks * width, 6 * local.size),
         name="finish",
-    )(rows, returned, heads, local)
+    )(place, rows, local, low, own, side, *far, *heads)
+
+
+def trade(value, axis, k):
+    return lax.ppermute(value, axis, [(r, r ^ k) for r in range(lax.axis_size(axis))])
+
+
+def trade_pieces(side, far):
+    side = trade(side, "grp", 1)
+    far = [
+        trade(jnp.stack([piece, side[j + 1]]), "grp", 2 * j + 2) for j, piece in enumerate(far)
+    ]
+    return side, far
 
 
 def on_device(
@@ -339,31 +440,40 @@
     device_count = groups * row_count
     values = tile_values[0]
     index = tile_index[0]
-    owners = hub_owner[0]
-    rows = send_rows[0].reshape(-1)
-
-    heads = jnp.broadcast_to(features[:HUB][None], (row_count, HUB, width))
-    heads = lax.all_to_all(heads, "row", split_axis=0, concat_axis=0, tiled=True)
-    outgoing = pick_rows(rows[:, None], features)
-    arrived = lax.all_to_all(outgoing, "grp", split_axis=0, concat_axis=0, tiled=True)
+    rows = send_rows[0]
+    group = lax.axis_index("grp").astype(jnp.int32)
+    place = jnp.concatenate([group[None], hub_owner[0] ^ lax.axis_index("row")])
+
+    heads = [features[:HUB]]
+    for k in range(2, row_count, 2):
+        heads.append(trade(heads[0], "row", k))
+    heads = [x for head in heads for x in (head, trade(head, "row", 1))]
+    own, side, far = pick_rows(place, rows, features)
+    pieces = trade_pieces(side, far)
     scale = lax.rsqrt(degrees.astype(F32))[:, None]
     local = local_forward(index, values, features)
     hidden, grad, weights = forward(
-        owners, hub_adjacency, heads, cut_adjacency, arrived, local, scale,
-        features, cotangent, self_weight, neighbor_weight,
+        place, hub_adjacency, cut_adjacency, local, scale, features, cotangent,
+        self_weight, neighbor_weight, heads, (own, pieces[0], *pieces[1]),
     )
     parts = lax.all_to_all(weights, everyone, split_axis=0, concat_axis=0, tiled=True)
-    aggregate, head_parts, back_rows = backward(
-        owners, hub_adjacency, cut_adjacency, scale, grad, neighbor_weight, row_count
+    aggregate, low, high, evens, own, side, far = backward(
+        place, hub_adjacency, cut_adjacency, scale, grad, neighbor_weight, groups, row_count
     )
-    head_parts = lax.all_to_all(head_parts, "row", split_axis=0, concat_axis=0, tiled=True)
-    returned = lax.all_to_all(back_rows, "grp", split_axis=0, concat_axis=0, tiled=True)
+    half = row_count // 4
+    high = trade(high, "row", 1)
+    low = trade(low, "row", 1)
+    back = [evens[0]]
+    for j in reversed(range(1, 2 * half)):
+        other = high[j - half] if j >= half else low[j]
+        back.append(trade((evens[j].astype(F32) + other.astype(F32)).astype(BF16), "row", 2 * j))
+    side, far = trade_pieces(side, far)
     local_grad = local_backward(index, values, aggregate, grad, self_weight)
     summed = jnp.sum(parts.reshape(device_count, -1, width).astype(F32), axis=0).astype(BF16)
     spread = jnp.broadcast_to(summed[None], (device_count, *summed.shape))
     spread = lax.all_to_all(spread, everyone, split_axis=0, concat_axis=0, tiled=True)
     weight_grads = spread.reshape(2 * width, width).astype(F32)
-    grad_features = finish(rows[None, :], returned, head_parts, local_grad)
+    grad_features = finish(place, rows.reshape(1, -1), local_grad, low, own, side, far, back)
     return hidden, grad_features, weight_grads[:width], weight_grads[width:]
 
 

time: 111 us -> 92.1 us (0.83)
  waiting for transfers between devices: 24.1 us -> 1.25 us
  blocking collectives: 20.4 us -> 0 us
  starting transfers between devices: 17.4 us -> 30.2 us
  other arithmetic: 0.06 us -> 5.61 us
  local copies, waits for them, and re-layouts: 11.1 us -> 16.6 us
    all_to_all x3 -> x1, waiting for transfers between devices: 24.1 us -> 0.01 us  [on_device(): lax.all_to_all(weights, everyone, split_axis=0, concat_axis=0, tiled=True)]
    all_to_all x2 -> x0, blocking collectives: 20.4 us -> none  [the longest x1 13.2 us: on_device(): lax.all_to_all(weights, everyone, split_axis=0, concat_axis=0, tiled=True)]
    ppermute x0 -> x16, starting transfers between devices: none -> 20.3 us  [trade(): lax.ppermute(value, axis, [(r, r ^ k) for r in range(lax.axis_size(axis))])]
    all_to_all x3 -> x1, starting transfers between devices: 14 us -> 5.25 us  [on_device(): lax.all_to_all(weights, everyone, split_axis=0, concat_axis=0, tiled=True)]
    unnamed x36 -> x46, local copies, waits for them, and re-layouts: 5.9 us -> 13 us
    convert_element_type x0 -> x2, other arithmetic: none -> 1.77 us  [on_device(): (evens[j].astype(F32) + other.astype(F32)).astype(BF16)]
    another operation x0 -> x2, other arithmetic: none -> 1.41 us  [trade_pieces(): jnp.stack([piece, side[j + 1]])]
    ppermute x0 -> x16, waiting for transfers between devices: none -> 1.25 us  [trade(): lax.ppermute(value, axis, [(r, r ^ k) for r in range(lax.axis_size(axis))])]
  transfers between devices with their start and end apart: 4 -> 18, of which waited for: 3 -> 2; matrix products, arithmetic and copies ran while one was open for 2% -> 8% of each run, Pallas kernels for 13% -> 26%
where the time goes in v2:
time: 92.1 us; the launch traced here: 91 us
  Pallas kernels  36.5 us (40%)
  starting transfers between devices  30.2 us (33%)
  local copies, waits for them, and re-layouts  16.6 us (18%)
  other arithmetic  5.61 us (6%)
  waiting for transfers between devices  1.25 us (1%)
    ppermute x16, starting transfers between devices, trade(): lax.ppermute(value, axis, [(r, r ^ k) for r in range(lax.axis_size(axis))])  20.3 us
    unnamed x46, local copies, waits for them, and re-layouts  13 us
    pallas_call x1, Pallas kernels, forward(): pl.pallas_call(functools.partial(forward_kernel, len(heads)), grid_spec=p...  11.5 us
    pallas_call x1, Pallas kernels, backward(): pl.pallas_call(backward_kernel, grid_spec=pltpu.PrefetchScalarGridSpec(nu...  8.92 us
    pallas_call x1, Pallas kernels, local_backward(): pl.pallas_call(local_back_kernel, grid_spec=pltpu.PrefetchScalarGridSpec(...  7.13 us
    all_to_all x1, starting transfers between devices, on_device(): lax.all_to_all(weights, everyone, split_axis=0, concat_axis=0, tiled=True)  5.25 us
    all_to_all x1, starting transfers between devices, on_device(): lax.all_to_all(spread, everyone, split_axis=0, concat_axis=0, tiled=True)  4.63 us
    pallas_call x1, Pallas kernels, finish(): pl.pallas_call(functools.partial(finish_kernel, len(far)), grid_spec=pltp...  4.24 us
  transfers between devices with their start and end apart: 18, of which 2 were waited for; matrix products, arithmetic and copies ran while one was open for 8% of the time, Pallas kernels for 26%

profile of v2, /device:TPU:0, one launch (start us, length us, event | category | flops | bytes accessed | tf_op | source)
XLA Modules:
  0.0 91.0 jit_solution(14010202192609198523)
XLA Ops:
  0.6 0.8 reshape_squeeze.6.rows_ref
  1.4 0.7 xor_bitcast_fusion
  2.1 1.2 %copy-done = bf16[2048,256]{1,0:T(8,128)(2,1)S(1)} copy-done((bf16[2048,256]{1,0:T(8,128)(2,1)S(1)}, bf16[2048,256]{1,0:T(8,128)(2,1)}, u32[]{:S(2)}) %copy-start) | copy-done | bytes 1048600
  3.4 1.0 %pick_rows.1 = (bf16[64,256]{1,0:T(8,128)(2,1)S(1)}, bf16[2,64,256]{2,1,0:T(8,128)(2,1)S(1)}, bf16[64,256]{1,0:T(8,128)(2,1)S(1)}) custom-call(s32[9]{0:T(128)S(1)} %pad_add_fusion.place_ref, s32[2,128]{1,0:T(2,128)S(1)} %reshape_squeeze.6.rows_ref, bf16[2048,256]{1,0:T(8,128)(2,1)S(1)} %copy-done), custom_call_target="tpu_custom_call" | custom-call | flops 268435456 | bytes 1048576 | tf_op jit(solution)/shard_map/pick_rows/pallas_call | solution.py:73
  4.4 0.5 collective-permute-start.7
  4.9 2.7 %collective-permute-start.1 = (bf16[128,256]{1,0:T(8,128)(2,1)S(1)}, bf16[128,256]{1,0:T(8,128)(2,1)}, u32[]{:S(2)}, u32[]{:S(2)}) collective-permute-start(bf16[128,256]{1,0:T(8,128)(2,1)S(1)} %slice.30.rest_0_), channel_id=1, source_target_pairs={{0,2},{1,3},{2,0},{3,1},{4,6},{5,7},{6,4},{7,5},{8,10},{9,11},{10,... | collective-permute-start | bytes 196616 | tf_op jit(solution)/shard_map/ppermute | solution.py:412
  7.6 2.6 %collective-permute-start.3 = (bf16[128,256]{1,0:T(8,128)(2,1)S(1)}, bf16[128,256]{1,0:T(8,128)(2,1)}, u32[]{:S(2)}, u32[]{:S(2)}) collective-permute-start(bf16[128,256]{1,0:T(8,128)(2,1)S(1)} %slice.30.rest_0_), channel_id=1, source_target_pairs={{0,4},{1,5},{2,6},{3,7},{4,0},{5,1},{6,2},{7,3},{8,12},{9,13},{10,... | collective-permute-start | bytes 196616 | tf_op jit(solution)/shard_map/ppermute | solution.py:412
  10.2 1.7 %collective-permute-start = (bf16[128,256]{1,0:T(8,128)(2,1)S(1)}, bf16[128,256]{1,0:T(8,128)(2,1)}, u32[]{:S(2)}, u32[]{:S(2)}) collective-permute-start(bf16[128,256]{1,0:T(8,128)(2,1)S(1)} %slice.30.rest_0_), channel_id=1, source_target_pairs={{0,1},{1,0},{2,3},{3,2},{4,5},{5,4},{6,7},{7,6},{8,9},{9,8},{10,11... | collective-permute-start | bytes 196616 | tf_op jit(solution)/shard_map/ppermute | solution.py:412
  11.9 0.6 pad_maximum_fusion
  12.6 1.5 %collective-permute-start.8 = (bf16[2,64,256]{2,1,0:T(8,128)(2,1)}, bf16[2,64,256]{2,1,0:T(8,128)(2,1)}, u32[]{:S(2)}, u32[]{:S(2)}) collective-permute-start(bf16[2,64,256]{2,1,0:T(8,128)(2,1)} %pad_maximum_fusion), channel_id=1, source_target_pairs={{0,16},{8,24},{16,0},{24,8},{1,17},{9,25},{17,1},{25,9},{2,18},{10... | collective-permute-start | bytes 196616 | tf_op jit(solution)/shard_map/ppermute | solution.py:412
  14.1 0.5 collective-permute-start.2
  14.6 0.8 collective-permute-done.3.rest_4_
  15.4 1.5 %collective-permute-start.4 = (bf16[128,256]{1,0:T(8,128)(2,1)}, bf16[128,256]{1,0:T(8,128)(2,1)}, u32[]{:S(2)}, u32[]{:S(2)}) collective-permute-start(bf16[128,256]{1,0:T(8,128)(2,1)} %collective-permute-done.3.rest_4_), channel_id=1, source_target_pairs={{0,1},{1,0},{2,3},{3,2},{4,5},{5,4},{6,7},{7,6},{8,9},{9,8},{10,11... | collective-permute-start | bytes 196616 | tf_op jit(solution)/shard_map/ppermute | solution.py:412
  16.9 1.0 %collective-permute-start.6 = (bf16[128,256]{1,0:T(8,128)(2,1)}, bf16[128,256]{1,0:T(8,128)(2,1)}, u32[]{:S(2)}, u32[]{:S(2)}) collective-permute-start(bf16[128,256]{1,0:T(8,128)(2,1)} %collective-permute-done.5.rest_6_), channel_id=1, source_target_pairs={{0,1},{1,0},{2,3},{3,2},{4,5},{5,4},{6,7},{7,6},{8,9},{9,8},{10,11... | collective-permute-start | bytes 196616 | tf_op jit(solution)/shard_map/ppermute | solution.py:412
  17.9 0.7 convert_rsqrt_fusion
  18.6 0.8 copy.17.index_ref
  19.4 0.4 copy.18.scale_ref
  19.8 1.6 %copy-done.2 = bf16[1,64,128,128]{3,2,1,0:T(8,128)(2,1)S(1)} copy-done((bf16[1,64,128,128]{3,2,1,0:T(8,128)(2,1)S(1)}, bf16[1,64,128,128]{3,2,1,0:T(8,128)(2,1)}, u32[]{:S(2)}) %copy-start.2) | copy-done | bytes 2097176
  21.4 3.7 %local_forward.1.local_ref = f32[2048,256]{1,0:T(8,128)S(1)} custom-call(s32[64,2]{1,0:T(8,128)S(1)} %copy.17.index_ref, bf16[64,128,128]{2,1,0:T(8,128)(2,1)S(1)} %bitcast.27, bf16[2048,256]{1,0:T(8,128)(2,1)S(1)} %copy-done.1), custom_call_target="tpu_custom_call" | custom-call | flops 536870912 | bytes 5242880 | tf_op jit(solution)/shard_map/local_forward/pallas_call | solution.py:108
  25.1 1.3 %copy-done.3 = f32[2048,256]{1,0:T(8,128)} copy-done((f32[2048,256]{1,0:T(8,128)}, f32[2048,256]{1,0:T(8,128)S(1)}, u32[]{:S(2)}) %copy-start.3) | copy-done | bytes 2097176
  26.5 11.5 %forward.1 = (bf16[2048,256]{1,0:T(8,128)(2,1)}, bf16[2048,256]{1,0:T(8,128)(2,1)S(1)}, bf16[512,256]{1,0:T(8,128)(2,1)S(1)}) custom-call(s32[9]{0:T(128)S(1)} %pad_add_fusion.place_ref, bf16[2048,1024]{1,0:T(8,128)(2,1)} %hub_ref.3, bf16[2048,256]{1,0:T(8,128)(2,1)S(1)} %copy-done.4, f32[2048,256]{1,0:T(8,128)} %copy-done.3, f32[2048,1]{1,0:T(8,128)S(1)} %copy.18.scale_ref, ...), custom_call_target="tpu_custom_call" | custom-call | flops 2415919104 | bytes 12582912 | tf_op jit(solution)/shard_map/forward/pallas_call | solution.py:188
  38.0 1.0 %copy-done.5 = bf16[2048,256]{1,0:T(8,128)(2,1)} copy-done((bf16[2048,256]{1,0:T(8,128)(2,1)}, bf16[2048,256]{1,0:T(8,128)(2,1)S(1)}, u32[]{:S(2)}) %copy-start.5) | copy-done | bytes 1048600
  39.0 0.7 copy-done.12
  39.7 5.3 %all-to-all-start = ((bf16[32,16,256]{2,1,0:T(8,128)(2,1)}), bf16[32,16,256]{2,1,0:T(8,128)(2,1)}, u32[]{:S(2)}, u32[]{:S(2)}) async-start(bf16[32,16,256]{2,1,0:T(8,128)(2,1)} %bitcast.28), calls=%async_computation | async-start | bytes 524288 | tf_op jit(solution)/shard_map/all_to_all | solution.py:459
  44.9 1.2 %copy-done.6 = bf16[2048,256]{1,0:T(8,128)(2,1)S(1)} copy-done((bf16[2048,256]{1,0:T(8,128)(2,1)S(1)}, bf16[2048,256]{1,0:T(8,128)(2,1)}, u32[]{:S(2)}) %copy-start.6) | copy-done | bytes 1048600
  46.2 8.9 %backward.1 = (bf16[2048,256]{1,0:T(8,128)(2,1)S(1)}, bf16[2,128,256]{2,1,0:T(8,128)(2,1)}, bf16[2,128,256]{2,1,0:T(8,128)(2,1)S(1)}, bf16[64,256]{1,0:T(8,128)(...) custom-call(s32[9]{0:T(128)S(1)} %pad_add_fusion.place_ref, ...), custom_call_target="tpu_custom_call" | custom-call | flops 1610612736 | bytes 7340032 | tf_op jit(solution)/shard_map/backward/pallas_call | solution.py:292
  55.1 1.0 %copy-done.8 = bf16[2048,256]{1,0:T(8,128)(2,1)} copy-done((bf16[2048,256]{1,0:T(8,128)(2,1)}, bf16[2048,256]{1,0:T(8,128)(2,1)S(1)}, u32[]{:S(2)}) %copy-start.8) | copy-done | bytes 1048600
  56.1 0.6 copy-done.15
  56.7 0.6 copy-done.17
  57.3 0.6 copy-done.18
  57.9 0.6 copy-done.19
  58.6 0.6 copy-done.20
  59.2 0.6 copy-done.21
  60.0 1.7 %collective-permute-start.9 = (bf16[2,128,256]{2,1,0:T(8,128)(2,1)}, bf16[2,128,256]{2,1,0:T(8,128)(2,1)S(1)}, u32[]{:S(2)}, u32[]{:S(2)}) collective-permute-start(bf16[2,128,256]{2,1,0:T(8,128)(2,1)} %get-tuple-element.26), channel_id=1, source_target_pairs={{0,1},{1,0},{2,3},{3,2},{4,5},{5,4},{6,7},{7,6},{8,9},{9,8},{10,11... | collective-permute-start | bytes 393224 | tf_op jit(solution)/shard_map/ppermute | solution.py:412
  62.1 0.8 pad_maximum_fusion.1
  62.9 1.7 %collective-permute-start.11 = (bf16[2,64,256]{2,1,0:T(8,128)(2,1)S(1)}, bf16[2,64,256]{2,1,0:T(8,128)(2,1)S(1)}, u32[]{:S(2)}, u32[]{:S(2)}) collective-permute-start(bf16[2,64,256]{2,1,0:T(8,128)(2,1)S(1)} %pad_maximum_fusion.1), channel_id=1, source_target_pairs={{0,16},{8,24},{16,0},{24,8},{1,17},{9,25},{17,1},{25,9},{2,18},{10... | collective-permute-start | bytes 196616 | tf_op jit(solution)/shard_map/ppermute | solution.py:412
  64.6 1.0 %reduce_sum.12 = bf16[16,256]{1,0:T(8,128)(2,1)S(1)} reduce(bf16[32,16,256]{2,1,0:T(8,128)(2,1)} %all-to-all-done, bf16[]{:T(256)} %constant.10.clone.1), dimensions={0}, to_apply=%region_0.0 | reduce | flops 126976 | bytes 270338 | tf_op jit(solution)/shard_map/reduce_sum | solution.py:472
  65.6 0.7 broadcast_in_dim.14
  66.3 4.6 %all-to-all-start.1 = ((bf16[32,16,256]{2,1,0:T(8,128)(2,1)}), bf16[32,16,256]{2,1,0:T(8,128)(2,1)S(1)}, u32[]{:S(2)}, u32[]{:S(2)}) async-start(bf16[32,16,256]{2,1,0:T(8,128)(2,1)} %broadcast_in_dim.14), calls=%async_computation.1 | async-start | bytes 524288 | tf_op jit(solution)/shard_map/all_to_all | solution.py:474
  70.9 0.9 fusion
  71.8 1.8 %collective-permute-start.15 = (bf16[128,256]{1,0:T(8,128)(2,1)S(1)}, bf16[128,256]{1,0:T(8,128)(2,1)S(1)}, u32[]{:S(2)}, u32[]{:S(2)}) collective-permute-start(bf16[128,256]{1,0:T(8,128)(2,1)S(1)} %fusion), channel_id=1, source_target_pairs={{0,2},{1,3},{2,0},{3,1},{4,6},{5,7},{6,4},{7,5},{8,10},{9,11},{10,... | collective-permute-start | bytes 196616 | tf_op jit(solution)/shard_map/ppermute | solution.py:412
  73.6 0.9 %fusion.1 = (bf16[128,256]{1,0:T(8,128)(2,1)S(1)}, bf16[128,256]{1,0:T(8,128)(2,1)S(1)}) fusion(bf16[128,256]{1,0:T(8,128)(2,1)} %copy-done.18, bf16[2,128,256]{2,1,0:T(8,128)(2,1)S(1)} %collective-permute-done.12, bf16[128,256]{1,0:T(8,128)(2,1)} %copy-done.19), kind=kLoop, calls=%fused_computation.3 | loop fusion | flops 262144 | bytes 393216 | tf_op jit(solution)/shard_map/convert_element_type | solution.py:469
  74.6 2.4 %collective-permute-start.13 = (bf16[128,256]{1,0:T(8,128)(2,1)S(1)}, bf16[128,256]{1,0:T(8,128)(2,1)S(1)}, u32[]{:S(2)}, u32[]{:S(2)}) collective-permute-start(bf16[128,256]{1,0:T(8,128)(2,1)S(1)} %get-tuple-element.39), channel_id=1, source_target_pairs={{0,6},{1,7},{2,4},{3,5},{4,2},{5,3},{6,0},{7,1},{8,14},{9,15},{10,... | collective-permute-start | bytes 196616 | tf_op jit(solution)/shard_map/ppermute | solution.py:412
  77.1 1.2 %copy-done.9 = bf16[2048,256]{1,0:T(8,128)(2,1)S(1)} copy-done((bf16[2048,256]{1,0:T(8,128)(2,1)S(1)}, bf16[2048,256]{1,0:T(8,128)(2,1)}, u32[]{:S(2)}) %copy-start.9) | copy-done | bytes 1048600
  78.3 7.1 %local_backward.1.local_ref = f32[2048,256]{1,0:T(8,128)S(1)} custom-call(s32[64,2]{1,0:T(8,128)S(1)} %copy.17.index_ref, bf16[64,128,128]{2,1,0:T(8,128)(2,1)} %bitcast.26, bf16[2048,256]{1,0:T(8,128)(2,1)S(1)} %copy-done.9, bf16[2048,256]{1,0:T(8,128)(2,1)S(1)} %copy-done.7, bf16[256,256]{1,0:T(8,128)(2,1)S(1)} %copy-done.11), custom_call_target="tpu_custom_call" | custom-call | flops 805306368 | bytes 6291456 | tf_op jit(solution)/shard_map/local_backward/pallas_call | solution.py:337
  85.5 0.4 collective-permute-done.14.rest_3_
  85.9 4.2 %finish.1 = bf16[2048,256]{1,0:T(8,128)(2,1)} custom-call(s32[9]{0:T(128)S(1)} %pad_add_fusion.place_ref, s32[1,256]{1,0:T(1,128)S(1)} %reshape_squeeze.7.rows_ref, f32[2048,256]{1,0:T(8,128)S(1)} %local_backward.1.local_ref, bf16[2,128,256]{2,1,0:T(8,128)(2,1)S(1)} %collective-permute-done.9.low_ref, bf16[64,256]{1,0:T(8,128)(2,1)S(1)} %get-tuple-element.27.own_ref, ...), custom_call_target="tpu_custom_call" | custom-call | flops 268435456 | bytes 3145728 | tf_op jit(solution)/shard_map/finish/pallas_call | solution.py:394
  90.2 0.8 fusion.3
  (57 shorter events, 0.9 us)
Async XLA Ops:
  2.1 1.2 %copy-start = (bf16[2048,256]{1,0:T(8,128)(2,1)S(1)}, bf16[2048,256]{1,0:T(8,128)(2,1)}, u32[]{:S(2)}) copy-start(bf16[2048,256]{1,0:T(8,128)(2,1)} %features_ref.5) | copy-start | bytes 3145732
  3.4 16.4 %copy-start.1 = (bf16[2048,256]{1,0:T(8,128)(2,1)S(1)}, bf16[2048,256]{1,0:T(8,128)(2,1)}, u32[]{:S(2)}) copy-start(bf16[2048,256]{1,0:T(8,128)(2,1)} %features_ref.5) | copy-start | bytes 3145732
  4.4 7.5 %collective-permute-start.7 = (bf16[2,64,256]{2,1,0:T(8,128)(2,1)S(1)}, bf16[2,64,256]{2,1,0:T(8,128)(2,1)S(1)}, u32[]{:S(2)}, u32[]{:S(2)}) collective-permute-start(bf16[2,64,256]{2,1,0:T(8,128)(2,1)S(1)} %get-tuple-element.21), channel_id=1, source_target_pairs={{0,8},{8,0},{16,24},{24,16},{1,9},{9,1},{17,25},{25,17},{2,10},{10... | collective-permute-start | bytes 196616 | tf_op jit(solution)/shard_map/ppermute | solution.py:412
  4.9 9.1 %collective-permute-start.1 = (bf16[128,256]{1,0:T(8,128)(2,1)S(1)}, bf16[128,256]{1,0:T(8,128)(2,1)}, u32[]{:S(2)}, u32[]{:S(2)}) collective-permute-start(bf16[128,256]{1,0:T(8,128)(2,1)S(1)} %slice.30.rest_0_), channel_id=1, source_target_pairs={{0,2},{1,3},{2,0},{3,1},{4,6},{5,7},{6,4},{7,5},{8,10},{9,11},{10,... | collective-permute-start | bytes 196616 | tf_op jit(solution)/shard_map/ppermute | solution.py:412
  7.6 7.8 %collective-permute-start.3 = (bf16[128,256]{1,0:T(8,128)(2,1)S(1)}, bf16[128,256]{1,0:T(8,128)(2,1)}, u32[]{:S(2)}, u32[]{:S(2)}) collective-permute-start(bf16[128,256]{1,0:T(8,128)(2,1)S(1)} %slice.30.rest_0_), channel_id=1, source_target_pairs={{0,4},{1,5},{2,6},{3,7},{4,0},{5,1},{6,2},{7,3},{8,12},{9,13},{10,... | collective-permute-start | bytes 196616 | tf_op jit(solution)/shard_map/ppermute | solution.py:412
  10.2 6.7 %collective-permute-start.5 = (bf16[128,256]{1,0:T(8,128)(2,1)S(1)}, bf16[128,256]{1,0:T(8,128)(2,1)}, u32[]{:S(2)}, u32[]{:S(2)}) collective-permute-start(bf16[128,256]{1,0:T(8,128)(2,1)S(1)} %slice.30.rest_0_), channel_id=1, source_target_pairs={{0,6},{1,7},{2,4},{3,5},{4,2},{5,3},{6,0},{7,1},{8,14},{9,15},{10,... | collective-permute-start | bytes 196616 | tf_op jit(solution)/shard_map/ppermute | solution.py:412
  10.2 16.2 %collective-permute-start = (bf16[128,256]{1,0:T(8,128)(2,1)S(1)}, bf16[128,256]{1,0:T(8,128)(2,1)}, u32[]{:S(2)}, u32[]{:S(2)}) collective-permute-start(bf16[128,256]{1,0:T(8,128)(2,1)S(1)} %slice.30.rest_0_), channel_id=1, source_target_pairs={{0,1},{1,0},{2,3},{3,2},{4,5},{5,4},{6,7},{7,6},{8,9},{9,8},{10,11... | collective-permute-start | bytes 196616 | tf_op jit(solution)/shard_map/ppermute | solution.py:412
  11.9 6.7 %copy-start.13 = (bf16[2,64,256]{2,1,0:T(8,128)(2,1)}, bf16[2,64,256]{2,1,0:T(8,128)(2,1)S(1)}, u32[]{:S(2)}) copy-start(bf16[2,64,256]{2,1,0:T(8,128)(2,1)S(1)} %collective-permute-done.7.rest_9_) | copy-start | bytes 196612
  12.6 13.9 %collective-permute-start.8 = (bf16[2,64,256]{2,1,0:T(8,128)(2,1)}, bf16[2,64,256]{2,1,0:T(8,128)(2,1)}, u32[]{:S(2)}, u32[]{:S(2)}) collective-permute-start(bf16[2,64,256]{2,1,0:T(8,128)(2,1)} %pad_maximum_fusion), channel_id=1, source_target_pairs={{0,16},{8,24},{16,0},{24,8},{1,17},{9,25},{17,1},{25,9},{2,18},{10... | collective-permute-start | bytes 196616 | tf_op jit(solution)/shard_map/ppermute | solution.py:412
  14.1 12.4 %collective-permute-start.2 = (bf16[128,256]{1,0:T(8,128)(2,1)}, bf16[128,256]{1,0:T(8,128)(2,1)}, u32[]{:S(2)}, u32[]{:S(2)}) collective-permute-start(bf16[128,256]{1,0:T(8,128)(2,1)} %collective-permute-done.1.rest_2_), channel_id=1, source_target_pairs={{0,1},{1,0},{2,3},{3,2},{4,5},{5,4},{6,7},{7,6},{8,9},{9,8},{10,11... | collective-permute-start | bytes 196616 | tf_op jit(solution)/shard_map/ppermute | solution.py:412
  15.4 11.0 %collective-permute-start.4 = (bf16[128,256]{1,0:T(8,128)(2,1)}, bf16[128,256]{1,0:T(8,128)(2,1)}, u32[]{:S(2)}, u32[]{:S(2)}) collective-permute-start(bf16[128,256]{1,0:T(8,128)(2,1)} %collective-permute-done.3.rest_4_), channel_id=1, source_target_pairs={{0,1},{1,0},{2,3},{3,2},{4,5},{5,4},{6,7},{7,6},{8,9},{9,8},{10,11... | collective-permute-start | bytes 196616 | tf_op jit(solution)/shard_map/ppermute | solution.py:412
  16.9 9.5 %collective-permute-start.6 = (bf16[128,256]{1,0:T(8,128)(2,1)}, bf16[128,256]{1,0:T(8,128)(2,1)}, u32[]{:S(2)}, u32[]{:S(2)}) collective-permute-start(bf16[128,256]{1,0:T(8,128)(2,1)} %collective-permute-done.5.rest_6_), channel_id=1, source_target_pairs={{0,1},{1,0},{2,3},{3,2},{4,5},{5,4},{6,7},{7,6},{8,9},{9,8},{10,11... | collective-permute-start | bytes 196616 | tf_op jit(solution)/shard_map/ppermute | solution.py:412
  19.8 1.6 %copy-start.2 = (bf16[1,64,128,128]{3,2,1,0:T(8,128)(2,1)S(1)}, bf16[1,64,128,128]{3,2,1,0:T(8,128)(2,1)}, u32[]{:S(2)}) copy-start(bf16[1,64,128,128]{3,2,1,0:T(8,128)(2,1)} %param.15) | copy-start | bytes 6291460
  21.3 5.1 %copy-start.4 = (bf16[2048,256]{1,0:T(8,128)(2,1)S(1)}, bf16[2048,256]{1,0:T(8,128)(2,1)}, u32[]{:S(2)}) copy-start(bf16[2048,256]{1,0:T(8,128)(2,1)} %cut_ref.3) | copy-start | bytes 3145732
  21.4 5.1 %copy-start.10 = (bf16[256,256]{1,0:T(8,128)(2,1)S(1)}, bf16[256,256]{1,0:T(8,128)(2,1)}, u32[]{:S(2)}) copy-start(bf16[256,256]{1,0:T(8,128)(2,1)} %neighbor_ref.3) | copy-start | bytes 393220
  21.4 5.1 %copy-start.11 = (bf16[256,256]{1,0:T(8,128)(2,1)S(1)}, bf16[256,256]{1,0:T(8,128)(2,1)}, u32[]{:S(2)}) copy-start(bf16[256,256]{1,0:T(8,128)(2,1)} %self_ref.3) | copy-start | bytes 393220
  21.4 5.1 %copy-start.14 = (bf16[2,64,256]{2,1,0:T(8,128)(2,1)S(1)}, bf16[2,64,256]{2,1,0:T(8,128)(2,1)}, u32[]{:S(2)}) copy-start(bf16[2,64,256]{2,1,0:T(8,128)(2,1)} %copy-done.13) | copy-start | bytes 196612
  25.1 1.4 %copy-start.3 = (f32[2048,256]{1,0:T(8,128)}, f32[2048,256]{1,0:T(8,128)S(1)}, u32[]{:S(2)}) copy-start(f32[2048,256]{1,0:T(8,128)S(1)} %local_forward.1.local_ref) | copy-start | bytes 6291460
  38.0 1.0 %copy-start.5 = (bf16[2048,256]{1,0:T(8,128)(2,1)}, bf16[2048,256]{1,0:T(8,128)(2,1)S(1)}, u32[]{:S(2)}) copy-start(bf16[2048,256]{1,0:T(8,128)(2,1)S(1)} %get-tuple-element.24.grad_ref) | copy-start | bytes 3145732
  39.0 0.7 copy-start.12
  39.7 24.9 %all-to-all-start = ((bf16[32,16,256]{2,1,0:T(8,128)(2,1)}), bf16[32,16,256]{2,1,0:T(8,128)(2,1)}, u32[]{:S(2)}, u32[]{:S(2)}) async-start(bf16[32,16,256]{2,1,0:T(8,128)(2,1)} %bitcast.28), calls=%async_computation | async-start | bytes 524288 | tf_op jit(solution)/shard_map/all_to_all | solution.py:459
  44.9 1.2 %copy-start.6 = (bf16[2048,256]{1,0:T(8,128)(2,1)S(1)}, bf16[2048,256]{1,0:T(8,128)(2,1)}, u32[]{:S(2)}) copy-start(bf16[2048,256]{1,0:T(8,128)(2,1)} %copy-done.5) | copy-start | bytes 3145732
  46.2 15.5 %copy-start.22 = (s32[1,4,64]{2,1,0:T(4,128)S(1)}, s32[1,4,64]{2,1,0:T(4,128)}, u32[]{:S(2)}) copy-start(s32[1,4,64]{2,1,0:T(4,128)} %param.19) | copy-start | bytes 3076
  55.1 1.0 %copy-start.8 = (bf16[2048,256]{1,0:T(8,128)(2,1)}, bf16[2048,256]{1,0:T(8,128)(2,1)S(1)}, u32[]{:S(2)}) copy-start(bf16[2048,256]{1,0:T(8,128)(2,1)S(1)} %get-tuple-element.25.aggregate_ref) | copy-start | bytes 3145732
  56.1 0.6 copy-start.15
  56.7 0.6 copy-start.17
  57.3 0.6 copy-start.18
  57.9 0.6 copy-start.19
  58.6 0.6 copy-start.20
  59.2 0.7 copy-start.21
  59.8 17.3 %copy-start.7 = (bf16[2048,256]{1,0:T(8,128)(2,1)S(1)}, bf16[2048,256]{1,0:T(8,128)(2,1)}, u32[]{:S(2)}) copy-start(bf16[2048,256]{1,0:T(8,128)(2,1)} %copy-done.5) | copy-start | bytes 3145732
  59.8 2.3 %collective-permute-start.10 = (bf16[2,64,256]{2,1,0:T(8,128)(2,1)}, bf16[2,64,256]{2,1,0:T(8,128)(2,1)S(1)}, u32[]{:S(2)}, u32[]{:S(2)}) collective-permute-start(bf16[2,64,256]{2,1,0:T(8,128)(2,1)} %get-tuple-element.28), channel_id=1, source_target_pairs={{0,8},{8,0},{16,24},{24,16},{1,9},{9,1},{17,25},{25,17},{2,10},{10... | collective-permute-start | bytes 196616 | tf_op jit(solution)/shard_map/ppermute | solution.py:412
  60.0 10.9 %collective-permute-start.9 = (bf16[2,128,256]{2,1,0:T(8,128)(2,1)}, bf16[2,128,256]{2,1,0:T(8,128)(2,1)S(1)}, u32[]{:S(2)}, u32[]{:S(2)}) collective-permute-start(bf16[2,128,256]{2,1,0:T(8,128)(2,1)} %get-tuple-element.26), channel_id=1, source_target_pairs={{0,1},{1,0},{2,3},{3,2},{4,5},{5,4},{6,7},{7,6},{8,9},{9,8},{10,11... | collective-permute-start | bytes 393224 | tf_op jit(solution)/shard_map/ppermute | solution.py:412
  61.8 11.9 %collective-permute-start.12 = (bf16[2,128,256]{2,1,0:T(8,128)(2,1)}, bf16[2,128,256]{2,1,0:T(8,128)(2,1)S(1)}, u32[]{:S(2)}, u32[]{:S(2)}) collective-permute-start(bf16[2,128,256]{2,1,0:T(8,128)(2,1)} %copy-done.21), channel_id=1, source_target_pairs={{0,1},{1,0},{2,3},{3,2},{4,5},{5,4},{6,7},{7,6},{8,9},{9,8},{10,11... | collective-permute-start | bytes 393224 | tf_op jit(solution)/shard_map/ppermute | solution.py:412
  62.9 22.6 %collective-permute-start.11 = (bf16[2,64,256]{2,1,0:T(8,128)(2,1)S(1)}, bf16[2,64,256]{2,1,0:T(8,128)(2,1)S(1)}, u32[]{:S(2)}, u32[]{:S(2)}) collective-permute-start(bf16[2,64,256]{2,1,0:T(8,128)(2,1)S(1)} %pad_maximum_fusion.1), channel_id=1, source_target_pairs={{0,16},{8,24},{16,0},{24,8},{1,17},{9,25},{17,1},{25,9},{2,18},{10... | collective-permute-start | bytes 196616 | tf_op jit(solution)/shard_map/ppermute | solution.py:412
  66.3 23.9 %all-to-all-start.1 = ((bf16[32,16,256]{2,1,0:T(8,128)(2,1)}), bf16[32,16,256]{2,1,0:T(8,128)(2,1)S(1)}, u32[]{:S(2)}, u32[]{:S(2)}) async-start(bf16[32,16,256]{2,1,0:T(8,128)(2,1)} %broadcast_in_dim.14), calls=%async_computation.1 | async-start | bytes 524288 | tf_op jit(solution)/shard_map/all_to_all | solution.py:474
  71.8 13.7 %collective-permute-start.15 = (bf16[128,256]{1,0:T(8,128)(2,1)S(1)}, bf16[128,256]{1,0:T(8,128)(2,1)S(1)}, u32[]{:S(2)}, u32[]{:S(2)}) collective-permute-start(bf16[128,256]{1,0:T(8,128)(2,1)S(1)} %fusion), channel_id=1, source_target_pairs={{0,2},{1,3},{2,0},{3,1},{4,6},{5,7},{6,4},{7,5},{8,10},{9,11},{10,... | collective-permute-start | bytes 196616 | tf_op jit(solution)/shard_map/ppermute | solution.py:412
  74.6 10.9 %collective-permute-start.13 = (bf16[128,256]{1,0:T(8,128)(2,1)S(1)}, bf16[128,256]{1,0:T(8,128)(2,1)S(1)}, u32[]{:S(2)}, u32[]{:S(2)}) collective-permute-start(bf16[128,256]{1,0:T(8,128)(2,1)S(1)} %get-tuple-element.39), channel_id=1, source_target_pairs={{0,6},{1,7},{2,4},{3,5},{4,2},{5,3},{6,0},{7,1},{8,14},{9,15},{10,... | collective-permute-start | bytes 196616 | tf_op jit(solution)/shard_map/ppermute | solution.py:412
  77.0 8.9 %collective-permute-start.14 = (bf16[128,256]{1,0:T(8,128)(2,1)S(1)}, bf16[128,256]{1,0:T(8,128)(2,1)S(1)}, u32[]{:S(2)}, u32[]{:S(2)}) collective-permute-start(bf16[128,256]{1,0:T(8,128)(2,1)S(1)} %get-tuple-element.38), channel_id=1, source_target_pairs={{0,4},{1,5},{2,6},{3,7},{4,0},{5,1},{6,2},{7,3},{8,12},{9,13},{10,... | collective-permute-start | bytes 196616 | tf_op jit(solution)/shard_map/ppermute | solution.py:412
  77.1 1.2 %copy-start.9 = (bf16[2048,256]{1,0:T(8,128)(2,1)S(1)}, bf16[2048,256]{1,0:T(8,128)(2,1)}, u32[]{:S(2)}) copy-start(bf16[2048,256]{1,0:T(8,128)(2,1)} %copy-done.8) | copy-start | bytes 3145732
  78.3 7.6 %copy-start.16 = (bf16[128,256]{1,0:T(8,128)(2,1)S(1)}, bf16[128,256]{1,0:T(8,128)(2,1)}, u32[]{:S(2)}) copy-start(bf16[128,256]{1,0:T(8,128)(2,1)} %copy-done.15) | copy-start | bytes 196612

commit v3 on v0

v3 whole, which is shorter than its diff:
```python
import jax
import jax.numpy as jnp
from jax import lax
from jax.experimental import pallas as pl
from jax.experimental.pallas import tpu as pltpu
from jax.sharding import PartitionSpec as P

TILE = 128
HUB = 128
CHUNK = 512
VMEM_LIMIT = 40 * 2**20
ROWS = (((0,), (0,)), ((), ()))
COLS = (((1,), (1,)), ((), ()))
F32 = jnp.float32
BF16 = jnp.bfloat16
ANY = pl.BlockSpec(memory_space=pl.ANY)
NEAR = pl.BlockSpec(memory_space=pltpu.VMEM)
SCALARS = pl.BlockSpec(memory_space=pltpu.SMEM)


def call(kernel, name, ins, outs, in_specs, out_specs, scratch, flops, moved):
    return pl.pallas_call(
        kernel,
        in_specs=in_specs,
        out_specs=out_specs,
        out_shape=[jax.ShapeDtypeStruct(shape, dtype) for shape, dtype in outs],
        scratch_shapes=scratch,
        compiler_params=pltpu.CompilerParams(vmem_limit_bytes=VMEM_LIMIT),
        cost_estimate=pl.CostEstimate(flops=flops, bytes_accessed=moved, transcendentals=0),
        name=name,
    )(*ins)


def dot(a, b, dims=(((1,), (0,)), ((), ()))):
    return lax.dot_general(a, b, dims, preferred_element_type=F32)


def aligned(start, size):
    return pl.ds(pl.multiple_of(start, size), size)


def copies(pairs, sems):
    started = [pltpu.make_async_copy(a, b, sems.at[i]) for i, (a, b) in enumerate(pairs)]
    for copy in started:
        copy.start()
    return started


def wait(started):
    for copy in started:
        copy.wait()


def pick_kernel(rows_ref, features_ref, own_ref, *rest):
    out_refs, (picked, sems) = rest[:-2], rest[-2:]
    groups, cut = rows_ref.shape[1:]
    count = features_ref.shape[0]
    group = lax.axis_index("grp")
    across = lax.broadcasted_iota(jnp.int32, (cut, cut), 0)
    along = lax.broadcasted_iota(jnp.int32, (cut, cut), 1)
    columns = []
    for j in range(groups):
        line = jnp.broadcast_to(rows_ref[0, j : j + 1, :].astype(F32), (cut, cut))
        columns.append(jnp.sum(jnp.where(across == along, line, 0.0), axis=1, keepdims=True))
    column = jnp.concatenate(columns, axis=0).astype(jnp.int32)
    where = lax.broadcasted_iota(jnp.int32, (groups * cut, count), 1)
    table = jnp.where(where == column, 1.0, 0.0).astype(BF16)
    picked[...] = dot(table, features_ref[...]).astype(BF16)
    sent = copies(
        [(picked.at[aligned((group ^ (k + 1)) * cut, cut)], ref) for k, ref in enumerate(out_refs)],
        sems,
    )
    own_ref[...] = picked[aligned(group * cut, cut), :]
    wait(sent)


def pick_rows(rows, features):
    _, groups, cut = rows.shape
    count, width = features.shape
    out = call(
        pick_kernel,
        "pick_rows",
        (rows, features),
        [((cut, width), BF16)] * groups,
        [NEAR, NEAR],
        [NEAR] + [ANY] * (groups - 1),
        [pltpu.VMEM((groups * cut, width), BF16), pltpu.SemaphoreType.DMA((groups - 1,))],
        2 * groups * cut * count * width,
        2 * count * width,
    )
    return out


def local_kernel(
    index_ref, values_ref, features_ref, degrees_ref, self_ref, sum_ref, base_ref, scale_ref, turned_ref
):
    count = features_ref.shape[0]
    base_ref[...] = dot(features_ref[...], self_ref[...])
    turned_ref[...] = features_ref[...].T
    scale = lax.rsqrt(degrees_ref[...].astype(F32))
    for j in range(count // TILE):
        line = jnp.broadcast_to(scale[j : j + 1, :], (TILE, TILE))
        scale_ref[j * TILE : (j + 1) * TILE, :] = line.T
    sum_ref[...] = jnp.zeros_like(sum_ref)
    for t in range(values_ref.shape[0]):
        row = aligned(index_ref[0, t, 0] * TILE, TILE)
        col = aligned(index_ref[0, t, 1] * TILE, TILE)
        sum_ref[row, :] += dot(values_ref[t], features_ref[col, :])


def local_forward(index, values, features, degrees, self_weight):
    tiles = values.shape[0]
    count, width = features.shape
    return call(
        local_kernel,
        "local_forward",
        (index, values, features, degrees.reshape(count // TILE, TILE), self_weight),
        [((count, width), F32), ((count, width), F32), ((count, TILE), F32), ((width, count), BF16)],
        [SCALARS, NEAR, NEAR, NEAR, NEAR],
        [NEAR] * 4,
        [],
        2 * tiles * TILE * TILE * width + 2 * count * width * width,
        2 * values.size + 6 * features.size,
    )


def forward_kernel(row_count, groups, *refs):
    owner_ref, hub_ref, cut_ref, local_ref, base_ref, scale_ref, features_ref, turned_ref = refs[:8]
    cotangent_ref, neighbor_ref, own_ref = refs[8:11]
    head_refs = refs[11 : 11 + row_count - 1]
    piece_refs = refs[10 + row_count : 9 + row_count + groups]
    hidden_ref, grad_ref, weights_ref = refs[9 + row_count + groups : 12 + row_count + groups]
    heads, panels, arrived, hidden, aggregated, weights, head_sems, piece_sems, out_sems = refs[
        12 + row_count + groups :
    ]
    sections = panels.shape[0] // HUB
    count, width = features_ref.shape
    cut = own_ref.shape[0]
    group, place = lax.axis_index("grp"), lax.axis_index("row")

    coming = copies([(ref, heads.at[k + 1]) for k, ref in enumerate(head_refs)], head_sems)
    coming += copies(
        [(ref, arrived.at[aligned((group ^ (k + 1)) * cut, cut)]) for k, ref in enumerate(piece_refs)],
        piece_sems,
    )
    heads[0] = features_ref[:HUB, :]
    arrived[aligned(group * cut, cut), :] = own_ref[...]
    wait(coming)
    for s in range(sections):
        panels[s * HUB : (s + 1) * HUB, :] = heads[owner_ref[0, s] ^ place]

    root = 0.7978845608028654
    going = []
    for c in range(count // CHUNK):
        part = slice(c * CHUNK, (c + 1) * CHUNK)
        summed = dot(hub_ref[part, :], panels[...]) + dot(cut_ref[part, :], arrived[...])
        summed = summed + local_ref[part, :]
        scale = jnp.concatenate([scale_ref[part, :]] * (width // TILE), axis=1)
        mixed = (summed * scale).astype(BF16)
        aggregated[part, :] = mixed
        before = base_ref[part, :] + dot(mixed, neighbor_ref[...])
        square = before * before
        bend = jnp.tanh(root * before * (1.0 + 0.044715 * square))
        half = 0.5 + 0.5 * bend
        hidden[part, :] = (before * half).astype(BF16)
        slope = half + (0.5 * root) * before * (1.0 - bend * bend) * (1.0 + (3 * 0.044715) * square)
        grad_ref[part, :] = (cotangent_ref[part, :].astype(F32) * slope).astype(BF16)
        out = pltpu.make_async_copy(hidden.at[part], hidden_ref.at[part], out_sems.at[c])
        out.start()
        going.append(out)
    grad = grad_ref[...]
    weights[:width, :] = dot(turned_ref[...], grad).astype(BF16)
    weights[width:, :] = dot(aggregated[...], grad, ROWS).astype(BF16)
    out = pltpu.make_async_copy(weights, weights_ref, out_sems.at[count // CHUNK])
    out.start()
    wait(going + [out])


def forward(owners, hub, cut, local, base, scale, features, turned, cotangent, neighbor_weight, own, heads, pieces):
    count, width = features.shape
    row_count, groups = len(heads) + 1, len(pieces) + 1
    flops = 2 * count * width * (hub.shape[1] + cut.shape[1] + 3 * width)

    def kernel(*refs):
        forward_kernel(row_count, groups, *refs)

    return call(
        kernel,
        "forward",
        (owners, hub, cut, local, base, scale, features, turned, cotangent, neighbor_weight, own, *heads, *pieces),
        [((count, width), BF16), ((count, width), BF16), ((2 * width, width), BF16)],
        [SCALARS] + [NEAR] * 10 + [ANY] * (row_count + groups - 2),
        [ANY, NEAR, ANY],
        [
            pltpu.VMEM((row_count, HUB, width), BF16),
            pltpu.VMEM((hub.shape[1], width), BF16),
            pltpu.VMEM((cut.shape[1], width), BF16),
            pltpu.VMEM((count, width), BF16),
            pltpu.VMEM((count, width), BF16),
            pltpu.VMEM((2 * width, width), BF16),
            pltpu.SemaphoreType.DMA((row_count - 1,)),
            pltpu.SemaphoreType.DMA((groups - 1,)),
            pltpu.SemaphoreType.DMA((count // CHUNK + 1,)),
        ],
        flops,
        2 * hub.size + 2 * cut.size + 14 * features.size,
    )


def backward_kernel(half, groups, *refs):
    owner_ref, hub_ref, cut_ref, scale_ref, grad_ref, neighbor_ref = refs[:6]
    aggregate_ref, own_ref = refs[6:8]
    even_refs = refs[8 : 8 + half]
    odd_ref = refs[8 + half]
    piece_refs = refs[9 + half : 8 + half + groups]
    heads, odds, back, sems = refs[8 + half + groups :]
    sections = hub_ref.shape[1] // HUB
    width = grad_ref.shape[1]
    cut = own_ref.shape[0]
    group, place = lax.axis_index("grp"), lax.axis_index("row")

    scale = jnp.concatenate([scale_ref[...]] * (width // TILE), axis=1)
    aggregate = (dot(grad_ref[...], neighbor_ref[...], COLS) * scale).astype(BF16)
    aggregate_ref[...] = aggregate
    heads[...] = jnp.zeros_like(heads)
    for s in range(sections):
        heads[owner_ref[0, s] ^ place] += dot(
            hub_ref[:, s * HUB : (s + 1) * HUB], aggregate_ref[...], ROWS
        )
    for j in range(half):
        odds[j] = heads[2 * j + 1].astype(BF16)
    sent = [pltpu.make_async_copy(odds, odd_ref, sems.at[0])]
    sent[0].start()
    for j, ref in enumerate(even_refs):
        ref[...] = heads[2 * j].astype(BF16)
    back[...] = dot(cut_ref[...], aggregate_ref[...], ROWS).astype(BF16)
    for k, ref in enumerate(piece_refs):
        piece = back.at[aligned((group ^ (k + 1)) * cut, cut)]
        sent.append(pltpu.make_async_copy(piece, ref, sems.at[k + 1]))
        sent[-1].start()
    own_ref[...] = back[aligned(group * cut, cut), :]
    wait(sent)


def backward(owners, hub, cut, scale, grad, neighbor_weight, groups, row_count):
    count, width = grad.shape
    half = row_count // 2
    piece = cut.shape[1] // groups

    def kernel(*refs):
        backward_kernel(half, groups, *refs)

    out = call(
        kernel,
        "backward",
        (owners, hub, cut, scale, grad, neighbor_weight),
        [((count, width), BF16), ((piece, width), BF16)]
        + [((HUB, width), BF16)] * half
        + [((half, HUB, width), BF16)]
        + [((piece, width), BF16)] * (groups - 1),
        [SCALARS] + [NEAR] * 5,
        [NEAR] * (2 + half) + [ANY] * groups,
        [
            pltpu.VMEM((row_count, HUB, width), F32),
            pltpu.VMEM((half, HUB, width), BF16),
            pltpu.VMEM((cut.shape[1], width), BF16),
            pltpu.SemaphoreType.DMA((groups,)),
        ],
        2 * count * width * (hub.shape[1] + cut.shape[1] + width),
        2 * hub.size + 2 * cut.size + 4 * grad.size,
    )
    return out[0], out[1], out[2 : 2 + half], out[2 + half], out[3 + half :]


def local_back_kernel(index_ref, values_ref, aggregate_ref, grad_ref, self_ref, out_ref):
    out_ref[...] = dot(grad_ref[...], self_ref[...], COLS)
    for t in range(values_ref.shape[0]):
        row = aligned(index_ref[0, t, 0] * TILE, TILE)
        col = aligned(index_ref[0, t, 1] * TILE, TILE)
        out_ref[col, :] += dot(values_ref[t], aggregate_ref[row, :], ROWS)


def local_backward(index, values, aggregate, grad, self_weight):
    tiles = values.shape[0]
    count, width = grad.shape
    return call(
        local_back_kernel,
        "local_backward",
        (index, values, aggregate, grad, self_weight),
        [((count, width), F32)],
        [SCALARS] + [NEAR] * 4,
        [NEAR],
        [],
        2 * tiles * TILE * TILE * width + 2 * count * width * width,
        2 * values.size + 8 * grad.size,
    )[0]


def finish_kernel(groups, *refs):
    rows_ref, local_ref, own_ref, mine_ref, side_ref = refs[:5]
    piece_refs = refs[5 : 4 + groups]
    head_refs = refs[4 + groups : -7]
    out_ref, returned, side, heads, result, sems, out_sems = refs[-7:]
    cut = own_ref.shape[0]
    count = local_ref.shape[0]
    picks = returned.shape[0]
    group = lax.axis_index("grp")

    coming = copies(
        [
            (ref, returned.at[aligned((group ^ (k + 1)) * cut, cut)])
            for k, ref in enumerate(piece_refs)
        ]
        + [(side_ref.at[0], side)]
        + [(ref, heads.at[k]) for k, ref in enumerate(head_refs)],
        sems,
    )
    returned[aligned(group * cut, cut), :] = own_ref[...]
    rows = jnp.concatenate([rows_ref[0, j : j + 1, :] for j in range(groups)], axis=1)
    wait(coming)
    going = []
    for c in range(count // CHUNK):
        part = slice(c * CHUNK, (c + 1) * CHUNK)
        where = lax.broadcasted_iota(jnp.int32, (CHUNK, picks), 0) + c * CHUNK
        table = jnp.where(where == rows, 1.0, 0.0).astype(BF16)
        total = local_ref[part, :] + dot(table, returned[...])
        result[part, :] = total.astype(BF16)
        if c == 0:
            extra = mine_ref[...].astype(F32) + side[...].astype(F32)
            for k in range(len(head_refs)):
                extra = extra + heads[k].astype(F32)
            result[:HUB, :] = (total[:HUB, :] + extra).astype(BF16)
        out = pltpu.make_async_copy(result.at[part], out_ref.at[part], out_sems.at[c])
        out.start()
        going.append(out)
    wait(going)


def finish(rows, local, own, mine, side, pieces, heads):
    count, width = local.shape
    groups = rows.shape[1]
    picks = groups * rows.shape[2]

    def kernel(*refs):
        finish_kernel(groups, *refs)

    return call(
        kernel,
        "finish",
        (rows, local, own, mine, side, *pieces, *heads),
        [((count, width), BF16)],
        [NEAR] * 4 + [ANY] * (1 + len(pieces) + len(heads)),
        [ANY],
        [
            pltpu.VMEM((picks, width), BF16),
            pltpu.VMEM((HUB, width), BF16),
            pltpu.VMEM((len(heads), HUB, width), BF16),
            pltpu.VMEM((count, width), BF16),
            pltpu.SemaphoreType.DMA((1 + len(pieces) + len(heads),)),
            pltpu.SemaphoreType.DMA((count // CHUNK,)),
        ],
        2 * count * picks * width,
        6 * local.size,
    )[0]


def trade(value, axis, k):
    return lax.ppermute(value, axis, [(r, r ^ k) for r in range(lax.axis_size(axis))])


def on_device(
    features,
    cotangent,
    self_weight,
    neighbor_weight,
    tile_values,
    tile_index,
    hub_adjacency,
    hub_owner,
    send_rows,
    cut_adjacency,
    degrees,
):
    count, width = features.shape
    groups = lax.axis_size("grp")
    row_count = lax.axis_size("row")
    everyone = ("grp", "row")
    device_count = groups * row_count
    values = tile_values[0]

    head = features[:HUB]
    evens = [head] + [trade(head, "row", k) for k in range(2, row_count, 2)]
    heads = [x for even in evens for x in (even, trade(even, "row", 1))][1:]
    own, *pieces = pick_rows(send_rows, features)
    pieces = [trade(piece, "grp", k + 1) for k, piece in enumerate(pieces)]
    local, base, scale, turned = local_forward(tile_index, values, features, degrees, self_weight)
    hidden, grad, weights = forward(
        hub_owner, hub_adjacency, cut_adjacency, local, base, scale, features, turned,
        cotangent, neighbor_weight, own, heads, pieces,
    )
    parts = lax.all_to_all(weights, everyone, split_axis=0, concat_axis=0, tiled=True)
    aggregate, own, evens, odds, pieces = backward(
        hub_owner, hub_adjacency, cut_adjacency, scale, grad, neighbor_weight, groups, row_count
    )
    odds = trade(odds, "row", 1)
    heads = [
        trade((even.astype(F32) + odds[j + 1].astype(F32)).astype(BF16), "row", 2 * j + 2)
        for j, even in enumerate(evens[1:])
    ]
    pieces = [trade(piece, "grp", k + 1) for k, piece in enumerate(pieces)]
    local_grad = local_backward(tile_index, values, aggregate, grad, self_weight)
    summed = jnp.sum(parts.reshape(device_count, -1, width).astype(F32), axis=0).astype(BF16)
    spread = jnp.broadcast_to(summed[None], (device_count, *summed.shape))
    spread = lax.all_to_all(spread, everyone, split_axis=0, concat_axis=0, tiled=True)
    weight_grads = spread.reshape(2 * width, width).astype(F32)
    grad_features = finish(send_rows, local_grad, own, evens[0], odds, pieces, heads)
    return hidden, grad_features, weight_grads[:width], weight_grads[width:]


def solution(mesh):
    nodes = P(("grp", "row"), None)
    in_specs = (
        nodes,
        nodes,
        P(),
        P(),
        P(("grp", "row"), None, None, None),
        P(("grp", "row"), None, None),
        nodes,
        P("grp", None),
        P(("grp", "row"), None, None),
        nodes,
        P(("grp", "row")),
    )
    out_specs = (nodes, nodes, P(), P())
    return jax.shard_map(
        on_device, mesh=mesh, in_specs=in_specs, out_specs=out_specs, check_vma=False
    )
```

time: 367 us -> 80.5 us (0.22)
  waiting for transfers between devices: 232 us -> 2.47 us
  matrix products: 57.5 us -> 0 us
  starting transfers between devices: 7.64 us -> 30.8 us
  local copies, waits for them, and re-layouts: 45.7 us -> 22.7 us
  Pallas kernels: 0 us -> 20.8 us
  between operations: 19.1 us -> 0.94 us
    psum x3 -> x0, waiting for transfers between devices: 231 us -> none  [the longest x1 114 us: on_device(): lax.psum((self_part, neighbor_part), ('grp', 'row'))]
    dot_general x23 -> x0, matrix products: 57.5 us -> none  [the longest x8 7.36 us: on_device(): jnp.dot(hub_adjacency[:, section * HUB:(section + 1) * HUB], panel, prefe...]
    dot_general x5 -> x0, local copies, waits for them, and re-layouts: 23.6 us -> none  [the longest x1 9.21 us: on_device(): jnp.einsum('lab,lbf->laf', values, picked, preferred_element_type=jnp.flo...]
    ppermute x0 -> x17, starting transfers between devices: none -> 21.1 us  [trade(): lax.ppermute(value, axis, [(r, r ^ k) for r in range(lax.axis_size(axis))])]
    pallas_call x0 -> x6, Pallas kernels: none -> 20.8 us  [call(): pl.pallas_call(kernel, in_specs=in_specs, out_specs=out_specs, out_shape=...]
    unnamed x51 -> x69, local copies, waits for them, and re-layouts: 7 us -> 19.3 us
    gather x3 -> x0, local copies, waits for them, and re-layouts: 8.64 us -> none  [the longest x1 3.01 us: on_device(): outgoing = features[send_rows[0]]]
    reshape x2 -> x0, local copies, waits for them, and re-layouts: 4.63 us -> none  [the longest x1 2.94 us: on_device(): local_sum = jnp.einsum('nl,laf->naf', row_select, product, precision=lax....]
  transfers between devices with their start and end apart: 5 -> 19, of which waited for: 3 -> 1; matrix products, arithmetic and copies ran while one was open for 16% -> 4% of each run, Pallas kernels for 0% -> 15%
where the time goes in v3:
time: 80.5 us; the launch traced here: 79.6 us
  starting transfers between devices  30.8 us (38%)
  local copies, waits for them, and re-layouts  22.7 us (28%)
  Pallas kernels  20.8 us (26%)
  waiting for transfers between devices  2.47 us (3%)
  other arithmetic  1.95 us (2%)
  between operations  0.94 us (1%)
    ppermute x17, starting transfers between devices, trade(): lax.ppermute(value, axis, [(r, r ^ k) for r in range(lax.axis_size(axis))])  21.1 us
    pallas_call x6, Pallas kernels, call(): pl.pallas_call(kernel, in_specs=in_specs, out_specs=out_specs, out_shape=...  20.8 us
    unnamed x69, local copies, waits for them, and re-layouts  19.3 us
    all_to_all x1, starting transfers between devices, on_device(): lax.all_to_all(spread, everyone, split_axis=0, concat_axis=0, tiled=True)  4.94 us
    all_to_all x1, starting transfers between devices, on_device(): lax.all_to_all(weights, everyone, split_axis=0, concat_axis=0, tiled=True)  4.71 us
    ppermute x17, waiting for transfers between devices, trade(): lax.ppermute(value, axis, [(r, r ^ k) for r in range(lax.axis_size(axis))])  2.46 us
    slice x1, local copies, waits for them, and re-layouts, on_device(): return (hidden, grad_features, weight_grads[:width], weight_grads[width:])  1.82 us
  transfers between devices with their start and end apart: 19, of which 1 were waited for; matrix products, arithmetic and copies ran while one was open for 4% of the time, Pallas kernels for 15%

profile of v3, /device:TPU:0, one launch (start us, length us, event | category | flops | bytes accessed | tf_op | source)
XLA Modules:
  0.0 79.6 jit_solution(17370977326961032621)
XLA Ops:
  0.6 0.9 %slice.24 = bf16[128,256]{1,0:T(8,128)(2,1)S(1)} slice(bf16[2048,256]{1,0:T(8,128)(2,1)} %refs_6_.1), slice={[0:128], [0:256]} | slice | bytes 131072 | tf_op jit(solution)/shard_map/slice | solution.py:391
  1.5 5.0 %collective-permute-start.5 = (bf16[128,256]{1,0:T(8,128)(2,1)S(1)}, bf16[128,256]{1,0:T(8,128)(2,1)S(1)}, u32[]{:S(2)}, u32[]{:S(2)}) collective-permute-start(bf16[128,256]{1,0:T(8,128)(2,1)S(1)} %slice.24), channel_id=1, source_target_pairs={{0,6},{1,7},{2,4},{3,5},{4,2},{5,3},{6,0},{7,1},{8,14},{9,15},{10,... | collective-permute-start | bytes 196616 | tf_op jit(solution)/shard_map/ppermute | solution.py:368
  6.6 0.6 collective-permute-start.1
  7.1 1.2 %copy-done.1 = bf16[2048,256]{1,0:T(8,128)(2,1)S(1)} copy-done((bf16[2048,256]{1,0:T(8,128)(2,1)S(1)}, bf16[2048,256]{1,0:T(8,128)(2,1)}, u32[]{:S(2)}) %copy-start.1) | copy-done | bytes 1048600
  8.4 0.7 copy-done.27
  9.1 0.8 pick_rows.1
  9.9 1.8 %collective-permute-start.8 = (bf16[64,256]{1,0:T(8,128)(2,1)S(1)}, bf16[64,256]{1,0:T(8,128)(2,1)S(1)}, u32[]{:S(2)}, u32[]{:S(2)}) collective-permute-start(bf16[64,256]{1,0:T(8,128)(2,1)S(1)} %get-tuple-element.31), channel_id=1, source_target_pairs={{0,16},{8,24},{16,0},{24,8},{1,17},{9,25},{17,1},{25,9},{2,18},{10... | collective-permute-start | bytes 98312 | tf_op jit(solution)/shard_map/ppermute | solution.py:368
  11.7 0.8 copy.15.index_ref
  12.5 1.6 %collective-permute-start = (bf16[128,256]{1,0:T(8,128)(2,1)S(1)}, bf16[128,256]{1,0:T(8,128)(2,1)S(1)}, u32[]{:S(2)}, u32[]{:S(2)}) collective-permute-start(bf16[128,256]{1,0:T(8,128)(2,1)S(1)} %slice.24), channel_id=1, source_target_pairs={{0,1},{1,0},{2,3},{3,2},{4,5},{5,4},{6,7},{7,6},{8,9},{9,8},{10,11... | collective-permute-start | bytes 196616 | tf_op jit(solution)/shard_map/ppermute | solution.py:368
  14.1 0.5 collective-permute-start.9
  14.6 1.5 %collective-permute-start.6 = (bf16[128,256]{1,0:T(8,128)(2,1)S(1)}, bf16[128,256]{1,0:T(8,128)(2,1)S(1)}, u32[]{:S(2)}, u32[]{:S(2)}) collective-permute-start(bf16[128,256]{1,0:T(8,128)(2,1)S(1)} %collective-permute-done.5.refs_16_), channel_id=1, source_target_pairs={{0,1},{1,0},{2,3},{3,2},{4,5},{5,4},{6,7},{7,6},{8,9},{9,8},{10,11... | collective-permute-start | bytes 196616 | tf_op jit(solution)/shard_map/ppermute | solution.py:368
  16.0 0.5 collective-permute-start.4
  16.6 1.5 %collective-permute-start.2 = (bf16[128,256]{1,0:T(8,128)(2,1)S(1)}, bf16[128,256]{1,0:T(8,128)(2,1)S(1)}, u32[]{:S(2)}, u32[]{:S(2)}) collective-permute-start(bf16[128,256]{1,0:T(8,128)(2,1)S(1)} %collective-permute-done.1.refs_12_), channel_id=1, source_target_pairs={{0,1},{1,0},{2,3},{3,2},{4,5},{5,4},{6,7},{7,6},{8,9},{9,8},{10,11... | collective-permute-start | bytes 196616 | tf_op jit(solution)/shard_map/ppermute | solution.py:368
  18.1 1.2 %copy-done.2 = bf16[2048,256]{1,0:T(8,128)(2,1)S(1)} copy-done((bf16[2048,256]{1,0:T(8,128)(2,1)S(1)}, bf16[2048,256]{1,0:T(8,128)(2,1)}, u32[]{:S(2)}) %copy-start.2) | copy-done | bytes 1048600
  19.3 1.6 %copy-done.4 = bf16[1,64,128,128]{3,2,1,0:T(8,128)(2,1)S(1)} copy-done((bf16[1,64,128,128]{3,2,1,0:T(8,128)(2,1)S(1)}, bf16[1,64,128,128]{3,2,1,0:T(8,128)(2,1)}, u32[]{:S(2)}) %copy-start.4) | copy-done | bytes 2097176
  20.9 0.9 %copy-done.14 = bf16[256,256]{1,0:T(8,128)(2,1)S(1)} copy-done((bf16[256,256]{1,0:T(8,128)(2,1)S(1)}, bf16[256,256]{1,0:T(8,128)(2,1)}, u32[]{:S(2)}) %copy-start.14) | copy-done | bytes 131096
  21.8 0.7 copy-done.29
  22.5 2.8 %local_forward.1 = (f32[2048,256]{1,0:T(8,128)S(1)}, f32[2048,256]{1,0:T(8,128)S(1)}, f32[2048,128]{1,0:T(8,128)S(1)}, bf16[256,2048]{1,0:T(8,128)(2,1)S(1)}) custom-call(s32[1,64,2]{2,1,0:T(8,128)S(1)} %copy.15.index_ref, bf16[64,128,128]{2,1,0:T(8,128)(2,1)S(1)} %bitcast.20, bf16[2048,256]{1,0:T(8,128)(2,1)S(1)} %copy-done.2, s32[16,128]{1,0:T(8,128)S(1)} %bitcast.22, ...), custom_call_target="tpu_custom_call" | custom-call | flops 805306368 | bytes 5242880 | tf_op jit(solution)/shard_map/local_forward/pallas_call | solution.py:22
  25.5 0.8 copy-done.26
  26.3 8.6 %forward.1 = (bf16[2048,256]{1,0:T(8,128)(2,1)}, bf16[2048,256]{1,0:T(8,128)(2,1)S(1)}, bf16[512,256]{1,0:T(8,128)(2,1)}) custom-call(s32[1,8]{1,0:T(1,128)S(1)} %copy-done.30, bf16[2048,1024]{1,0:T(8,128)(2,1)} %refs_1_.3, bf16[2048,256]{1,0:T(8,128)(2,1)S(1)} %copy-done.6, f32[2048,256]{1,0:T(8,128)S(1)} %get-tuple-element.25.refs_3_, ...), custom_call_target="tpu_custom_call" | custom-call | flops 2147483648 | bytes 12582912 | tf_op jit(solution)/shard_map/forward/pallas_call | solution.py:22
  34.8 4.7 %all-to-all-start = ((bf16[32,16,256]{2,1,0:T(8,128)(2,1)}), bf16[32,16,256]{2,1,0:T(8,128)(2,1)}, u32[]{:S(2)}, u32[]{:S(2)}) async-start(bf16[32,16,256]{2,1,0:T(8,128)(2,1)} %bitcast.5), calls=%async_computation | async-start | bytes 524288 | tf_op jit(solution)/shard_map/all_to_all | solution.py:401
  39.6 2.2 %copy-done = bf16[2048,1024]{1,0:T(8,128)(2,1)S(1)} copy-done((bf16[2048,1024]{1,0:T(8,128)(2,1)S(1)}, bf16[2048,1024]{1,0:T(8,128)(2,1)}, u32[]{:S(2)}) %copy-start) | copy-done | bytes 4194328
  41.7 1.2 %copy-done.7 = bf16[2048,256]{1,0:T(8,128)(2,1)S(1)} copy-done((bf16[2048,256]{1,0:T(8,128)(2,1)S(1)}, bf16[2048,256]{1,0:T(8,128)(2,1)}, u32[]{:S(2)}) %copy-start.7) | copy-done | bytes 1048600
  43.0 1.2 %copy-done.9 = f32[2048,128]{1,0:T(8,128)S(1)} copy-done((f32[2048,128]{1,0:T(8,128)S(1)}, f32[2048,128]{1,0:T(8,128)}, u32[]{:S(2)}) %copy-start.9) | copy-done | bytes 1048600
  44.2 3.8 %backward.1 = (bf16[2048,256]{1,0:T(8,128)(2,1)S(1)}, bf16[64,256]{1,0:T(8,128)(2,1)S(1)}, bf16[128,256]{1,0:T(8,128)(2,1)S(1)}, bf16[128,256]{1,0:T(8,128)(2,1)...) custom-call(s32[1,8]{1,0:T(1,128)S(1)} %copy-done.30, ...), custom_call_target="tpu_custom_call" | custom-call | flops 1610612736 | bytes 7340032 | tf_op jit(solution)/shard_map/backward/pallas_call | solution.py:22
  48.0 1.0 %copy-done.10 = bf16[2048,256]{1,0:T(8,128)(2,1)} copy-done((bf16[2048,256]{1,0:T(8,128)(2,1)}, bf16[2048,256]{1,0:T(8,128)(2,1)S(1)}, u32[]{:S(2)}) %copy-start.10) | copy-done | bytes 1048600
  49.0 0.6 copy-done.18
  49.6 0.6 copy-done.20
  50.2 0.6 copy-done.23
  50.9 0.6 copy-done.32
  51.5 0.6 copy-done.33
  52.1 0.6 copy-done.21
  52.7 1.7 %collective-permute-start.10 = (bf16[4,128,256]{2,1,0:T(8,128)(2,1)}, bf16[4,128,256]{2,1,0:T(8,128)(2,1)S(1)}, u32[]{:S(2)}, u32[]{:S(2)}) collective-permute-start(bf16[4,128,256]{2,1,0:T(8,128)(2,1)} %get-tuple-element.38), channel_id=1, source_target_pairs={{0,1},{1,0},{2,3},{3,2},{4,5},{5,4},{6,7},{7,6},{8,9},{9,8},{10,11... | collective-permute-start | bytes 786440 | tf_op jit(solution)/shard_map/ppermute | solution.py:368
  54.4 1.0 %reduce_sum.12 = bf16[16,256]{1,0:T(8,128)(2,1)S(1)} reduce(bf16[32,16,256]{2,1,0:T(8,128)(2,1)} %all-to-all-done, bf16[]{:T(256)} %constant.2.clone.1), dimensions={0}, to_apply=%region_0.0 | reduce | flops 126976 | bytes 270338 | tf_op jit(solution)/shard_map/reduce_sum | solution.py:412
  55.4 0.7 broadcast_in_dim.2
  56.2 4.9 %all-to-all-start.1 = ((bf16[32,16,256]{2,1,0:T(8,128)(2,1)}), bf16[32,16,256]{2,1,0:T(8,128)(2,1)}, u32[]{:S(2)}, u32[]{:S(2)}) async-start(bf16[32,16,256]{2,1,0:T(8,128)(2,1)} %broadcast_in_dim.2), calls=%async_computation.1 | async-start | bytes 524288 | tf_op jit(solution)/shard_map/all_to_all | solution.py:414
  61.1 0.1 collective-permute-start.11
  61.2 1.7 %collective-permute-start.12 = (bf16[64,256]{1,0:T(8,128)(2,1)}, bf16[64,256]{1,0:T(8,128)(2,1)S(1)}, u32[]{:S(2)}, u32[]{:S(2)}) collective-permute-start(bf16[64,256]{1,0:T(8,128)(2,1)} %copy-done.32), channel_id=1, source_target_pairs={{0,16},{8,24},{16,0},{24,8},{1,17},{9,25},{17,1},{25,9},{2,18},{10... | collective-permute-start | bytes 98312 | tf_op jit(solution)/shard_map/ppermute | solution.py:368
  62.9 0.2 collective-permute-start.13
  63.1 0.9 %fusion = (bf16[128,256]{1,0:T(8,128)(2,1)S(1)}, bf16[128,256]{1,0:T(8,128)(2,1)S(1)}, bf16[128,256]{1,0:T(8,128)(2,1)S(1)}) fusion(bf16[128,256]{1,0:T(8,128)(2,1)} %copy-done.22, bf16[4,128,256]{2,1,0:T(8,128)(2,1)S(1)} %collective-permute-done.10.refs_4_, bf16[128,256]{1,0:T(8,128)(2,1)} %copy-done.21, bf16[128,256]{1,0:T(8,128)(2,1)} %copy-done.20), kind=kLoop, calls=%fused_computation.1 | loop fusion | flops 393216 | bytes 589824 | tf_op jit(solution)/shard_map/convert_element_type | solution.py:407
  64.0 3.4 %collective-permute-start.16 = (bf16[128,256]{1,0:T(8,128)(2,1)S(1)}, bf16[128,256]{1,0:T(8,128)(2,1)S(1)}, u32[]{:S(2)}, u32[]{:S(2)}) collective-permute-start(bf16[128,256]{1,0:T(8,128)(2,1)S(1)} %get-tuple-element.48), channel_id=1, source_target_pairs={{0,6},{1,7},{2,4},{3,5},{4,2},{5,3},{6,0},{7,1},{8,14},{9,15},{10,... | collective-permute-start | bytes 196616 | tf_op jit(solution)/shard_map/ppermute | solution.py:368
  67.4 1.0 %collective-permute-start.14 = (bf16[128,256]{1,0:T(8,128)(2,1)S(1)}, bf16[128,256]{1,0:T(8,128)(2,1)S(1)}, u32[]{:S(2)}, u32[]{:S(2)}) collective-permute-start(bf16[128,256]{1,0:T(8,128)(2,1)S(1)} %get-tuple-element.50), channel_id=1, source_target_pairs={{0,2},{1,3},{2,0},{3,1},{4,6},{5,7},{6,4},{7,5},{8,10},{9,11},{10,... | collective-permute-start | bytes 196616 | tf_op jit(solution)/shard_map/ppermute | solution.py:368
  68.5 1.2 %copy-done.11 = bf16[2048,256]{1,0:T(8,128)(2,1)S(1)} copy-done((bf16[2048,256]{1,0:T(8,128)(2,1)S(1)}, bf16[2048,256]{1,0:T(8,128)(2,1)}, u32[]{:S(2)}) %copy-start.11) | copy-done | bytes 1048600
  69.7 0.8 copy-done.17
  70.5 2.9 %local_backward.1.refs_1_ = f32[2048,256]{1,0:T(8,128)S(1)} custom-call(s32[1,64,2]{2,1,0:T(8,128)S(1)} %copy-done.17, bf16[64,128,128]{2,1,0:T(8,128)(2,1)S(1)} %bitcast.21, bf16[2048,256]{1,0:T(8,128)(2,1)S(1)} %copy-done.11, bf16[2048,256]{1,0:T(8,128)(2,1)S(1)} %get-tuple-element.34.refs_4_.grad_ref, bf16[256,256]{1,0:T(8,128)(2,1)S(1)} %copy-done.15), custom_call_target="tpu_custom_call" | custom-call | flops 805306368 | bytes 6291456 | tf_op jit(solution)/shard_map/local_backward/pallas_call | solution.py:22
  73.4 2.4 %collective-permute-done.15.refs_9_ = bf16[128,256]{1,0:T(8,128)(2,1)S(1)} collective-permute-done((bf16[128,256]{1,0:T(8,128)(2,1)S(1)}, bf16[128,256]{1,0:T(8,128)(2,1)S(1)}, u32[]{:S(2)}, u32[]{:S(2)}) %collective-permute-start.15) | collective-permute-done | bytes 65568 | tf_op jit(solution)/shard_map/ppermute | solution.py:368
  75.8 1.9 %finish.1 = bf16[2048,256]{1,0:T(8,128)(2,1)} custom-call(s32[1,4,64]{2,1,0:T(4,128)S(1)} %copy-done.28, f32[2048,256]{1,0:T(8,128)S(1)} %local_backward.1.refs_1_, bf16[64,256]{1,0:T(8,128)(2,1)S(1)} %copy-done.24, bf16[128,256]{1,0:T(8,128)(2,1)S(1)} %copy-done.19, bf16[4,128,256]{2,1,0:T(8,128)(2,1)S(1)} %collective-permute-done.10.refs_4_, ...), custom_call_target="tpu_custom_call" | custom-call | flops 268435456 | bytes 3145728 | tf_op jit(solution)/shard_map/finish/pallas_call | solution.py:22
  77.8 1.8 %fusion.3 = (f32[16,16,256]{2,1,0:T(8,128)}, f32[16,16,256]{2,1,0:T(8,128)}) fusion(bf16[32,16,256]{2,1,0:T(8,128)(2,1)} %all-to-all-done.1), kind=kLoop, calls=%fused_computation.9 | loop fusion | bytes 1048576 | tf_op jit(solution)/shard_map/slice | solution.py:417
  (70 shorter events, 0.3 us)
Async XLA Ops:
  0.6 24.8 %copy-start.13 = (bf16[256,256]{1,0:T(8,128)(2,1)S(1)}, bf16[256,256]{1,0:T(8,128)(2,1)}, u32[]{:S(2)}) copy-start(bf16[256,256]{1,0:T(8,128)(2,1)} %refs_5_.1) | copy-start | bytes 393220
  1.5 13.0 %collective-permute-start.5 = (bf16[128,256]{1,0:T(8,128)(2,1)S(1)}, bf16[128,256]{1,0:T(8,128)(2,1)S(1)}, u32[]{:S(2)}, u32[]{:S(2)}) collective-permute-start(bf16[128,256]{1,0:T(8,128)(2,1)S(1)} %slice.24), channel_id=1, source_target_pairs={{0,6},{1,7},{2,4},{3,5},{4,2},{5,3},{6,0},{7,1},{8,14},{9,15},{10,... | collective-permute-start | bytes 196616 | tf_op jit(solution)/shard_map/ppermute | solution.py:368
  6.6 9.5 %collective-permute-start.3 = (bf16[128,256]{1,0:T(8,128)(2,1)S(1)}, bf16[128,256]{1,0:T(8,128)(2,1)S(1)}, u32[]{:S(2)}, u32[]{:S(2)}) collective-permute-start(bf16[128,256]{1,0:T(8,128)(2,1)S(1)} %slice.24), channel_id=1, source_target_pairs={{0,4},{1,5},{2,6},{3,7},{4,0},{5,1},{6,2},{7,3},{8,12},{9,13},{10,... | collective-permute-start | bytes 196616 | tf_op jit(solution)/shard_map/ppermute | solution.py:368
  6.6 10.0 %collective-permute-start.1 = (bf16[128,256]{1,0:T(8,128)(2,1)S(1)}, bf16[128,256]{1,0:T(8,128)(2,1)S(1)}, u32[]{:S(2)}, u32[]{:S(2)}) collective-permute-start(bf16[128,256]{1,0:T(8,128)(2,1)S(1)} %slice.24), channel_id=1, source_target_pairs={{0,2},{1,3},{2,0},{3,1},{4,6},{5,7},{6,4},{7,5},{8,10},{9,11},{10,... | collective-permute-start | bytes 196616 | tf_op jit(solution)/shard_map/ppermute | solution.py:368
  7.1 1.2 %copy-start.1 = (bf16[2048,256]{1,0:T(8,128)(2,1)S(1)}, bf16[2048,256]{1,0:T(8,128)(2,1)}, u32[]{:S(2)}) copy-start(bf16[2048,256]{1,0:T(8,128)(2,1)} %refs_6_.1) | copy-start | bytes 3145732
  8.4 0.7 copy-start.27
  9.0 16.4 %copy-start.3 = (bf16[2048,256]{1,0:T(8,128)(2,1)S(1)}, bf16[2048,256]{1,0:T(8,128)(2,1)}, u32[]{:S(2)}) copy-start(bf16[2048,256]{1,0:T(8,128)(2,1)} %refs_6_.1) | copy-start | bytes 3145732
  9.0 16.4 %copy-start.30 = (s32[1,8]{1,0:T(1,128)S(1)}, s32[1,8]{1,0:T(1,128)}, u32[]{:S(2)}) copy-start(s32[1,8]{1,0:T(1,128)} %refs_0_.4) | copy-start | bytes 100
  9.8 2.7 %collective-permute-start.7 = (bf16[64,256]{1,0:T(8,128)(2,1)S(1)}, bf16[64,256]{1,0:T(8,128)(2,1)S(1)}, u32[]{:S(2)}, u32[]{:S(2)}) collective-permute-start(bf16[64,256]{1,0:T(8,128)(2,1)S(1)} %get-tuple-element.30), channel_id=1, source_target_pairs={{0,8},{8,0},{16,24},{24,16},{1,9},{9,1},{17,25},{25,17},{2,10},{10... | collective-permute-start | bytes 98312 | tf_op jit(solution)/shard_map/ppermute | solution.py:368
  9.9 4.1 %collective-permute-start.8 = (bf16[64,256]{1,0:T(8,128)(2,1)S(1)}, bf16[64,256]{1,0:T(8,128)(2,1)S(1)}, u32[]{:S(2)}, u32[]{:S(2)}) collective-permute-start(bf16[64,256]{1,0:T(8,128)(2,1)S(1)} %get-tuple-element.31), channel_id=1, source_target_pairs={{0,16},{8,24},{16,0},{24,8},{1,17},{9,25},{17,1},{25,9},{2,18},{10... | collective-permute-start | bytes 98312 | tf_op jit(solution)/shard_map/ppermute | solution.py:368
  12.5 12.9 %copy-start.16 = (s32[1,64,2]{2,1,0:T(8,128)}, s32[1,64,2]{2,1,0:T(8,128)S(1)}, u32[]{:S(2)}) copy-start(s32[1,64,2]{2,1,0:T(8,128)S(1)} %copy.15.index_ref) | copy-start | bytes 1540
  12.5 12.8 %collective-permute-start = (bf16[128,256]{1,0:T(8,128)(2,1)S(1)}, bf16[128,256]{1,0:T(8,128)(2,1)S(1)}, u32[]{:S(2)}, u32[]{:S(2)}) collective-permute-start(bf16[128,256]{1,0:T(8,128)(2,1)S(1)} %slice.24), channel_id=1, source_target_pairs={{0,1},{1,0},{2,3},{3,2},{4,5},{5,4},{6,7},{7,6},{8,9},{9,8},{10,11... | collective-permute-start | bytes 196616 | tf_op jit(solution)/shard_map/ppermute | solution.py:368
  14.1 11.3 %copy-start.25 = (bf16[64,256]{1,0:T(8,128)(2,1)}, bf16[64,256]{1,0:T(8,128)(2,1)S(1)}, u32[]{:S(2)}) copy-start(bf16[64,256]{1,0:T(8,128)(2,1)S(1)} %collective-permute-done.8.refs_19_) | copy-start | bytes 98308
  14.1 11.3 %collective-permute-start.9 = (bf16[64,256]{1,0:T(8,128)(2,1)S(1)}, bf16[64,256]{1,0:T(8,128)(2,1)S(1)}, u32[]{:S(2)}, u32[]{:S(2)}) collective-permute-start(bf16[64,256]{1,0:T(8,128)(2,1)S(1)} %get-tuple-element.32), channel_id=1, source_target_pairs={{0,24},{8,16},{16,8},{24,0},{1,25},{9,17},{17,9},{25,1},{2,26},{10... | collective-permute-start | bytes 98312 | tf_op jit(solution)/shard_map/ppermute | solution.py:368
  14.6 10.8 %collective-permute-start.6 = (bf16[128,256]{1,0:T(8,128)(2,1)S(1)}, bf16[128,256]{1,0:T(8,128)(2,1)S(1)}, u32[]{:S(2)}, u32[]{:S(2)}) collective-permute-start(bf16[128,256]{1,0:T(8,128)(2,1)S(1)} %collective-permute-done.5.refs_16_), channel_id=1, source_target_pairs={{0,1},{1,0},{2,3},{3,2},{4,5},{5,4},{6,7},{7,6},{8,9},{9,8},{10,11... | collective-permute-start | bytes 196616 | tf_op jit(solution)/shard_map/ppermute | solution.py:368
  16.0 9.3 %collective-permute-start.4 = (bf16[128,256]{1,0:T(8,128)(2,1)S(1)}, bf16[128,256]{1,0:T(8,128)(2,1)S(1)}, u32[]{:S(2)}, u32[]{:S(2)}) collective-permute-start(bf16[128,256]{1,0:T(8,128)(2,1)S(1)} %collective-permute-done.3.refs_14_), channel_id=1, source_target_pairs={{0,1},{1,0},{2,3},{3,2},{4,5},{5,4},{6,7},{7,6},{8,9},{9,8},{10,11... | collective-permute-start | bytes 196616 | tf_op jit(solution)/shard_map/ppermute | solution.py:368
  16.6 8.8 %collective-permute-start.2 = (bf16[128,256]{1,0:T(8,128)(2,1)S(1)}, bf16[128,256]{1,0:T(8,128)(2,1)S(1)}, u32[]{:S(2)}, u32[]{:S(2)}) collective-permute-start(bf16[128,256]{1,0:T(8,128)(2,1)S(1)} %collective-permute-done.1.refs_12_), channel_id=1, source_target_pairs={{0,1},{1,0},{2,3},{3,2},{4,5},{5,4},{6,7},{7,6},{8,9},{9,8},{10,11... | collective-permute-start | bytes 196616 | tf_op jit(solution)/shard_map/ppermute | solution.py:368
  18.1 1.2 %copy-start.2 = (bf16[2048,256]{1,0:T(8,128)(2,1)S(1)}, bf16[2048,256]{1,0:T(8,128)(2,1)}, u32[]{:S(2)}) copy-start(bf16[2048,256]{1,0:T(8,128)(2,1)} %refs_6_.1) | copy-start | bytes 3145732
  19.3 1.6 %copy-start.4 = (bf16[1,64,128,128]{3,2,1,0:T(8,128)(2,1)S(1)}, bf16[1,64,128,128]{3,2,1,0:T(8,128)(2,1)}, u32[]{:S(2)}) copy-start(bf16[1,64,128,128]{3,2,1,0:T(8,128)(2,1)} %param.15) | copy-start | bytes 6291460
  20.9 0.9 %copy-start.14 = (bf16[256,256]{1,0:T(8,128)(2,1)S(1)}, bf16[256,256]{1,0:T(8,128)(2,1)}, u32[]{:S(2)}) copy-start(bf16[256,256]{1,0:T(8,128)(2,1)} %self_ref.3) | copy-start | bytes 393220
  21.8 0.7 copy-start.29
  22.5 2.9 %copy-start.6 = (bf16[2048,256]{1,0:T(8,128)(2,1)S(1)}, bf16[2048,256]{1,0:T(8,128)(2,1)}, u32[]{:S(2)}) copy-start(bf16[2048,256]{1,0:T(8,128)(2,1)} %refs_2_.3) | copy-start | bytes 3145732
  22.5 2.9 %copy-start.12 = (bf16[2048,256]{1,0:T(8,128)(2,1)S(1)}, bf16[2048,256]{1,0:T(8,128)(2,1)}, u32[]{:S(2)}) copy-start(bf16[2048,256]{1,0:T(8,128)(2,1)} %refs_8_.1) | copy-start | bytes 3145732
  25.3 9.5 %copy-start.8 = (f32[2048,128]{1,0:T(8,128)}, f32[2048,128]{1,0:T(8,128)S(1)}, u32[]{:S(2)}) copy-start(f32[2048,128]{1,0:T(8,128)S(1)} %get-tuple-element.27.refs_5_.refs_3_) | copy-start | bytes 3145732
  25.5 0.8 %copy-start.26 = (bf16[64,256]{1,0:T(8,128)(2,1)S(1)}, bf16[64,256]{1,0:T(8,128)(2,1)}, u32[]{:S(2)}) copy-start(bf16[64,256]{1,0:T(8,128)(2,1)} %copy-done.25) | copy-start | bytes 98308
  34.8 19.6 %all-to-all-start = ((bf16[32,16,256]{2,1,0:T(8,128)(2,1)}), bf16[32,16,256]{2,1,0:T(8,128)(2,1)}, u32[]{:S(2)}, u32[]{:S(2)}) async-start(bf16[32,16,256]{2,1,0:T(8,128)(2,1)} %bitcast.5), calls=%async_computation | async-start | bytes 524288 | tf_op jit(solution)/shard_map/all_to_all | solution.py:401
  39.6 2.2 %copy-start = (bf16[2048,1024]{1,0:T(8,128)(2,1)S(1)}, bf16[2048,1024]{1,0:T(8,128)(2,1)}, u32[]{:S(2)}) copy-start(bf16[2048,1024]{1,0:T(8,128)(2,1)} %refs_1_.3) | copy-start | bytes 12582916
  41.7 1.2 %copy-start.7 = (bf16[2048,256]{1,0:T(8,128)(2,1)S(1)}, bf16[2048,256]{1,0:T(8,128)(2,1)}, u32[]{:S(2)}) copy-start(bf16[2048,256]{1,0:T(8,128)(2,1)} %refs_2_.3) | copy-start | bytes 3145732
  43.0 1.2 %copy-start.9 = (f32[2048,128]{1,0:T(8,128)S(1)}, f32[2048,128]{1,0:T(8,128)}, u32[]{:S(2)}) copy-start(f32[2048,128]{1,0:T(8,128)} %copy-done.8) | copy-start | bytes 3145732
  44.2 24.3 %copy-start.5 = (bf16[1,64,128,128]{3,2,1,0:T(8,128)(2,1)S(1)}, bf16[1,64,128,128]{3,2,1,0:T(8,128)(2,1)}, u32[]{:S(2)}) copy-start(bf16[1,64,128,128]{3,2,1,0:T(8,128)(2,1)} %param.15) | copy-start | bytes 6291460
  44.2 24.3 %copy-start.15 = (bf16[256,256]{1,0:T(8,128)(2,1)S(1)}, bf16[256,256]{1,0:T(8,128)(2,1)}, u32[]{:S(2)}) copy-start(bf16[256,256]{1,0:T(8,128)(2,1)} %self_ref.3) | copy-start | bytes 393220
  48.0 1.0 %copy-start.10 = (bf16[2048,256]{1,0:T(8,128)(2,1)}, bf16[2048,256]{1,0:T(8,128)(2,1)S(1)}, u32[]{:S(2)}) copy-start(bf16[2048,256]{1,0:T(8,128)(2,1)S(1)} %get-tuple-element.35.aggregate_ref) | copy-start | bytes 3145732
  49.0 0.6 copy-start.18
  52.1 0.7 copy-start.22
  52.1 0.7 copy-start.31
  52.7 10.3 %collective-permute-start.10 = (bf16[4,128,256]{2,1,0:T(8,128)(2,1)}, bf16[4,128,256]{2,1,0:T(8,128)(2,1)S(1)}, u32[]{:S(2)}, u32[]{:S(2)}) collective-permute-start(bf16[4,128,256]{2,1,0:T(8,128)(2,1)} %get-tuple-element.38), channel_id=1, source_target_pairs={{0,1},{1,0},{2,3},{3,2},{4,5},{5,4},{6,7},{7,6},{8,9},{9,8},{10,11... | collective-permute-start | bytes 786440 | tf_op jit(solution)/shard_map/ppermute | solution.py:368
  56.2 21.6 %all-to-all-start.1 = ((bf16[32,16,256]{2,1,0:T(8,128)(2,1)}), bf16[32,16,256]{2,1,0:T(8,128)(2,1)}, u32[]{:S(2)}, u32[]{:S(2)}) async-start(bf16[32,16,256]{2,1,0:T(8,128)(2,1)} %broadcast_in_dim.2), calls=%async_computation.1 | async-start | bytes 524288 | tf_op jit(solution)/shard_map/all_to_all | solution.py:414
  61.1 6.3 %collective-permute-start.11 = (bf16[64,256]{1,0:T(8,128)(2,1)}, bf16[64,256]{1,0:T(8,128)(2,1)S(1)}, u32[]{:S(2)}, u32[]{:S(2)}) collective-permute-start(bf16[64,256]{1,0:T(8,128)(2,1)} %copy-done.33), channel_id=1, source_target_pairs={{0,8},{8,0},{16,24},{24,16},{1,9},{9,1},{17,25},{25,17},{2,10},{10... | collective-permute-start | bytes 98312 | tf_op jit(solution)/shard_map/ppermute | solution.py:368
  61.2 12.2 %collective-permute-start.12 = (bf16[64,256]{1,0:T(8,128)(2,1)}, bf16[64,256]{1,0:T(8,128)(2,1)S(1)}, u32[]{:S(2)}, u32[]{:S(2)}) collective-permute-start(bf16[64,256]{1,0:T(8,128)(2,1)} %copy-done.32), channel_id=1, source_target_pairs={{0,16},{8,24},{16,0},{24,8},{1,17},{9,25},{17,1},{25,9},{2,18},{10... | collective-permute-start | bytes 98312 | tf_op jit(solution)/shard_map/ppermute | solution.py:368
  62.9 10.5 %collective-permute-start.13 = (bf16[64,256]{1,0:T(8,128)(2,1)}, bf16[64,256]{1,0:T(8,128)(2,1)S(1)}, u32[]{:S(2)}, u32[]{:S(2)}) collective-permute-start(bf16[64,256]{1,0:T(8,128)(2,1)} %copy-done.31), channel_id=1, source_target_pairs={{0,24},{8,16},{16,8},{24,0},{1,25},{9,17},{17,9},{25,1},{2,26},{10... | collective-permute-start | bytes 98312 | tf_op jit(solution)/shard_map/ppermute | solution.py:368
  64.0 9.4 %collective-permute-start.16 = (bf16[128,256]{1,0:T(8,128)(2,1)S(1)}, bf16[128,256]{1,0:T(8,128)(2,1)S(1)}, u32[]{:S(2)}, u32[]{:S(2)}) collective-permute-start(bf16[128,256]{1,0:T(8,128)(2,1)S(1)} %get-tuple-element.48), channel_id=1, source_target_pairs={{0,6},{1,7},{2,4},{3,5},{4,2},{5,3},{6,0},{7,1},{8,14},{9,15},{10,... | collective-permute-start | bytes 196616 | tf_op jit(solution)/shard_map/ppermute | solution.py:368
  67.4 8.4 %collective-permute-start.15 = (bf16[128,256]{1,0:T(8,128)(2,1)S(1)}, bf16[128,256]{1,0:T(8,128)(2,1)S(1)}, u32[]{:S(2)}, u32[]{:S(2)}) collective-permute-start(bf16[128,256]{1,0:T(8,128)(2,1)S(1)} %get-tuple-element.49), channel_id=1, source_target_pairs={{0,4},{1,5},{2,6},{3,7},{4,0},{5,1},{6,2},{7,3},{8,12},{9,13},{10,... | collective-permute-start | bytes 196616 | tf_op jit(solution)/shard_map/ppermute | solution.py:368
  67.4 8.4 %collective-permute-start.14 = (bf16[128,256]{1,0:T(8,128)(2,1)S(1)}, bf16[128,256]{1,0:T(8,128)(2,1)S(1)}, u32[]{:S(2)}, u32[]{:S(2)}) collective-permute-start(bf16[128,256]{1,0:T(8,128)(2,1)S(1)} %get-tuple-element.50), channel_id=1, source_target_pairs={{0,2},{1,3},{2,0},{3,1},{4,6},{5,7},{6,4},{7,5},{8,10},{9,11},{10,... | collective-permute-start | bytes 196616 | tf_op jit(solution)/shard_map/ppermute | solution.py:368
  68.5 1.2 %copy-start.11 = (bf16[2048,256]{1,0:T(8,128)(2,1)S(1)}, bf16[2048,256]{1,0:T(8,128)(2,1)}, u32[]{:S(2)}) copy-start(bf16[2048,256]{1,0:T(8,128)(2,1)} %copy-done.10) | copy-start | bytes 3145732
  69.7 0.8 copy-start.17
  70.5 5.4 %copy-start.19 = (bf16[128,256]{1,0:T(8,128)(2,1)S(1)}, bf16[128,256]{1,0:T(8,128)(2,1)}, u32[]{:S(2)}) copy-start(bf16[128,256]{1,0:T(8,128)(2,1)} %copy-done.18) | copy-start | bytes 196612
  70.5 5.4 %copy-start.24 = (bf16[64,256]{1,0:T(8,128)(2,1)S(1)}, bf16[64,256]{1,0:T(8,128)(2,1)}, u32[]{:S(2)}) copy-start(bf16[64,256]{1,0:T(8,128)(2,1)} %copy-done.23) | copy-start | bytes 98308
  70.5 5.4 %copy-start.28 = (s32[1,4,64]{2,1,0:T(4,128)S(1)}, s32[1,4,64]{2,1,0:T(4,128)}, u32[]{:S(2)}) copy-start(s32[1,4,64]{2,1,0:T(4,128)} %refs_0_.5) | copy-start | bytes 3076
  (5 other events, 3.1 us)

commit v4 on v0

v4 whole, which is shorter than its diff:
```python
import jax
import jax.numpy as jnp
from jax import lax
from jax.experimental import pallas as pl
from jax.experimental.pallas import tpu as pltpu
from jax.sharding import PartitionSpec as P

TILE = 128
HUB = 128
CHUNK = 512
TILE_STEP = 16
VMEM_LIMIT = 62 * 2**20
ROWS = (((0,), (0,)), ((), ()))
COLS = (((1,), (1,)), ((), ()))
F32 = jnp.float32
BF16 = jnp.bfloat16
ANY = pl.BlockSpec(memory_space=pl.ANY)
NEAR = pl.BlockSpec(memory_space=pltpu.VMEM)
SCALARS = pl.BlockSpec(memory_space=pltpu.SMEM)


def call(kernel, name, ins, outs, in_specs, out_specs, scratch, flops, moved):
    return pl.pallas_call(
        kernel,
        in_specs=in_specs,
        out_specs=out_specs,
        out_shape=[jax.ShapeDtypeStruct(shape, dtype) for shape, dtype in outs],
        scratch_shapes=scratch,
        compiler_params=pltpu.CompilerParams(vmem_limit_bytes=VMEM_LIMIT),
        cost_estimate=pl.CostEstimate(flops=flops, bytes_accessed=moved, transcendentals=0),
        name=name,
    )(*ins)


def dot(a, b, dims=(((1,), (0,)), ((), ()))):
    return lax.dot_general(a, b, dims, preferred_element_type=F32)


def aligned(start, size):
    return pl.ds(pl.multiple_of(start, size), size)


class Mover:
    def __init__(self, sems):
        self.sems, self.used, self.out = sems, 0, []

    def get(self, source, target):
        copy = pltpu.make_async_copy(source, target, self.sems.at[self.used])
        self.used += 1
        copy.start()
        return copy

    def put(self, source, target):
        self.out.append(self.get(source, target))

    def drain(self):
        wait(self.out)


def wait(started):
    for copy in started:
        copy.wait()


def split(count, step):
    return [slice(i, i + step) for i in range(0, count, step)]


def pick_kernel(rows_ref, features_ref, head_ref, *rest):
    out_refs, (features, picked, sems) = rest[:-3], rest[-3:]
    groups, cut = rows_ref.shape[1:]
    count = features_ref.shape[0]
    group = lax.axis_index("grp")
    mover = Mover(sems)
    parts = split(count, CHUNK)
    coming = [mover.get(features_ref.at[part], features.at[part]) for part in parts]
    across = lax.broadcasted_iota(jnp.int32, (cut, cut), 0)
    along = lax.broadcasted_iota(jnp.int32, (cut, cut), 1)
    columns = []
    for j in range(groups):
        line = jnp.broadcast_to(rows_ref[0, j : j + 1, :].astype(F32), (cut, cut))
        columns.append(jnp.sum(jnp.where(across == along, line, 0.0), axis=1, keepdims=True))
    column = jnp.concatenate(columns, axis=0).astype(jnp.int32)
    where = lax.broadcasted_iota(jnp.int32, (groups * cut, count), 1)
    table = jnp.where(where == column, 1.0, 0.0).astype(BF16)
    wait(coming)
    mover.put(features.at[:HUB], head_ref)
    picked[...] = dot(table, features[...]).astype(BF16)
    for k, ref in enumerate(out_refs):
        mover.put(picked.at[aligned((group ^ k) * cut, cut)], ref)
    mover.drain()


def pick_rows(rows, features):
    _, groups, cut = rows.shape
    count, width = features.shape
    return call(
        pick_kernel,
        "pick_rows",
        (rows, features),
        [((HUB, width), BF16)] + [((cut, width), BF16)] * groups,
        [NEAR, ANY],
        [ANY] * (1 + groups),
        [
            pltpu.VMEM((count, width), BF16),
            pltpu.VMEM((groups * cut, width), BF16),
            pltpu.SemaphoreType.DMA((1 + groups + count // CHUNK,)),
        ],
        2 * groups * cut * count * width,
        2 * count * width,
    )


def scale_of(degrees_ref, part, width):
    lines = lax.rsqrt(degrees_ref[part.start // TILE : part.stop // TILE, :].astype(F32))
    blocks = [
        jnp.broadcast_to(lines[j : j + 1, :], (TILE, TILE)).T for j in range(lines.shape[0])
    ]
    return jnp.concatenate([jnp.concatenate(blocks, axis=0)] * (width // TILE), axis=1)


def block_kernel(row_count, groups, *refs):
    index_ref, owner_ref, degrees_ref, self_ref, neighbor_ref = refs[:5]
    features_ref, values_ref, hub_ref, cut_ref, cotangent_ref = refs[5:10]
    head_refs = refs[10 : 9 + row_count]
    piece_refs = refs[9 + row_count : 9 + row_count + groups]
    outs = refs[9 + row_count + groups : -17]
    hidden_ref, grad_ref, aggregate_ref, weights_ref, odd_ref = outs[:5]
    even_refs, back_refs = outs[5 : 5 + row_count // 2], outs[5 + row_count // 2 :]
    features, values, hub, cut, cotangent, heads, panels, arrived = refs[-17:-9]
    total, hidden, grad, aggregated, aggregate, weights, sums, back, sems = refs[-9:]
    sections = panels.shape[0] // HUB
    count, width = features_ref.shape
    size = piece_refs[0].shape[0]
    group, place = lax.axis_index("grp"), lax.axis_index("row")

    mover = Mover(sems)
    parts = split(count, CHUNK)
    steps = split(values_ref.shape[0], TILE_STEP)
    rows = [mover.get(features_ref.at[part], features.at[part]) for part in parts]
    tiles = [mover.get(values_ref.at[part], values.at[part]) for part in steps]
    first = [mover.get(ref, heads.at[k + 1]) for k, ref in enumerate(head_refs)]
    first += [
        mover.get(ref, arrived.at[aligned((group ^ k) * size, size)])
        for k, ref in enumerate(piece_refs)
    ]
    coming = []
    for part in parts:
        pairs = [(hub_ref, hub), (cut_ref, cut), (cotangent_ref, cotangent)]
        coming.append([mover.get(a.at[part], b.at[part]) for a, b in pairs])

    total[...] = jnp.zeros_like(total)
    wait(rows)
    for part, copy in zip(steps, tiles):
        copy.wait()
        for t in range(part.start, part.stop):
            row = aligned(index_ref[0, 0, t] * TILE, TILE)
            col = aligned(index_ref[0, 1, t] * TILE, TILE)
            total[row, :] += dot(values[t], features[col, :])

    wait(first)
    heads[0] = features[:HUB, :]
    for s in range(sections):
        panels[s * HUB : (s + 1) * HUB, :] = heads[owner_ref[0, s] ^ place]
    root = 0.7978845608028654
    for part, copies in zip(parts, coming):
        scale = scale_of(degrees_ref, part, width)
        wait(copies)
        summed = dot(hub[part, :], panels[...]) + dot(cut[part, :], arrived[...])
        mixed = ((summed + total[part, :]) * scale).astype(BF16)
        aggregated[part, :] = mixed
        before = dot(features[part, :], self_ref[...]) + dot(mixed, neighbor_ref[...])
        square = before * before
        bend = jnp.tanh(root * before * (1.0 + 0.044715 * square))
        half = 0.5 + 0.5 * bend
        hidden[part, :] = (before * half).astype(BF16)
        slope = half + (0.5 * root) * before * (1.0 - bend * bend) * (1.0 + (3 * 0.044715) * square)
        new = (cotangent[part, :].astype(F32) * slope).astype(BF16)
        grad[part, :] = new
        aggregate[part, :] = (dot(new, neighbor_ref[...], COLS) * scale).astype(BF16)
        mover.put(hidden.at[part], hidden_ref.at[part])
        mover.put(grad.at[part], grad_ref.at[part])
        mover.put(aggregate.at[part], aggregate_ref.at[part])
    weights[:width, :] = dot(features[...], grad[...], ROWS).astype(BF16)
    weights[width:, :] = dot(aggregated[...], grad[...], ROWS).astype(BF16)
    mover.put(weights, weights_ref)
    sums[...] = jnp.zeros_like(sums)
    returns = dot(hub[...], aggregate[...], ROWS)
    for s in range(sections):
        sums[owner_ref[0, s] ^ place] += returns[s * HUB : (s + 1) * HUB, :]
    for j in list(range(1, row_count, 2)) + list(range(0, row_count, 2)):
        heads[j] = sums[j].astype(BF16)
        mover.put(heads.at[j], odd_ref.at[j // 2] if j % 2 else even_refs[j // 2])
    back[...] = dot(cut[...], aggregate[...], ROWS).astype(BF16)
    for k, ref in enumerate(back_refs):
        mover.put(back.at[aligned((group ^ k) * size, size)], ref)
    mover.drain()


def block(index, owners, degrees, self_weight, neighbor_weight, features, values, hub, cut, cotangent, heads, pieces):
    count, width = features.shape
    tiles = values.shape[0]
    row_count, groups = len(heads) + 1, len(pieces)
    half = row_count // 2
    piece = cut.shape[1] // groups
    flops = 2 * count * width * (2 * hub.shape[1] + 2 * cut.shape[1] + 5 * width)
    near = pltpu.VMEM((count, width), BF16)

    def kernel(*refs):
        block_kernel(row_count, groups, *refs)

    out = call(
        kernel,
        "block",
        (
            index, owners, degrees, self_weight, neighbor_weight,
            features, values, hub, cut, cotangent, *heads, *pieces,
        ),
        [((count, width), BF16)] * 3
        + [((2 * width, width), BF16), ((half, HUB, width), BF16)]
        + [((HUB, width), BF16)] * half
        + [((piece, width), BF16)] * groups,
        [SCALARS, SCALARS, NEAR, NEAR, NEAR] + [ANY] * (5 + len(heads) + groups),
        [ANY] * (5 + half + groups),
        [
            near,
            pltpu.VMEM(values.shape, BF16),
            pltpu.VMEM(hub.shape, BF16),
            pltpu.VMEM(cut.shape, BF16),
            near,
            pltpu.VMEM((row_count, HUB, width), BF16),
            pltpu.VMEM((hub.shape[1], width), BF16),
            pltpu.VMEM((cut.shape[1], width), BF16),
            pltpu.VMEM((count, width), F32),
            near,
            near,
            near,
            near,
            pltpu.VMEM((2 * width, width), BF16),
            pltpu.VMEM((row_count, HUB, width), F32),
            pltpu.VMEM((cut.shape[1], width), BF16),
            pltpu.SemaphoreType.DMA(
                (7 * count // CHUNK + tiles // TILE_STEP + 2 * row_count + 2 * groups,)
            ),
        ],
        flops + 2 * tiles * TILE * TILE * width,
        2 * hub.size + 2 * cut.size + 2 * values.size + 14 * features.size,
    )
    hidden, grad, aggregate, weights, odds = out[:5]
    return hidden, grad, aggregate, weights, odds, out[5 : 5 + half], out[5 + half :]


def local_back_kernel(groups, *refs):
    index_ref, self_ref, rows_ref, values_ref, aggregate_ref, grad_ref = refs[:6]
    piece_refs = refs[6 : 6 + groups]
    out_ref, head_ref, values, aggregate, grad, returned, total, result, sems = refs[6 + groups :]
    size = piece_refs[0].shape[0]
    picks = returned.shape[0]
    group = lax.axis_index("grp")

    mover = Mover(sems)
    parts = split(grad_ref.shape[0], CHUNK)
    first = [mover.get(grad_ref.at[part], grad.at[part]) for part in parts]
    back = [
        mover.get(ref, returned.at[aligned((group ^ k) * size, size)])
        for k, ref in enumerate(piece_refs)
    ]
    coming = [mover.get(aggregate_ref.at[part], aggregate.at[part]) for part in parts]
    steps = split(values_ref.shape[0], TILE_STEP)
    tiles = [mover.get(values_ref.at[part], values.at[part]) for part in steps]
    rows = jnp.concatenate([rows_ref[0, j : j + 1, :] for j in range(groups)], axis=1)
    wait(back)
    for part, copy in zip(parts, first):
        where = lax.broadcasted_iota(jnp.int32, (CHUNK, picks), 0) + part.start
        table = jnp.where(where == rows, 1.0, 0.0).astype(BF16)
        copy.wait()
        total[part, :] = dot(grad[part, :], self_ref[...], COLS) + dot(table, returned[...])
    wait(coming)
    for part, copy in zip(steps, tiles):
        copy.wait()
        for t in range(part.start, part.stop):
            row = aligned(index_ref[0, 0, t] * TILE, TILE)
            col = aligned(index_ref[0, 1, t] * TILE, TILE)
            total[col, :] += dot(values[t], aggregate[row, :], ROWS)
    mover.put(total.at[:HUB], head_ref)
    for part in parts:
        result[part, :] = total[part, :].astype(BF16)
        mover.put(result.at[part], out_ref.at[part])
    mover.drain()


def local_backward(index, self_weight, rows, values, aggregate, grad, pieces):
    tiles = values.shape[0]
    count, width = grad.shape
    groups = len(pieces)
    picks = groups * rows.shape[2]
    near = pltpu.VMEM((count, width), BF16)

    def kernel(*refs):
        local_back_kernel(groups, *refs)

    return call(
        kernel,
        "local_backward",
        (index, self_weight, rows, values, aggregate, grad, *pieces),
        [((count, width), BF16), ((HUB, width), F32)],
        [SCALARS, NEAR, NEAR] + [ANY] * (3 + groups),
        [ANY, ANY],
        [
            pltpu.VMEM(values.shape, BF16),
            near,
            near,
            pltpu.VMEM((picks, width), BF16),
            pltpu.VMEM((count, width), F32),
            near,
            pltpu.SemaphoreType.DMA((3 * count // CHUNK + groups + tiles // TILE_STEP + 1,)),
        ],
        2 * tiles * TILE * TILE * width + 2 * count * width * (width + picks),
        2 * values.size + 8 * grad.size,
    )


def finish_kernel(grad_ref, local_ref, weights_ref, mine_ref, side_ref, *refs):
    head_refs = refs[:-8]
    out_ref, self_ref, neighbor_ref, local, weights, sums, heads, sems = refs[-8:]
    width = weights_ref.shape[1]
    mover = Mover(sems)
    ends = [mine_ref, side_ref.at[0], *head_refs]
    first = [mover.get(local_ref, local)]
    first += [mover.get(ref, heads.at[k]) for k, ref in enumerate(ends)]
    mover.get(weights_ref, weights).wait()
    sums[...] = weights[...].astype(F32)
    mover.put(sums.at[:width], self_ref)
    mover.put(sums.at[width:], neighbor_ref)
    wait(first)
    total = local[...] + jnp.sum(heads[...].astype(F32), axis=0)
    heads[0] = total.astype(BF16)
    mover.put(heads.at[0], out_ref.at[:HUB])
    mover.drain()


def finish(grad, local, weights, mine, side, heads):
    width = grad.shape[1]
    return pl.pallas_call(
        finish_kernel,
        in_specs=[ANY] * (5 + len(heads)),
        out_specs=[ANY] * 3,
        out_shape=[
            jax.ShapeDtypeStruct(grad.shape, BF16),
            jax.ShapeDtypeStruct((width, width), F32),
            jax.ShapeDtypeStruct((width, width), F32),
        ],
        scratch_shapes=[
            pltpu.VMEM((HUB, width), F32),
            pltpu.VMEM((2 * width, width), BF16),
            pltpu.VMEM((2 * width, width), F32),
            pltpu.VMEM((len(heads) + 2, HUB, width), BF16),
            pltpu.SemaphoreType.DMA((len(heads) + 7,)),
        ],
        input_output_aliases={0: 0},
        compiler_params=pltpu.CompilerParams(vmem_limit_bytes=VMEM_LIMIT),
        cost_estimate=pl.CostEstimate(flops=weights.size, bytes_accessed=8 * weights.size, transcendentals=0),
        name="finish",
    )(grad, local, weights, mine, side, *heads)


def trade(value, axis, k):
    return lax.ppermute(value, axis, [(r, r ^ k) for r in range(lax.axis_size(axis))])


def on_device(
    features,
    cotangent,
    self_weight,
    neighbor_weight,
    tile_values,
    tile_index,
    hub_adjacency,
    hub_owner,
    send_rows,
    cut_adjacency,
    degrees,
):
    count, width = features.shape
    groups = lax.axis_size("grp")
    row_count = lax.axis_size("row")
    everyone = ("grp", "row")
    values = tile_values[0]
    index = tile_index.transpose(0, 2, 1)
    degrees = degrees.reshape(count // TILE, TILE)

    head, *pieces = pick_rows(send_rows, features)
    evens = [head] + [trade(head, "row", k) for k in range(2, row_count, 2)]
    heads = [x for even in evens for x in (even, trade(even, "row", 1))][1:]
    pieces = [pieces[0]] + [trade(pieces[k], "grp", k) for k in range(1, groups)]
    hidden, grad, aggregate, weights, odds, evens, pieces = block(
        index, hub_owner, degrees, self_weight, neighbor_weight, features, values,
        hub_adjacency, cut_adjacency, cotangent, heads, pieces,
    )
    parts = weights.reshape(groups * row_count, -1, width)
    parts = lax.all_to_all(parts, everyone, split_axis=0, concat_axis=0, tiled=True)
    odds = trade(odds, "row", 1)
    heads = [
        trade((even.astype(F32) + odds[j + 1].astype(F32)).astype(BF16), "row", 2 * j + 2)
        for j, even in enumerate(evens[1:])
    ]
    pieces = [pieces[0]] + [trade(pieces[k], "grp", k) for k in range(1, groups)]
    parts, pieces = lax.optimization_barrier((parts, pieces))
    sums = jnp.sum(parts.astype(F32), axis=0).astype(BF16)
    sums = jnp.broadcast_to(sums[None], parts.shape)
    sums = lax.all_to_all(sums, everyone, split_axis=0, concat_axis=0, tiled=True)
    grad_features, head = local_backward(
        index, self_weight, send_rows, values, aggregate, grad, pieces
    )
    grad_features, grad_self, grad_neighbor = finish(
        grad_features, head, sums.reshape(2 * width, width), evens[0], odds, heads
    )
    return hidden, grad_features, grad_self, grad_neighbor


def solution(mesh):
    nodes = P(("grp", "row"), None)
    in_specs = (
        nodes,
        nodes,
        P(),
        P(),
        P(("grp", "row"), None, None, None),
        P(("grp", "row"), None, None),
        nodes,
        P("grp", None),
        P(("grp", "row"), None, None),
        nodes,
        P(("grp", "row")),
    )
    out_specs = (nodes, nodes, P(), P())
    return jax.shard_map(
        on_device, mesh=mesh, in_specs=in_specs, out_specs=out_specs, check_vma=False
    )
```

time: 367 us -> 71.8 us (0.20)
  waiting for transfers between devices: 232 us -> 13.4 us
  matrix products: 57.5 us -> 0 us
  local copies, waits for them, and re-layouts: 45.7 us -> 2.06 us
  Pallas kernels: 0 us -> 25.5 us
  starting transfers between devices: 7.64 us -> 28.4 us
  between operations: 19.1 us -> 1 us
    psum x3 -> x0, waiting for transfers between devices: 231 us -> none  [the longest x1 114 us: on_device(): lax.psum((self_part, neighbor_part), ('grp', 'row'))]
    dot_general x23 -> x0, matrix products: 57.5 us -> none  [the longest x8 7.36 us: on_device(): jnp.dot(hub_adjacency[:, section * HUB:(section + 1) * HUB], panel, prefe...]
    pallas_call x0 -> x4, Pallas kernels: none -> 25.5 us  [the longest x3 23.4 us: call(): pl.pallas_call(kernel, in_specs=in_specs, out_specs=out_specs, out_shape=...]
    dot_general x5 -> x0, local copies, waits for them, and re-layouts: 23.6 us -> none  [the longest x1 9.21 us: on_device(): jnp.einsum('lab,lbf->laf', values, picked, preferred_element_type=jnp.flo...]
    ppermute x0 -> x17, starting transfers between devices: none -> 20.9 us  [trade(): lax.ppermute(value, axis, [(r, r ^ k) for r in range(lax.axis_size(axis))])]
    ppermute x0 -> x17, waiting for transfers between devices: none -> 9.76 us  [trade(): lax.ppermute(value, axis, [(r, r ^ k) for r in range(lax.axis_size(axis))])]
    gather x3 -> x0, local copies, waits for them, and re-layouts: 8.64 us -> none  [the longest x1 3.01 us: on_device(): outgoing = features[send_rows[0]]]
    unnamed x51 -> x36, local copies, waits for them, and re-layouts: 7 us -> 1.34 us
  transfers between devices with their start and end apart: 5 -> 19, of which waited for: 3 -> 6; matrix products, arithmetic and copies ran while one was open for 16% -> 3% of each run, Pallas kernels for 0% -> 10%
where the time goes in v4:
time: 71.8 us; the launch traced here: 71.4 us
  starting transfers between devices  28.4 us (40%)
  Pallas kernels  25.5 us (36%)
  waiting for transfers between devices  13.4 us (19%)
  local copies, waits for them, and re-layouts  2.06 us (3%)
  other arithmetic  1.1 us (2%)
  between operations  1 us (1%)
    pallas_call x3, Pallas kernels, call(): pl.pallas_call(kernel, in_specs=in_specs, out_specs=out_specs, out_shape=...  23.4 us
    ppermute x17, starting transfers between devices, trade(): lax.ppermute(value, axis, [(r, r ^ k) for r in range(lax.axis_size(axis))])  20.9 us
    ppermute x17, waiting for transfers between devices, trade(): lax.ppermute(value, axis, [(r, r ^ k) for r in range(lax.axis_size(axis))])  9.76 us
    all_to_all x1, starting transfers between devices, on_device(): lax.all_to_all(parts, everyone, split_axis=0, concat_axis=0, tiled=True)  4.69 us
    all_to_all x1, waiting for transfers between devices, on_device(): lax.all_to_all(parts, everyone, split_axis=0, concat_axis=0, tiled=True)  3.58 us
    all_to_all x1, starting transfers between devices, on_device(): lax.all_to_all(sums, everyone, split_axis=0, concat_axis=0, tiled=True)  2.77 us
    pallas_call x1, Pallas kernels, finish(): pl.pallas_call(finish_kernel, in_specs=[ANY] * (5 + len(heads)), out_spec...  2.1 us
  transfers between devices with their start and end apart: 19, of which 6 were waited for; matrix products, arithmetic and copies ran while one was open for 3% of the time, Pallas kernels for 10%

profile of v4, /device:TPU:0, one launch (start us, length us, event | category | flops | bytes accessed | tf_op | source)
XLA Modules:
  0.0 71.4 jit_solution(6147486927605544548)
XLA Ops:
  0.6 3.0 %pick_rows.1 = (bf16[128,256]{1,0:T(8,128)(2,1)}, bf16[64,256]{1,0:T(8,128)(2,1)}, bf16[64,256]{1,0:T(8,128)(2,1)}, bf16[64,256]{1,0:T(8,128)(2,1)}, bf16[64,256]{1,0:T(8,128)(2,1)}) custom-call(s32[1,4,64]{2,1,0:T(4,128)} %refs_2_.1, bf16[2048,256]{1,0:T(8,128)(2,1)} %refs_5_.1), custom_call_target="tpu_custom_call" | custom-call | flops 268435456 | bytes 1048576 | tf_op jit(solution)/shard_map/pick_rows/pallas_call | solution.py:23
  3.7 5.1 %collective-permute-start.5 = (bf16[128,256]{1,0:T(8,128)(2,1)}, bf16[128,256]{1,0:T(8,128)(2,1)S(1)}, u32[]{:S(2)}, u32[]{:S(2)}) collective-permute-start(bf16[128,256]{1,0:T(8,128)(2,1)} %get-tuple-element.32), channel_id=1, source_target_pairs={{0,6},{1,7},{2,4},{3,5},{4,2},{5,3},{6,0},{7,1},{8,14},{9,15},{10,... | collective-permute-start | bytes 196616 | tf_op jit(solution)/shard_map/ppermute | solution.py:368
  8.8 0.0 collective-permute-start.3
  8.8 0.6 collective-permute-start.1
  9.4 1.6 %collective-permute-start = (bf16[128,256]{1,0:T(8,128)(2,1)}, bf16[128,256]{1,0:T(8,128)(2,1)S(1)}, u32[]{:S(2)}, u32[]{:S(2)}) collective-permute-start(bf16[128,256]{1,0:T(8,128)(2,1)} %get-tuple-element.32), channel_id=1, source_target_pairs={{0,1},{1,0},{2,3},{3,2},{4,5},{5,4},{6,7},{7,6},{8,9},{9,8},{10,11... | collective-permute-start | bytes 196616 | tf_op jit(solution)/shard_map/ppermute | solution.py:368
  11.1 0.0 collective-permute-done.7.refs_18_
  11.1 1.5 %collective-permute-start.8 = (bf16[64,256]{1,0:T(8,128)(2,1)}, bf16[64,256]{1,0:T(8,128)(2,1)S(1)}, u32[]{:S(2)}, u32[]{:S(2)}) collective-permute-start(bf16[64,256]{1,0:T(8,128)(2,1)} %get-tuple-element.35), channel_id=1, source_target_pairs={{0,16},{8,24},{16,0},{24,8},{1,17},{9,25},{17,1},{25,9},{2,18},{10... | collective-permute-start | bytes 98312 | tf_op jit(solution)/shard_map/ppermute | solution.py:368
  12.6 0.0 collective-permute-done.5.refs_15_
  12.6 1.4 %collective-permute-start.6 = (bf16[128,256]{1,0:T(8,128)(2,1)S(1)}, bf16[128,256]{1,0:T(8,128)(2,1)S(1)}, u32[]{:S(2)}, u32[]{:S(2)}) collective-permute-start(bf16[128,256]{1,0:T(8,128)(2,1)S(1)} %collective-permute-done.5.refs_15_), channel_id=1, source_target_pairs={{0,1},{1,0},{2,3},{3,2},{4,5},{5,4},{6,7},{7,6},{8,9},{9,8},{10,11... | collective-permute-start | bytes 196616 | tf_op jit(solution)/shard_map/ppermute | solution.py:368
  14.0 0.6 collective-permute-done.3.refs_13_
  14.6 1.5 %collective-permute-start.4 = (bf16[128,256]{1,0:T(8,128)(2,1)S(1)}, bf16[128,256]{1,0:T(8,128)(2,1)S(1)}, u32[]{:S(2)}, u32[]{:S(2)}) collective-permute-start(bf16[128,256]{1,0:T(8,128)(2,1)S(1)} %collective-permute-done.3.refs_13_), channel_id=1, source_target_pairs={{0,1},{1,0},{2,3},{3,2},{4,5},{5,4},{6,7},{7,6},{8,9},{9,8},{10,11... | collective-permute-start | bytes 196616 | tf_op jit(solution)/shard_map/ppermute | solution.py:368
  16.1 0.5 collective-permute-start.2
  16.6 0.0 collective-permute-done.8.refs_19_
  16.6 0.4 collective-permute-start.9
  17.1 3.4 %collective-permute-done.9.refs_20_ = bf16[64,256]{1,0:T(8,128)(2,1)S(1)} collective-permute-done((bf16[64,256]{1,0:T(8,128)(2,1)}, bf16[64,256]{1,0:T(8,128)(2,1)S(1)}, u32[]{:S(2)}, u32[]{:S(2)}) %collective-permute-start.9) | collective-permute-done | bytes 32800 | tf_op jit(solution)/shard_map/ppermute | solution.py:368
  20.5 0.0 collective-permute-done.refs_10_
  20.5 0.0 collective-permute-done.6.refs_16_
  20.5 0.0 collective-permute-done.4.refs_14_
  20.5 0.0 collective-permute-done.2.refs_12_
  20.6 0.5 copy-done.17
  21.1 0.0 copy-done.11
  21.1 0.0 copy-done.12
  21.1 0.0 copy-done.13
  21.2 0.0 copy-done.14
  21.2 13.5 %block.1 = (bf16[2048,256]{1,0:T(8,128)(2,1)}, bf16[2048,256]{1,0:T(8,128)(2,1)}, bf16[2048,256]{1,0:T(8,128)(2,1)}, bf16[512,256]{1,0:T(8,128)(2,1)}, bf16[4,12...) custom-call(s32[1,2,64]{2,1,0:T(2,128)} %bitcast.24, ...), custom_call_target="tpu_custom_call" | custom-call | flops 4563402752 | bytes 14680064 | tf_op jit(solution)/shard_map/block/pallas_call | solution.py:23
  34.7 4.7 %all-to-all-start = ((bf16[32,16,256]{2,1,0:T(8,128)(2,1)}), bf16[32,16,256]{2,1,0:T(8,128)(2,1)S(1)}, u32[]{:S(2)}, u32[]{:S(2)}) async-start(bf16[32,16,256]{2,1,0:T(8,128)(2,1)} %bitcast.23), calls=%async_computation | async-start | bytes 524288 | tf_op jit(solution)/shard_map/all_to_all | solution.py:401
  39.4 1.8 %collective-permute-start.13 = (bf16[4,128,256]{2,1,0:T(8,128)(2,1)}, bf16[4,128,256]{2,1,0:T(8,128)(2,1)S(1)}, u32[]{:S(2)}, u32[]{:S(2)}) collective-permute-start(bf16[4,128,256]{2,1,0:T(8,128)(2,1)} %get-tuple-element.53), channel_id=1, source_target_pairs={{0,1},{1,0},{2,3},{3,2},{4,5},{5,4},{6,7},{7,6},{8,9},{9,8},{10,11... | collective-permute-start | bytes 786440 | tf_op jit(solution)/shard_map/ppermute | solution.py:368
  41.2 1.5 %collective-permute-start.11 = (bf16[64,256]{1,0:T(8,128)(2,1)}, bf16[64,256]{1,0:T(8,128)(2,1)S(1)}, u32[]{:S(2)}, u32[]{:S(2)}) collective-permute-start(bf16[64,256]{1,0:T(8,128)(2,1)} %get-tuple-element.43), channel_id=1, source_target_pairs={{0,16},{8,24},{16,0},{24,8},{1,17},{9,25},{17,1},{25,9},{2,18},{10... | collective-permute-start | bytes 98312 | tf_op jit(solution)/shard_map/ppermute | solution.py:368
  42.7 0.4 collective-permute-start.12
  43.1 0.0 collective-permute-done.10.refs_7_
  43.1 2.5 %collective-permute-done.11.refs_8_ = bf16[64,256]{1,0:T(8,128)(2,1)S(1)} collective-permute-done((bf16[64,256]{1,0:T(8,128)(2,1)}, bf16[64,256]{1,0:T(8,128)(2,1)S(1)}, u32[]{:S(2)}, u32[]{:S(2)}) %collective-permute-start.11) | collective-permute-done | bytes 32800 | tf_op jit(solution)/shard_map/ppermute | solution.py:368
  45.6 0.9 %collective-permute-done.12.refs_9_ = bf16[64,256]{1,0:T(8,128)(2,1)S(1)} collective-permute-done((bf16[64,256]{1,0:T(8,128)(2,1)}, bf16[64,256]{1,0:T(8,128)(2,1)S(1)}, u32[]{:S(2)}, u32[]{:S(2)}) %collective-permute-start.12) | collective-permute-done | bytes 32800 | tf_op jit(solution)/shard_map/ppermute | solution.py:368
  46.5 3.6 %all-to-all-done = bf16[32,16,256]{2,1,0:T(8,128)(2,1)S(1)} async-done(((bf16[32,16,256]{2,1,0:T(8,128)(2,1)}), bf16[32,16,256]{2,1,0:T(8,128)(2,1)S(1)}, u32[]{:S(2)}, u32[]{:S(2)}) %all-to-all-start) | async-done | bytes 262176 | tf_op jit(solution)/shard_map/all_to_all | solution.py:401
  50.1 0.1 reduce_sum.12
  50.1 0.7 %broadcast_in_dim.2 = bf16[32,16,256]{2,1,0:T(8,128)(2,1)} broadcast(bf16[16,256]{1,0:T(8,128)(2,1)S(1)} %reduce_sum.12), dimensions={1,2} | broadcast | bytes 270336 | tf_op jit(solution)/shard_map/broadcast_in_dim | solution.py:410
  50.8 2.8 %all-to-all-start.1 = ((bf16[32,16,256]{2,1,0:T(8,128)(2,1)}), bf16[32,16,256]{2,1,0:T(8,128)(2,1)S(1)}, u32[]{:S(2)}, u32[]{:S(2)}) async-start(bf16[32,16,256]{2,1,0:T(8,128)(2,1)} %broadcast_in_dim.2), calls=%async_computation.1 | async-start | bytes 524288 | tf_op jit(solution)/shard_map/all_to_all | solution.py:411
  53.6 1.0 %fusion = (bf16[128,256]{1,0:T(8,128)(2,1)S(1)}, bf16[128,256]{1,0:T(8,128)(2,1)S(1)}, bf16[128,256]{1,0:T(8,128)(2,1)S(1)}) fusion(bf16[128,256]{1,0:T(8,128)(2,1)} %get-tuple-element.56, bf16[4,128,256]{2,1,0:T(8,128)(2,1)S(1)} %collective-permute-done.13.side_ref, bf16[128,256]{1,0:T(8,128)(2,1)} %get-tuple-element.55, bf16[128,256]{1,0:T(8,128)(2,1)} %get-tuple-element.54), kind=kLoop, calls=%fused_computation.1 | loop fusion | flops 393216 | bytes 589824 | tf_op jit(solution)/shard_map/convert_element_type | solution.py:404
  54.7 3.5 %collective-permute-start.16 = (bf16[128,256]{1,0:T(8,128)(2,1)S(1)}, bf16[128,256]{1,0:T(8,128)(2,1)S(1)}, u32[]{:S(2)}, u32[]{:S(2)}) collective-permute-start(bf16[128,256]{1,0:T(8,128)(2,1)S(1)} %get-tuple-element.60), channel_id=1, source_target_pairs={{0,6},{1,7},{2,4},{3,5},{4,2},{5,3},{6,0},{7,1},{8,14},{9,15},{10,... | collective-permute-start | bytes 196616 | tf_op jit(solution)/shard_map/ppermute | solution.py:368
  58.2 0.9 %collective-permute-start.14 = (bf16[128,256]{1,0:T(8,128)(2,1)S(1)}, bf16[128,256]{1,0:T(8,128)(2,1)S(1)}, u32[]{:S(2)}, u32[]{:S(2)}) collective-permute-start(bf16[128,256]{1,0:T(8,128)(2,1)S(1)} %get-tuple-element.62), channel_id=1, source_target_pairs={{0,2},{1,3},{2,0},{3,1},{4,6},{5,7},{6,4},{7,5},{8,10},{9,11},{10,... | collective-permute-start | bytes 196616 | tf_op jit(solution)/shard_map/ppermute | solution.py:368
  59.1 6.9 %local_backward.1 = (bf16[2048,256]{1,0:T(8,128)(2,1)}, f32[128,256]{1,0:T(8,128)}) custom-call(s32[1,2,64]{2,1,0:T(2,128)} %bitcast.25, bf16[256,256]{1,0:T(8,128)(2,1)} %refs_1_.3, s32[1,4,64]{2,1,0:T(4,128)} %refs_2_.1, bf16[64,128,128]{2,1,0:T(8,128)(2,1)} %bitcast.21, bf16[2048,256]{1,0:T(8,128)(2,1)} %get-tuple-element.38.refs_4_, ...), custom_call_target="tpu_custom_call" | custom-call | flops 1073741824 | bytes 6291456 | tf_op jit(solution)/shard_map/local_backward/pallas_call | solution.py:23
  66.0 0.0 collective-permute-done.16.refs_2_
  66.0 2.4 %collective-permute-done.15.refs_1_ = bf16[128,256]{1,0:T(8,128)(2,1)S(1)} collective-permute-done((bf16[128,256]{1,0:T(8,128)(2,1)S(1)}, bf16[128,256]{1,0:T(8,128)(2,1)S(1)}, u32[]{:S(2)}, u32[]{:S(2)}) %collective-permute-start.15) | collective-permute-done | bytes 65568 | tf_op jit(solution)/shard_map/ppermute | solution.py:368
  68.4 0.0 collective-permute-done.14.refs_0_
  68.4 0.0 all-to-all-done.1
  68.5 0.6 copy-done.3
  69.0 0.0 copy-done.4
  69.1 0.1 copy-done
  69.2 2.1 %finish.1 = (bf16[2048,256]{1,0:T(8,128)(2,1)}, f32[256,256]{1,0:T(8,128)}, f32[256,256]{1,0:T(8,128)}) custom-call(bf16[2048,256]{1,0:T(8,128)(2,1)} %get-tuple-element.49.grad_ref, f32[128,256]{1,0:T(8,128)} %get-tuple-element.50.local_ref, bf16[512,256]{1,0:T(8,128)(2,1)} %bitcast.22, ...), custom_call_target="tpu_custom_call", output_to_operand_aliasing={{0}: (0, {})} | custom-call | flops 131072 | bytes 1048576 | tf_op jit(solution)/shard_map/finish/pallas_call | solution.py:344
  (33 shorter events, 0.1 us)
Async XLA Ops:
  3.7 8.9 %collective-permute-start.5 = (bf16[128,256]{1,0:T(8,128)(2,1)}, bf16[128,256]{1,0:T(8,128)(2,1)S(1)}, u32[]{:S(2)}, u32[]{:S(2)}) collective-permute-start(bf16[128,256]{1,0:T(8,128)(2,1)} %get-tuple-element.32), channel_id=1, source_target_pairs={{0,6},{1,7},{2,4},{3,5},{4,2},{5,3},{6,0},{7,1},{8,14},{9,15},{10,... | collective-permute-start | bytes 196616 | tf_op jit(solution)/shard_map/ppermute | solution.py:368
  8.8 5.8 %collective-permute-start.3 = (bf16[128,256]{1,0:T(8,128)(2,1)}, bf16[128,256]{1,0:T(8,128)(2,1)S(1)}, u32[]{:S(2)}, u32[]{:S(2)}) collective-permute-start(bf16[128,256]{1,0:T(8,128)(2,1)} %get-tuple-element.32), channel_id=1, source_target_pairs={{0,4},{1,5},{2,6},{3,7},{4,0},{5,1},{6,2},{7,3},{8,12},{9,13},{10,... | collective-permute-start | bytes 196616 | tf_op jit(solution)/shard_map/ppermute | solution.py:368
  8.8 7.3 %collective-permute-start.1 = (bf16[128,256]{1,0:T(8,128)(2,1)}, bf16[128,256]{1,0:T(8,128)(2,1)S(1)}, u32[]{:S(2)}, u32[]{:S(2)}) collective-permute-start(bf16[128,256]{1,0:T(8,128)(2,1)} %get-tuple-element.32), channel_id=1, source_target_pairs={{0,2},{1,3},{2,0},{3,1},{4,6},{5,7},{6,4},{7,5},{8,10},{9,11},{10,... | collective-permute-start | bytes 196616 | tf_op jit(solution)/shard_map/ppermute | solution.py:368
  9.4 1.6 %collective-permute-start.7 = (bf16[64,256]{1,0:T(8,128)(2,1)}, bf16[64,256]{1,0:T(8,128)(2,1)S(1)}, u32[]{:S(2)}, u32[]{:S(2)}) collective-permute-start(bf16[64,256]{1,0:T(8,128)(2,1)} %get-tuple-element.34), channel_id=1, source_target_pairs={{0,8},{8,0},{16,24},{24,16},{1,9},{9,1},{17,25},{25,17},{2,10},{10... | collective-permute-start | bytes 98312 | tf_op jit(solution)/shard_map/ppermute | solution.py:368
  9.4 11.0 %collective-permute-start = (bf16[128,256]{1,0:T(8,128)(2,1)}, bf16[128,256]{1,0:T(8,128)(2,1)S(1)}, u32[]{:S(2)}, u32[]{:S(2)}) collective-permute-start(bf16[128,256]{1,0:T(8,128)(2,1)} %get-tuple-element.32), channel_id=1, source_target_pairs={{0,1},{1,0},{2,3},{3,2},{4,5},{5,4},{6,7},{7,6},{8,9},{9,8},{10,11... | collective-permute-start | bytes 196616 | tf_op jit(solution)/shard_map/ppermute | solution.py:368
  11.1 9.5 %copy-start.15 = (bf16[64,256]{1,0:T(8,128)(2,1)}, bf16[64,256]{1,0:T(8,128)(2,1)S(1)}, u32[]{:S(2)}) copy-start(bf16[64,256]{1,0:T(8,128)(2,1)S(1)} %collective-permute-done.7.refs_18_) | copy-start | bytes 98308
  11.1 5.6 %collective-permute-start.8 = (bf16[64,256]{1,0:T(8,128)(2,1)}, bf16[64,256]{1,0:T(8,128)(2,1)S(1)}, u32[]{:S(2)}, u32[]{:S(2)}) collective-permute-start(bf16[64,256]{1,0:T(8,128)(2,1)} %get-tuple-element.35), channel_id=1, source_target_pairs={{0,16},{8,24},{16,0},{24,8},{1,17},{9,25},{17,1},{25,9},{2,18},{10... | collective-permute-start | bytes 98312 | tf_op jit(solution)/shard_map/ppermute | solution.py:368
  12.6 7.9 %copy-start.8 = (bf16[128,256]{1,0:T(8,128)(2,1)}, bf16[128,256]{1,0:T(8,128)(2,1)S(1)}, u32[]{:S(2)}) copy-start(bf16[128,256]{1,0:T(8,128)(2,1)S(1)} %collective-permute-done.5.refs_15_) | copy-start | bytes 196612
  12.6 7.9 %collective-permute-start.6 = (bf16[128,256]{1,0:T(8,128)(2,1)S(1)}, bf16[128,256]{1,0:T(8,128)(2,1)S(1)}, u32[]{:S(2)}, u32[]{:S(2)}) collective-permute-start(bf16[128,256]{1,0:T(8,128)(2,1)S(1)} %collective-permute-done.5.refs_15_), channel_id=1, source_target_pairs={{0,1},{1,0},{2,3},{3,2},{4,5},{5,4},{6,7},{7,6},{8,9},{9,8},{10,11... | collective-permute-start | bytes 196616 | tf_op jit(solution)/shard_map/ppermute | solution.py:368
  14.6 6.0 %copy-start.9 = (bf16[128,256]{1,0:T(8,128)(2,1)}, bf16[128,256]{1,0:T(8,128)(2,1)S(1)}, u32[]{:S(2)}) copy-start(bf16[128,256]{1,0:T(8,128)(2,1)S(1)} %collective-permute-done.3.refs_13_) | copy-start | bytes 196612
  14.6 5.9 %collective-permute-start.4 = (bf16[128,256]{1,0:T(8,128)(2,1)S(1)}, bf16[128,256]{1,0:T(8,128)(2,1)S(1)}, u32[]{:S(2)}, u32[]{:S(2)}) collective-permute-start(bf16[128,256]{1,0:T(8,128)(2,1)S(1)} %collective-permute-done.3.refs_13_), channel_id=1, source_target_pairs={{0,1},{1,0},{2,3},{3,2},{4,5},{5,4},{6,7},{7,6},{8,9},{9,8},{10,11... | collective-permute-start | bytes 196616 | tf_op jit(solution)/shard_map/ppermute | solution.py:368
  16.1 4.5 %copy-start.10 = (bf16[128,256]{1,0:T(8,128)(2,1)}, bf16[128,256]{1,0:T(8,128)(2,1)S(1)}, u32[]{:S(2)}) copy-start(bf16[128,256]{1,0:T(8,128)(2,1)S(1)} %collective-permute-done.1.refs_11_) | copy-start | bytes 196612
  16.1 4.4 %collective-permute-start.2 = (bf16[128,256]{1,0:T(8,128)(2,1)S(1)}, bf16[128,256]{1,0:T(8,128)(2,1)S(1)}, u32[]{:S(2)}, u32[]{:S(2)}) collective-permute-start(bf16[128,256]{1,0:T(8,128)(2,1)S(1)} %collective-permute-done.1.refs_11_), channel_id=1, source_target_pairs={{0,1},{1,0},{2,3},{3,2},{4,5},{5,4},{6,7},{7,6},{8,9},{9,8},{10,11... | collective-permute-start | bytes 196616 | tf_op jit(solution)/shard_map/ppermute | solution.py:368
  16.6 3.9 %copy-start.16 = (bf16[64,256]{1,0:T(8,128)(2,1)}, bf16[64,256]{1,0:T(8,128)(2,1)S(1)}, u32[]{:S(2)}) copy-start(bf16[64,256]{1,0:T(8,128)(2,1)S(1)} %collective-permute-done.8.refs_19_) | copy-start | bytes 98308
  16.6 3.8 %collective-permute-start.9 = (bf16[64,256]{1,0:T(8,128)(2,1)}, bf16[64,256]{1,0:T(8,128)(2,1)S(1)}, u32[]{:S(2)}, u32[]{:S(2)}) collective-permute-start(bf16[64,256]{1,0:T(8,128)(2,1)} %get-tuple-element.36), channel_id=1, source_target_pairs={{0,24},{8,16},{16,8},{24,0},{1,25},{9,17},{17,9},{25,1},{2,26},{10... | collective-permute-start | bytes 98312 | tf_op jit(solution)/shard_map/ppermute | solution.py:368
  20.5 0.6 copy-start.17
  20.5 0.6 copy-start.11
  20.5 0.6 copy-start.12
  20.5 0.6 copy-start.13
  20.5 0.6 copy-start.14
  34.7 15.3 %all-to-all-start = ((bf16[32,16,256]{2,1,0:T(8,128)(2,1)}), bf16[32,16,256]{2,1,0:T(8,128)(2,1)S(1)}, u32[]{:S(2)}, u32[]{:S(2)}) async-start(bf16[32,16,256]{2,1,0:T(8,128)(2,1)} %bitcast.23), calls=%async_computation | async-start | bytes 524288 | tf_op jit(solution)/shard_map/all_to_all | solution.py:401
  39.4 14.2 %collective-permute-start.13 = (bf16[4,128,256]{2,1,0:T(8,128)(2,1)}, bf16[4,128,256]{2,1,0:T(8,128)(2,1)S(1)}, u32[]{:S(2)}, u32[]{:S(2)}) collective-permute-start(bf16[4,128,256]{2,1,0:T(8,128)(2,1)} %get-tuple-element.53), channel_id=1, source_target_pairs={{0,1},{1,0},{2,3},{3,2},{4,5},{5,4},{6,7},{7,6},{8,9},{9,8},{10,11... | collective-permute-start | bytes 786440 | tf_op jit(solution)/shard_map/ppermute | solution.py:368
  41.2 1.9 %collective-permute-start.10 = (bf16[64,256]{1,0:T(8,128)(2,1)}, bf16[64,256]{1,0:T(8,128)(2,1)S(1)}, u32[]{:S(2)}, u32[]{:S(2)}) collective-permute-start(bf16[64,256]{1,0:T(8,128)(2,1)} %get-tuple-element.42), channel_id=1, source_target_pairs={{0,8},{8,0},{16,24},{24,16},{1,9},{9,1},{17,25},{25,17},{2,10},{10... | collective-permute-start | bytes 98312 | tf_op jit(solution)/shard_map/ppermute | solution.py:368
  41.2 4.3 %collective-permute-start.11 = (bf16[64,256]{1,0:T(8,128)(2,1)}, bf16[64,256]{1,0:T(8,128)(2,1)S(1)}, u32[]{:S(2)}, u32[]{:S(2)}) collective-permute-start(bf16[64,256]{1,0:T(8,128)(2,1)} %get-tuple-element.43), channel_id=1, source_target_pairs={{0,16},{8,24},{16,0},{24,8},{1,17},{9,25},{17,1},{25,9},{2,18},{10... | collective-permute-start | bytes 98312 | tf_op jit(solution)/shard_map/ppermute | solution.py:368
  42.7 3.8 %collective-permute-start.12 = (bf16[64,256]{1,0:T(8,128)(2,1)}, bf16[64,256]{1,0:T(8,128)(2,1)S(1)}, u32[]{:S(2)}, u32[]{:S(2)}) collective-permute-start(bf16[64,256]{1,0:T(8,128)(2,1)} %get-tuple-element.44), channel_id=1, source_target_pairs={{0,24},{8,16},{16,8},{24,0},{1,25},{9,17},{17,9},{25,1},{2,26},{10... | collective-permute-start | bytes 98312 | tf_op jit(solution)/shard_map/ppermute | solution.py:368
  43.1 16.0 %copy-start.5 = (bf16[64,256]{1,0:T(8,128)(2,1)}, bf16[64,256]{1,0:T(8,128)(2,1)S(1)}, u32[]{:S(2)}) copy-start(bf16[64,256]{1,0:T(8,128)(2,1)S(1)} %collective-permute-done.10.refs_7_) | copy-start | bytes 98308
  45.6 13.6 %copy-start.6 = (bf16[64,256]{1,0:T(8,128)(2,1)}, bf16[64,256]{1,0:T(8,128)(2,1)S(1)}, u32[]{:S(2)}) copy-start(bf16[64,256]{1,0:T(8,128)(2,1)S(1)} %collective-permute-done.11.refs_8_) | copy-start | bytes 98308
  46.5 12.7 %copy-start.7 = (bf16[64,256]{1,0:T(8,128)(2,1)}, bf16[64,256]{1,0:T(8,128)(2,1)S(1)}, u32[]{:S(2)}) copy-start(bf16[64,256]{1,0:T(8,128)(2,1)S(1)} %collective-permute-done.12.refs_9_) | copy-start | bytes 98308
  50.8 17.6 %all-to-all-start.1 = ((bf16[32,16,256]{2,1,0:T(8,128)(2,1)}), bf16[32,16,256]{2,1,0:T(8,128)(2,1)S(1)}, u32[]{:S(2)}, u32[]{:S(2)}) async-start(bf16[32,16,256]{2,1,0:T(8,128)(2,1)} %broadcast_in_dim.2), calls=%async_computation.1 | async-start | bytes 524288 | tf_op jit(solution)/shard_map/all_to_all | solution.py:411
  53.6 14.8 %copy-start.1 = (bf16[4,128,256]{2,1,0:T(8,128)(2,1)}, bf16[4,128,256]{2,1,0:T(8,128)(2,1)S(1)}, u32[]{:S(2)}) copy-start(bf16[4,128,256]{2,1,0:T(8,128)(2,1)S(1)} %collective-permute-done.13.side_ref) | copy-start | bytes 786436
  54.7 11.3 %collective-permute-start.16 = (bf16[128,256]{1,0:T(8,128)(2,1)S(1)}, bf16[128,256]{1,0:T(8,128)(2,1)S(1)}, u32[]{:S(2)}, u32[]{:S(2)}) collective-permute-start(bf16[128,256]{1,0:T(8,128)(2,1)S(1)} %get-tuple-element.60), channel_id=1, source_target_pairs={{0,6},{1,7},{2,4},{3,5},{4,2},{5,3},{6,0},{7,1},{8,14},{9,15},{10,... | collective-permute-start | bytes 196616 | tf_op jit(solution)/shard_map/ppermute | solution.py:368
  58.2 10.2 %collective-permute-start.15 = (bf16[128,256]{1,0:T(8,128)(2,1)S(1)}, bf16[128,256]{1,0:T(8,128)(2,1)S(1)}, u32[]{:S(2)}, u32[]{:S(2)}) collective-permute-start(bf16[128,256]{1,0:T(8,128)(2,1)S(1)} %get-tuple-element.61), channel_id=1, source_target_pairs={{0,4},{1,5},{2,6},{3,7},{4,0},{5,1},{6,2},{7,3},{8,12},{9,13},{10,... | collective-permute-start | bytes 196616 | tf_op jit(solution)/shard_map/ppermute | solution.py:368
  58.2 10.2 %collective-permute-start.14 = (bf16[128,256]{1,0:T(8,128)(2,1)S(1)}, bf16[128,256]{1,0:T(8,128)(2,1)S(1)}, u32[]{:S(2)}, u32[]{:S(2)}) collective-permute-start(bf16[128,256]{1,0:T(8,128)(2,1)S(1)} %get-tuple-element.62), channel_id=1, source_target_pairs={{0,2},{1,3},{2,0},{3,1},{4,6},{5,7},{6,4},{7,5},{8,10},{9,11},{10,... | collective-permute-start | bytes 196616 | tf_op jit(solution)/shard_map/ppermute | solution.py:368
  66.0 2.4 %copy-start.2 = (bf16[128,256]{1,0:T(8,128)(2,1)}, bf16[128,256]{1,0:T(8,128)(2,1)S(1)}, u32[]{:S(2)}) copy-start(bf16[128,256]{1,0:T(8,128)(2,1)S(1)} %collective-permute-done.16.refs_2_) | copy-start | bytes 196612
  68.4 0.6 copy-start.3
  68.4 0.6 copy-start.4
  68.4 0.7 %copy-start = (bf16[32,16,256]{2,1,0:T(8,128)(2,1)}, bf16[32,16,256]{2,1,0:T(8,128)(2,1)S(1)}, u32[]{:S(2)}) copy-start(bf16[32,16,256]{2,1,0:T(8,128)(2,1)S(1)} %all-to-all-done.1) | copy-start | bytes 786436

commit v5 on v4

--- a/solution.py
+++ b/solution.py
@@ -7,8 +7,8 @@
 
 TILE = 128
 HUB = 128
-CHUNK = 512
-TILE_STEP = 16
+CHUNK = 1024
+TILE_STEP = 32
 VMEM_LIMIT = 62 * 2**20
 ROWS = (((0,), (0,)), ((), ()))
 COLS = (((1,), (1,)), ((), ()))
@@ -86,7 +86,9 @@
     wait(coming)
     mover.put(features.at[:HUB], head_ref)
     picked[...] = dot(table, features[...]).astype(BF16)
-    for k, ref in enumerate(out_refs):
+    odd_ref, even_refs = out_refs[0], out_refs[1:]
+    for k in range(groups):
+        ref = odd_ref.at[k // 2] if k % 2 else even_refs[k // 2]
         mover.put(picked.at[aligned((group ^ k) * cut, cut)], ref)
     mover.drain()
 
@@ -98,9 +100,10 @@
         pick_kernel,
         "pick_rows",
         (rows, features),
-        [((HUB, width), BF16)] + [((cut, width), BF16)] * groups,
+        [((HUB, width), BF16), ((groups // 2, cut, width), BF16)]
+        + [((cut, width), BF16)] * (groups // 2),
         [NEAR, ANY],
-        [ANY] * (1 + groups),
+        [ANY] * (2 + groups // 2),
         [
             pltpu.VMEM((count, width), BF16),
             pltpu.VMEM((groups * cut, width), BF16),
@@ -124,30 +127,36 @@
     features_ref, values_ref, hub_ref, cut_ref, cotangent_ref = refs[5:10]
     head_refs = refs[10 : 9 + row_count]
     piece_refs = refs[9 + row_count : 9 + row_count + groups]
-    outs = refs[9 + row_count + groups : -17]
+    outs = refs[9 + row_count + groups : -15]
     hidden_ref, grad_ref, aggregate_ref, weights_ref, odd_ref = outs[:5]
     even_refs, back_refs = outs[5 : 5 + row_count // 2], outs[5 + row_count // 2 :]
-    features, values, hub, cut, cotangent, heads, panels, arrived = refs[-17:-9]
-    total, hidden, grad, aggregated, aggregate, weights, sums, back, sems = refs[-9:]
-    sections = panels.shape[0] // HUB
+    pair, stack, values, edges, cotangent, heads, panels = refs[-15:-8]
+    total, hidden, grad, aggregate, weights, sums, back, sems = refs[-8:]
     count, width = features_ref.shape
+    depth = hub_ref.shape[1]
+    sections = depth // HUB
     size = piece_refs[0].shape[0]
     group, place = lax.axis_index("grp"), lax.axis_index("row")
 
     mover = Mover(sems)
     parts = split(count, CHUNK)
     steps = split(values_ref.shape[0], TILE_STEP)
-    rows = [mover.get(features_ref.at[part], features.at[part]) for part in parts]
+    rows = [mover.get(features_ref, pair.at[:, :width])]
     tiles = [mover.get(values_ref.at[part], values.at[part]) for part in steps]
     first = [mover.get(ref, heads.at[k + 1]) for k, ref in enumerate(head_refs)]
+    for k in range(groups):
+        ref = piece_refs[groups // 2 + k // 2].at[k // 2] if k % 2 else piece_refs[k // 2]
+        first.append(mover.get(ref, panels.at[aligned(depth + (group ^ k) * size, size)]))
     first += [
-        mover.get(ref, arrived.at[aligned((group ^ k) * size, size)])
-        for k, ref in enumerate(piece_refs)
+        mover.get(self_ref, stack.at[:width]), mover.get(neighbor_ref, stack.at[width:])
     ]
     coming = []
     for part in parts:
-        pairs = [(hub_ref, hub), (cut_ref, cut), (cotangent_ref, cotangent)]
-        coming.append([mover.get(a.at[part], b.at[part]) for a, b in pairs])
+        coming.append([
+            mover.get(hub_ref.at[part], edges.at[part, :depth]),
+            mover.get(cut_ref.at[part], edges.at[part, depth:]),
+            mover.get(cotangent_ref.at[part], cotangent.at[part]),
+        ])
 
     total[...] = jnp.zeros_like(total)
     wait(rows)
@@ -156,53 +165,53 @@
         for t in range(part.start, part.stop):
             row = aligned(index_ref[0, 0, t] * TILE, TILE)
             col = aligned(index_ref[0, 1, t] * TILE, TILE)
-            total[row, :] += dot(values[t], features[col, :])
+            total[row, :] += dot(values[t], pair[col, :width])
 
     wait(first)
-    heads[0] = features[:HUB, :]
+    heads[0] = pair[:HUB, :width]
     for s in range(sections):
         panels[s * HUB : (s + 1) * HUB, :] = heads[owner_ref[0, s] ^ place]
-    root = 0.7978845608028654
+    neighbor = stack[width:, :]
+    root, bend = 0.7978845608028654, 0.044715
     for part, copies in zip(parts, coming):
+        wait(copies)
         scale = scale_of(degrees_ref, part, width)
-        wait(copies)
-        summed = dot(hub[part, :], panels[...]) + dot(cut[part, :], arrived[...])
-        mixed = ((summed + total[part, :]) * scale).astype(BF16)
-        aggregated[part, :] = mixed
-        before = dot(features[part, :], self_ref[...]) + dot(mixed, neighbor_ref[...])
-        square = before * before
-        bend = jnp.tanh(root * before * (1.0 + 0.044715 * square))
-        half = 0.5 + 0.5 * bend
+        summed = total[part, :] + dot(edges[part, :], panels[...])
+        pair[part, width:] = (summed * scale).astype(BF16)
+        before = dot(pair[part, :], stack[...])
+        slope = (root * bend) * (before * before) + root
+        wave = jnp.tanh(before * slope)
+        half = 0.5 * wave + 0.5
         hidden[part, :] = (before * half).astype(BF16)
-        slope = half + (0.5 * root) * before * (1.0 - bend * bend) * (1.0 + (3 * 0.044715) * square)
-        new = (cotangent[part, :].astype(F32) * slope).astype(BF16)
+        rise = half + (before * (1.5 * slope - root)) * (1.0 - wave * wave)
+        new = (cotangent[part, :].astype(F32) * rise).astype(BF16)
         grad[part, :] = new
-        aggregate[part, :] = (dot(new, neighbor_ref[...], COLS) * scale).astype(BF16)
+        aggregate[part, :] = (dot(new, neighbor, COLS) * scale).astype(BF16)
         mover.put(hidden.at[part], hidden_ref.at[part])
         mover.put(grad.at[part], grad_ref.at[part])
         mover.put(aggregate.at[part], aggregate_ref.at[part])
-    weights[:width, :] = dot(features[...], grad[...], ROWS).astype(BF16)
-    weights[width:, :] = dot(aggregated[...], grad[...], ROWS).astype(BF16)
+    weights[...] = dot(pair[...], grad[...], ROWS).astype(BF16)
     mover.put(weights, weights_ref)
     sums[...] = jnp.zeros_like(sums)
-    returns = dot(hub[...], aggregate[...], ROWS)
+    returns = dot(edges[...], aggregate[...], ROWS)
     for s in range(sections):
         sums[owner_ref[0, s] ^ place] += returns[s * HUB : (s + 1) * HUB, :]
     for j in list(range(1, row_count, 2)) + list(range(0, row_count, 2)):
         heads[j] = sums[j].astype(BF16)
         mover.put(heads.at[j], odd_ref.at[j // 2] if j % 2 else even_refs[j // 2])
-    back[...] = dot(cut[...], aggregate[...], ROWS).astype(BF16)
+    back[...] = returns[depth:, :].astype(BF16)
     for k, ref in enumerate(back_refs):
         mover.put(back.at[aligned((group ^ k) * size, size)], ref)
     mover.drain()
 
 
-def block(index, owners, degrees, self_weight, neighbor_weight, features, values, hub, cut, cotangent, heads, pieces):
+def block(index, owners, degrees, self_weight, neighbor_weight, features, values, hub, cut, cotangent, heads, pieces, passed):
     count, width = features.shape
     tiles = values.shape[0]
-    row_count, groups = len(heads) + 1, len(pieces)
+    row_count, groups = len(heads) + 1, 2 * len(pieces)
     half = row_count // 2
     piece = cut.shape[1] // groups
+    depth = hub.shape[1] + cut.shape[1]
     flops = 2 * count * width * (2 * hub.shape[1] + 2 * cut.shape[1] + 5 * width)
     near = pltpu.VMEM((count, width), BF16)
 
@@ -214,25 +223,23 @@
         "block",
         (
             index, owners, degrees, self_weight, neighbor_weight,
-            features, values, hub, cut, cotangent, *heads, *pieces,
+            features, values, hub, cut, cotangent, *heads, *pieces, *passed,
         ),
         [((count, width), BF16)] * 3
         + [((2 * width, width), BF16), ((half, HUB, width), BF16)]
         + [((HUB, width), BF16)] * half
         + [((piece, width), BF16)] * groups,
-        [SCALARS, SCALARS, NEAR, NEAR, NEAR] + [ANY] * (5 + len(heads) + groups),
+        [SCALARS, SCALARS, NEAR] + [ANY] * (7 + len(heads) + groups),
         [ANY] * (5 + half + groups),
         [
-            near,
+            pltpu.VMEM((count, 2 * width), BF16),
+            pltpu.VMEM((2 * width, width), BF16),
             pltpu.VMEM(values.shape, BF16),
-            pltpu.VMEM(hub.shape, BF16),
-            pltpu.VMEM(cut.shape, BF16),
+            pltpu.VMEM((count, depth), BF16),
             near,
             pltpu.VMEM((row_count, HUB, width), BF16),
-            pltpu.VMEM((hub.shape[1], width), BF16),
-            pltpu.VMEM((cut.shape[1], width), BF16),
+            pltpu.VMEM((depth, width), BF16),
             pltpu.VMEM((count, width), F32),
-            near,
             near,
             near,
             near,
@@ -240,7 +247,7 @@
             pltpu.VMEM((row_count, HUB, width), F32),
             pltpu.VMEM((cut.shape[1], width), BF16),
             pltpu.SemaphoreType.DMA(
-                (7 * count // CHUNK + tiles // TILE_STEP + 2 * row_count + 2 * groups,)
+                (7 * count // CHUNK + tiles // TILE_STEP + 2 * row_count + 2 * groups + 2,)
             ),
         ],
         flops + 2 * tiles * TILE * TILE * width,
@@ -389,13 +396,15 @@
     index = tile_index.transpose(0, 2, 1)
     degrees = degrees.reshape(count // TILE, TILE)
 
-    head, *pieces = pick_rows(send_rows, features)
+    head, odds, *pieces = pick_rows(send_rows, features)
     evens = [head] + [trade(head, "row", k) for k in range(2, row_count, 2)]
+    odds, evens[-1] = lax.optimization_barrier((trade(odds, "grp", 1), evens[-1]))
     heads = [x for even in evens for x in (even, trade(even, "row", 1))][1:]
-    pieces = [pieces[0]] + [trade(pieces[k], "grp", k) for k in range(1, groups)]
+    pieces = [pieces[0]] + [trade(pieces[k], "grp", 2 * k) for k in range(1, groups // 2)]
+    passed = [odds] + [trade(odds, "grp", 2 * k) for k in range(1, groups // 2)]
     hidden, grad, aggregate, weights, odds, evens, pieces = block(
         index, hub_owner, degrees, self_weight, neighbor_weight, features, values,
-        hub_adjacency, cut_adjacency, cotangent, heads, pieces,
+        hub_adjacency, cut_adjacency, cotangent, heads, pieces, passed,
     )
     parts = weights.reshape(groups * row_count, -1, width)
     parts = lax.all_to_all(parts, everyone, split_axis=0, concat_axis=0, tiled=True)

time: 71.8 us -> 69.6 us (0.969)
  Pallas kernels: 25.5 us -> 22.6 us
    pallas_call x3, Pallas kernels: 23.4 us -> 20.5 us  [call(): pl.pallas_call(kernel, in_specs=in_specs, out_specs=out_specs, out_shape=...]
  transfers between devices with their start and end apart: 19 -> 19, of which waited for: 6 -> 8; matrix products, arithmetic and copies ran while one was open for 3% -> 3% of each run, Pallas kernels for 10% -> 9%
where the time goes in v5:
time: 69.6 us; the launch traced here: 69.1 us
  starting transfers between devices  28.5 us (41%)
  Pallas kernels  22.6 us (32%)
  waiting for transfers between devices  13.9 us (20%)
  local copies, waits for them, and re-layouts  2.04 us (3%)
  other arithmetic  1.1 us (2%)
  between operations  0.98 us (1%)
    ppermute x17, starting transfers between devices, trade(): lax.ppermute(value, axis, [(r, r ^ k) for r in range(lax.axis_size(axis))])  21.6 us
    pallas_call x3, Pallas kernels, call(): pl.pallas_call(kernel, in_specs=in_specs, out_specs=out_specs, out_shape=...  20.5 us
    ppermute x17, waiting for transfers between devices, trade(): lax.ppermute(value, axis, [(r, r ^ k) for r in range(lax.axis_size(axis))])  10.3 us
    all_to_all x1, starting transfers between devices, on_device(): lax.all_to_all(parts, everyone, split_axis=0, concat_axis=0, tiled=True)  4.13 us
    all_to_all x1, waiting for transfers between devices, on_device(): lax.all_to_all(parts, everyone, split_axis=0, concat_axis=0, tiled=True)  3.58 us
    all_to_all x1, starting transfers between devices, on_device(): lax.all_to_all(sums, everyone, split_axis=0, concat_axis=0, tiled=True)  2.77 us
    pallas_call x1, Pallas kernels, finish(): pl.pallas_call(finish_kernel, in_specs=[ANY] * (5 + len(heads)), out_spec...  2.1 us
  transfers between devices with their start and end apart: 19, of which 8 were waited for; matrix products, arithmetic and copies ran while one was open for 3% of the time, Pallas kernels for 9%

profile of v5, /device:TPU:0, one launch (start us, length us, event | category | flops | bytes accessed | tf_op | source)
XLA Modules:
  0.0 69.1 jit_solution(11273900710819141841)
XLA Ops:
  0.6 3.0 %pick_rows.1 = (bf16[128,256]{1,0:T(8,128)(2,1)}, bf16[2,64,256]{2,1,0:T(8,128)(2,1)}, bf16[64,256]{1,0:T(8,128)(2,1)}, bf16[64,256]{1,0:T(8,128)(2,1)}) custom-call(s32[1,4,64]{2,1,0:T(4,128)} %refs_2_.1, bf16[2048,256]{1,0:T(8,128)(2,1)} %refs_5_.1), custom_call_target="tpu_custom_call" | custom-call | flops 268435456 | bytes 1048576 | tf_op jit(solution)/shard_map/pick_rows/pallas_call | solution.py:23
  3.7 0.5 collective-permute-start.5
  4.2 4.7 %collective-permute-start.6 = (bf16[128,256]{1,0:T(8,128)(2,1)}, bf16[128,256]{1,0:T(8,128)(2,1)S(1)}, u32[]{:S(2)}, u32[]{:S(2)}) collective-permute-start(bf16[128,256]{1,0:T(8,128)(2,1)} %get-tuple-element.33), channel_id=1, source_target_pairs={{0,6},{1,7},{2,4},{3,5},{4,2},{5,3},{6,0},{7,1},{8,14},{9,15},{10,... | collective-permute-start | bytes 196616 | tf_op jit(solution)/shard_map/ppermute | solution.py:375
  8.9 0.0 collective-permute-start.3
  8.9 0.7 collective-permute-start.1
  9.5 1.7 %collective-permute-start.8 = (bf16[64,256]{1,0:T(8,128)(2,1)}, bf16[64,256]{1,0:T(8,128)(2,1)S(1)}, u32[]{:S(2)}, u32[]{:S(2)}) collective-permute-start(bf16[64,256]{1,0:T(8,128)(2,1)} %get-tuple-element.37), channel_id=1, source_target_pairs={{0,16},{8,24},{16,0},{24,8},{1,17},{9,25},{17,1},{25,9},{2,18},{10... | collective-permute-start | bytes 98312 | tf_op jit(solution)/shard_map/ppermute | solution.py:375
  11.2 0.0 collective-permute-done.5.refs_19_
  11.2 1.5 %collective-permute-start = (bf16[128,256]{1,0:T(8,128)(2,1)}, bf16[128,256]{1,0:T(8,128)(2,1)S(1)}, u32[]{:S(2)}, u32[]{:S(2)}) collective-permute-start(bf16[128,256]{1,0:T(8,128)(2,1)} %get-tuple-element.33), channel_id=1, source_target_pairs={{0,1},{1,0},{2,3},{3,2},{4,5},{5,4},{6,7},{7,6},{8,9},{9,8},{10,11... | collective-permute-start | bytes 196616 | tf_op jit(solution)/shard_map/ppermute | solution.py:375
  12.7 0.0 collective-permute-done.6.refs_15_
  12.7 0.8 %collective-permute-start.7 = (bf16[128,256]{1,0:T(8,128)(2,1)S(1)}, bf16[128,256]{1,0:T(8,128)(2,1)S(1)}, u32[]{:S(2)}, u32[]{:S(2)}) collective-permute-start(bf16[128,256]{1,0:T(8,128)(2,1)S(1)} %collective-permute-done.6.refs_15_), channel_id=1, source_target_pairs={{0,1},{1,0},{2,3},{3,2},{4,5},{5,4},{6,7},{7,6},{8,9},{9,8},{10,11... | collective-permute-start | bytes 196616 | tf_op jit(solution)/shard_map/ppermute | solution.py:375
  13.5 0.2 collective-permute-done.8.refs_18_
  13.7 1.7 %collective-permute-start.9 = (bf16[2,64,256]{2,1,0:T(8,128)(2,1)S(1)}, bf16[2,64,256]{2,1,0:T(8,128)(2,1)S(1)}, u32[]{:S(2)}, u32[]{:S(2)}) collective-permute-start(bf16[2,64,256]{2,1,0:T(8,128)(2,1)S(1)} %collective-permute-done.5.refs_19_), channel_id=1, source_target_pairs={{0,16},{8,24},{16,0},{24,8},{1,17},{9,25},{17,1},{25,9},{2,18},{10... | collective-permute-start | bytes 196616 | tf_op jit(solution)/shard_map/ppermute | solution.py:375
  15.3 0.0 collective-permute-done.3.refs_13_
  15.3 1.5 %collective-permute-start.4 = (bf16[128,256]{1,0:T(8,128)(2,1)S(1)}, bf16[128,256]{1,0:T(8,128)(2,1)S(1)}, u32[]{:S(2)}, u32[]{:S(2)}) collective-permute-start(bf16[128,256]{1,0:T(8,128)(2,1)S(1)} %collective-permute-done.3.refs_13_), channel_id=1, source_target_pairs={{0,1},{1,0},{2,3},{3,2},{4,5},{5,4},{6,7},{7,6},{8,9},{9,8},{10,11... | collective-permute-start | bytes 196616 | tf_op jit(solution)/shard_map/ppermute | solution.py:375
  16.8 0.0 collective-permute-done.1.refs_11_
  16.8 0.5 collective-permute-start.2
  17.3 0.0 collective-permute-done.refs_10_
  17.3 0.0 collective-permute-done.7.refs_16_
  17.4 0.6 collective-permute-done.9.refs_20_
  17.9 2.1 %collective-permute-done.4.refs_14_ = bf16[128,256]{1,0:T(8,128)(2,1)S(1)} collective-permute-done((bf16[128,256]{1,0:T(8,128)(2,1)S(1)}, bf16[128,256]{1,0:T(8,128)(2,1)S(1)}, u32[]{:S(2)}, u32[]{:S(2)}) %collective-permute-start.4) | collective-permute-done | bytes 65568 | tf_op jit(solution)/shard_map/ppermute | solution.py:375
  20.0 1.0 %collective-permute-done.2.refs_12_ = bf16[128,256]{1,0:T(8,128)(2,1)S(1)} collective-permute-done((bf16[128,256]{1,0:T(8,128)(2,1)S(1)}, bf16[128,256]{1,0:T(8,128)(2,1)S(1)}, u32[]{:S(2)}, u32[]{:S(2)}) %collective-permute-start.2) | collective-permute-done | bytes 65568 | tf_op jit(solution)/shard_map/ppermute | solution.py:375
  21.1 0.5 copy-done.16
  21.7 11.3 %block.1 = (bf16[2048,256]{1,0:T(8,128)(2,1)}, bf16[2048,256]{1,0:T(8,128)(2,1)}, bf16[2048,256]{1,0:T(8,128)(2,1)}, bf16[512,256]{1,0:T(8,128)(2,1)}, bf16[4,12...) custom-call(s32[1,2,64]{2,1,0:T(2,128)} %bitcast.24, ...), custom_call_target="tpu_custom_call" | custom-call | flops 4563402752 | bytes 14680064 | tf_op jit(solution)/shard_map/block/pallas_call | solution.py:23
  33.0 4.1 %all-to-all-start = ((bf16[32,16,256]{2,1,0:T(8,128)(2,1)}), bf16[32,16,256]{2,1,0:T(8,128)(2,1)S(1)}, u32[]{:S(2)}, u32[]{:S(2)}) async-start(bf16[32,16,256]{2,1,0:T(8,128)(2,1)} %bitcast.23), calls=%async_computation | async-start | bytes 524288 | tf_op jit(solution)/shard_map/all_to_all | solution.py:410
  37.1 1.8 %collective-permute-start.13 = (bf16[4,128,256]{2,1,0:T(8,128)(2,1)}, bf16[4,128,256]{2,1,0:T(8,128)(2,1)S(1)}, u32[]{:S(2)}, u32[]{:S(2)}) collective-permute-start(bf16[4,128,256]{2,1,0:T(8,128)(2,1)} %get-tuple-element.55), channel_id=1, source_target_pairs={{0,1},{1,0},{2,3},{3,2},{4,5},{5,4},{6,7},{7,6},{8,9},{9,8},{10,11... | collective-permute-start | bytes 786440 | tf_op jit(solution)/shard_map/ppermute | solution.py:375
  39.0 0.0 collective-permute-start.10
  39.0 1.5 %collective-permute-start.11 = (bf16[64,256]{1,0:T(8,128)(2,1)}, bf16[64,256]{1,0:T(8,128)(2,1)S(1)}, u32[]{:S(2)}, u32[]{:S(2)}) collective-permute-start(bf16[64,256]{1,0:T(8,128)(2,1)} %get-tuple-element.45), channel_id=1, source_target_pairs={{0,16},{8,24},{16,0},{24,8},{1,17},{9,25},{17,1},{25,9},{2,18},{10... | collective-permute-start | bytes 98312 | tf_op jit(solution)/shard_map/ppermute | solution.py:375
  40.4 0.4 collective-permute-start.12
  40.8 0.0 collective-permute-done.10.refs_7_
  40.8 2.5 %collective-permute-done.11.refs_8_ = bf16[64,256]{1,0:T(8,128)(2,1)S(1)} collective-permute-done((bf16[64,256]{1,0:T(8,128)(2,1)}, bf16[64,256]{1,0:T(8,128)(2,1)S(1)}, u32[]{:S(2)}, u32[]{:S(2)}) %collective-permute-start.11) | collective-permute-done | bytes 32800 | tf_op jit(solution)/shard_map/ppermute | solution.py:375
  43.3 0.9 %collective-permute-done.12.refs_9_ = bf16[64,256]{1,0:T(8,128)(2,1)S(1)} collective-permute-done((bf16[64,256]{1,0:T(8,128)(2,1)}, bf16[64,256]{1,0:T(8,128)(2,1)S(1)}, u32[]{:S(2)}, u32[]{:S(2)}) %collective-permute-start.12) | collective-permute-done | bytes 32800 | tf_op jit(solution)/shard_map/ppermute | solution.py:375
  44.2 3.6 %all-to-all-done = bf16[32,16,256]{2,1,0:T(8,128)(2,1)S(1)} async-done(((bf16[32,16,256]{2,1,0:T(8,128)(2,1)}), bf16[32,16,256]{2,1,0:T(8,128)(2,1)S(1)}, u32[]{:S(2)}, u32[]{:S(2)}) %all-to-all-start) | async-done | bytes 262176 | tf_op jit(solution)/shard_map/all_to_all | solution.py:410
  47.8 0.1 reduce_sum.12
  47.8 0.7 %broadcast_in_dim.2 = bf16[32,16,256]{2,1,0:T(8,128)(2,1)} broadcast(bf16[16,256]{1,0:T(8,128)(2,1)S(1)} %reduce_sum.12), dimensions={1,2} | broadcast | bytes 270336 | tf_op jit(solution)/shard_map/broadcast_in_dim | solution.py:419
  48.5 2.8 %all-to-all-start.1 = ((bf16[32,16,256]{2,1,0:T(8,128)(2,1)}), bf16[32,16,256]{2,1,0:T(8,128)(2,1)S(1)}, u32[]{:S(2)}, u32[]{:S(2)}) async-start(bf16[32,16,256]{2,1,0:T(8,128)(2,1)} %broadcast_in_dim.2), calls=%async_computation.1 | async-start | bytes 524288 | tf_op jit(solution)/shard_map/all_to_all | solution.py:420
  51.3 0.0 collective-permute-done.13.side_ref
  51.3 1.0 %fusion = (bf16[128,256]{1,0:T(8,128)(2,1)S(1)}, bf16[128,256]{1,0:T(8,128)(2,1)S(1)}, bf16[128,256]{1,0:T(8,128)(2,1)S(1)}) fusion(bf16[128,256]{1,0:T(8,128)(2,1)} %get-tuple-element.58, bf16[4,128,256]{2,1,0:T(8,128)(2,1)S(1)} %collective-permute-done.13.side_ref, bf16[128,256]{1,0:T(8,128)(2,1)} %get-tuple-element.57, bf16[128,256]{1,0:T(8,128)(2,1)} %get-tuple-element.56), kind=kLoop, calls=%fused_computation.1 | loop fusion | flops 393216 | bytes 589824 | tf_op jit(solution)/shard_map/convert_element_type | solution.py:413
  52.4 3.5 %collective-permute-start.16 = (bf16[128,256]{1,0:T(8,128)(2,1)S(1)}, bf16[128,256]{1,0:T(8,128)(2,1)S(1)}, u32[]{:S(2)}, u32[]{:S(2)}) collective-permute-start(bf16[128,256]{1,0:T(8,128)(2,1)S(1)} %get-tuple-element.62), channel_id=1, source_target_pairs={{0,6},{1,7},{2,4},{3,5},{4,2},{5,3},{6,0},{7,1},{8,14},{9,15},{10,... | collective-permute-start | bytes 196616 | tf_op jit(solution)/shard_map/ppermute | solution.py:375
  55.9 0.0 collective-permute-start.15
  55.9 0.9 %collective-permute-start.14 = (bf16[128,256]{1,0:T(8,128)(2,1)S(1)}, bf16[128,256]{1,0:T(8,128)(2,1)S(1)}, u32[]{:S(2)}, u32[]{:S(2)}) collective-permute-start(bf16[128,256]{1,0:T(8,128)(2,1)S(1)} %get-tuple-element.64), channel_id=1, source_target_pairs={{0,2},{1,3},{2,0},{3,1},{4,6},{5,7},{6,4},{7,5},{8,10},{9,11},{10,... | collective-permute-start | bytes 196616 | tf_op jit(solution)/shard_map/ppermute | solution.py:375
  56.9 6.2 %local_backward.1 = (bf16[2048,256]{1,0:T(8,128)(2,1)}, f32[128,256]{1,0:T(8,128)}) custom-call(s32[1,2,64]{2,1,0:T(2,128)} %bitcast.25, bf16[256,256]{1,0:T(8,128)(2,1)} %refs_1_.3, s32[1,4,64]{2,1,0:T(4,128)} %refs_2_.1, bf16[64,128,128]{2,1,0:T(8,128)(2,1)} %bitcast.21, bf16[2048,256]{1,0:T(8,128)(2,1)} %get-tuple-element.40.refs_4_, ...), custom_call_target="tpu_custom_call" | custom-call | flops 1073741824 | bytes 6291456 | tf_op jit(solution)/shard_map/local_backward/pallas_call | solution.py:23
  63.1 3.1 %collective-permute-done.15.refs_1_ = bf16[128,256]{1,0:T(8,128)(2,1)S(1)} collective-permute-done((bf16[128,256]{1,0:T(8,128)(2,1)S(1)}, bf16[128,256]{1,0:T(8,128)(2,1)S(1)}, u32[]{:S(2)}, u32[]{:S(2)}) %collective-permute-start.15) | collective-permute-done | bytes 65568 | tf_op jit(solution)/shard_map/ppermute | solution.py:375
  66.1 0.0 collective-permute-done.14.refs_0_
  66.1 0.0 all-to-all-done.1
  66.2 0.6 copy-done.3
  66.7 0.0 copy-done.4
  66.8 0.1 copy-done
  66.9 2.1 %finish.1 = (bf16[2048,256]{1,0:T(8,128)(2,1)}, f32[256,256]{1,0:T(8,128)}, f32[256,256]{1,0:T(8,128)}) custom-call(bf16[2048,256]{1,0:T(8,128)(2,1)} %get-tuple-element.51.grad_ref, f32[128,256]{1,0:T(8,128)} %get-tuple-element.52.local_ref, bf16[512,256]{1,0:T(8,128)(2,1)} %bitcast.22, ...), custom_call_target="tpu_custom_call", output_to_operand_aliasing={{0}: (0, {})} | custom-call | flops 131072 | bytes 1048576 | tf_op jit(solution)/shard_map/finish/pallas_call | solution.py:351
  (33 shorter events, 0.1 us)
Async XLA Ops:
  3.7 7.5 %collective-permute-start.5 = (bf16[2,64,256]{2,1,0:T(8,128)(2,1)}, bf16[2,64,256]{2,1,0:T(8,128)(2,1)S(1)}, u32[]{:S(2)}, u32[]{:S(2)}) collective-permute-start(bf16[2,64,256]{2,1,0:T(8,128)(2,1)} %get-tuple-element.34), channel_id=1, source_target_pairs={{0,8},{8,0},{16,24},{24,16},{1,9},{9,1},{17,25},{25,17},{2,10},{10... | collective-permute-start | bytes 196616 | tf_op jit(solution)/shard_map/ppermute | solution.py:375
  4.2 8.5 %collective-permute-start.6 = (bf16[128,256]{1,0:T(8,128)(2,1)}, bf16[128,256]{1,0:T(8,128)(2,1)S(1)}, u32[]{:S(2)}, u32[]{:S(2)}) collective-permute-start(bf16[128,256]{1,0:T(8,128)(2,1)} %get-tuple-element.33), channel_id=1, source_target_pairs={{0,6},{1,7},{2,4},{3,5},{4,2},{5,3},{6,0},{7,1},{8,14},{9,15},{10,... | collective-permute-start | bytes 196616 | tf_op jit(solution)/shard_map/ppermute | solution.py:375
  8.9 6.4 %collective-permute-start.3 = (bf16[128,256]{1,0:T(8,128)(2,1)}, bf16[128,256]{1,0:T(8,128)(2,1)S(1)}, u32[]{:S(2)}, u32[]{:S(2)}) collective-permute-start(bf16[128,256]{1,0:T(8,128)(2,1)} %get-tuple-element.33), channel_id=1, source_target_pairs={{0,4},{1,5},{2,6},{3,7},{4,0},{5,1},{6,2},{7,3},{8,12},{9,13},{10,... | collective-permute-start | bytes 196616 | tf_op jit(solution)/shard_map/ppermute | solution.py:375
  8.9 7.9 %collective-permute-start.1 = (bf16[128,256]{1,0:T(8,128)(2,1)}, bf16[128,256]{1,0:T(8,128)(2,1)S(1)}, u32[]{:S(2)}, u32[]{:S(2)}) collective-permute-start(bf16[128,256]{1,0:T(8,128)(2,1)} %get-tuple-element.33), channel_id=1, source_target_pairs={{0,2},{1,3},{2,0},{3,1},{4,6},{5,7},{6,4},{7,5},{8,10},{9,11},{10,... | collective-permute-start | bytes 196616 | tf_op jit(solution)/shard_map/ppermute | solution.py:375
  9.5 4.1 %collective-permute-start.8 = (bf16[64,256]{1,0:T(8,128)(2,1)}, bf16[64,256]{1,0:T(8,128)(2,1)S(1)}, u32[]{:S(2)}, u32[]{:S(2)}) collective-permute-start(bf16[64,256]{1,0:T(8,128)(2,1)} %get-tuple-element.37), channel_id=1, source_target_pairs={{0,16},{8,24},{16,0},{24,8},{1,17},{9,25},{17,1},{25,9},{2,18},{10... | collective-permute-start | bytes 98312 | tf_op jit(solution)/shard_map/ppermute | solution.py:375
  11.2 9.9 %copy-start.8 = (bf16[2,64,256]{2,1,0:T(8,128)(2,1)}, bf16[2,64,256]{2,1,0:T(8,128)(2,1)S(1)}, u32[]{:S(2)}) copy-start(bf16[2,64,256]{2,1,0:T(8,128)(2,1)S(1)} %collective-permute-done.5.refs_19_) | copy-start | bytes 196612
  11.2 6.2 %collective-permute-start = (bf16[128,256]{1,0:T(8,128)(2,1)}, bf16[128,256]{1,0:T(8,128)(2,1)S(1)}, u32[]{:S(2)}, u32[]{:S(2)}) collective-permute-start(bf16[128,256]{1,0:T(8,128)(2,1)} %get-tuple-element.33), channel_id=1, source_target_pairs={{0,1},{1,0},{2,3},{3,2},{4,5},{5,4},{6,7},{7,6},{8,9},{9,8},{10,11... | collective-permute-start | bytes 196616 | tf_op jit(solution)/shard_map/ppermute | solution.py:375
  12.7 8.4 %copy-start.9 = (bf16[128,256]{1,0:T(8,128)(2,1)}, bf16[128,256]{1,0:T(8,128)(2,1)S(1)}, u32[]{:S(2)}) copy-start(bf16[128,256]{1,0:T(8,128)(2,1)S(1)} %collective-permute-done.6.refs_15_) | copy-start | bytes 196612
  12.7 4.7 %collective-permute-start.7 = (bf16[128,256]{1,0:T(8,128)(2,1)S(1)}, bf16[128,256]{1,0:T(8,128)(2,1)S(1)}, u32[]{:S(2)}, u32[]{:S(2)}) collective-permute-start(bf16[128,256]{1,0:T(8,128)(2,1)S(1)} %collective-permute-done.6.refs_15_), channel_id=1, source_target_pairs={{0,1},{1,0},{2,3},{3,2},{4,5},{5,4},{6,7},{7,6},{8,9},{9,8},{10,11... | collective-permute-start | bytes 196616 | tf_op jit(solution)/shard_map/ppermute | solution.py:375
  13.7 7.4 %copy-start.17 = (bf16[64,256]{1,0:T(8,128)(2,1)}, bf16[64,256]{1,0:T(8,128)(2,1)S(1)}, u32[]{:S(2)}) copy-start(bf16[64,256]{1,0:T(8,128)(2,1)S(1)} %collective-permute-done.8.refs_18_) | copy-start | bytes 98308
  13.7 4.3 %collective-permute-start.9 = (bf16[2,64,256]{2,1,0:T(8,128)(2,1)S(1)}, bf16[2,64,256]{2,1,0:T(8,128)(2,1)S(1)}, u32[]{:S(2)}, u32[]{:S(2)}) collective-permute-start(bf16[2,64,256]{2,1,0:T(8,128)(2,1)S(1)} %collective-permute-done.5.refs_19_), channel_id=1, source_target_pairs={{0,16},{8,24},{16,0},{24,8},{1,17},{9,25},{17,1},{25,9},{2,18},{10... | collective-permute-start | bytes 196616 | tf_op jit(solution)/shard_map/ppermute | solution.py:375
  15.3 5.8 %copy-start.10 = (bf16[128,256]{1,0:T(8,128)(2,1)}, bf16[128,256]{1,0:T(8,128)(2,1)S(1)}, u32[]{:S(2)}) copy-start(bf16[128,256]{1,0:T(8,128)(2,1)S(1)} %collective-permute-done.3.refs_13_) | copy-start | bytes 196612
  15.3 4.7 %collective-permute-start.4 = (bf16[128,256]{1,0:T(8,128)(2,1)S(1)}, bf16[128,256]{1,0:T(8,128)(2,1)S(1)}, u32[]{:S(2)}, u32[]{:S(2)}) collective-permute-start(bf16[128,256]{1,0:T(8,128)(2,1)S(1)} %collective-permute-done.3.refs_13_), channel_id=1, source_target_pairs={{0,1},{1,0},{2,3},{3,2},{4,5},{5,4},{6,7},{7,6},{8,9},{9,8},{10,11... | collective-permute-start | bytes 196616 | tf_op jit(solution)/shard_map/ppermute | solution.py:375
  16.8 4.3 %copy-start.11 = (bf16[128,256]{1,0:T(8,128)(2,1)}, bf16[128,256]{1,0:T(8,128)(2,1)S(1)}, u32[]{:S(2)}) copy-start(bf16[128,256]{1,0:T(8,128)(2,1)S(1)} %collective-permute-done.1.refs_11_) | copy-start | bytes 196612
  16.8 4.3 %collective-permute-start.2 = (bf16[128,256]{1,0:T(8,128)(2,1)S(1)}, bf16[128,256]{1,0:T(8,128)(2,1)S(1)}, u32[]{:S(2)}, u32[]{:S(2)}) collective-permute-start(bf16[128,256]{1,0:T(8,128)(2,1)S(1)} %collective-permute-done.1.refs_11_), channel_id=1, source_target_pairs={{0,1},{1,0},{2,3},{3,2},{4,5},{5,4},{6,7},{7,6},{8,9},{9,8},{10,11... | collective-permute-start | bytes 196616 | tf_op jit(solution)/shard_map/ppermute | solution.py:375
  17.3 3.8 %copy-start.12 = (bf16[128,256]{1,0:T(8,128)(2,1)}, bf16[128,256]{1,0:T(8,128)(2,1)S(1)}, u32[]{:S(2)}) copy-start(bf16[128,256]{1,0:T(8,128)(2,1)S(1)} %collective-permute-done.refs_10_) | copy-start | bytes 196612
  17.4 3.8 %copy-start.13 = (bf16[128,256]{1,0:T(8,128)(2,1)}, bf16[128,256]{1,0:T(8,128)(2,1)S(1)}, u32[]{:S(2)}) copy-start(bf16[128,256]{1,0:T(8,128)(2,1)S(1)} %collective-permute-done.7.refs_16_) | copy-start | bytes 196612
  17.9 3.2 %copy-start.14 = (bf16[2,64,256]{2,1,0:T(8,128)(2,1)}, bf16[2,64,256]{2,1,0:T(8,128)(2,1)S(1)}, u32[]{:S(2)}) copy-start(bf16[2,64,256]{2,1,0:T(8,128)(2,1)S(1)} %collective-permute-done.9.refs_20_) | copy-start | bytes 196612
  20.0 1.1 %copy-start.15 = (bf16[128,256]{1,0:T(8,128)(2,1)}, bf16[128,256]{1,0:T(8,128)(2,1)S(1)}, u32[]{:S(2)}) copy-start(bf16[128,256]{1,0:T(8,128)(2,1)S(1)} %collective-permute-done.4.refs_14_) | copy-start | bytes 196612
  21.1 0.6 copy-start.16
  33.0 14.8 %all-to-all-start = ((bf16[32,16,256]{2,1,0:T(8,128)(2,1)}), bf16[32,16,256]{2,1,0:T(8,128)(2,1)S(1)}, u32[]{:S(2)}, u32[]{:S(2)}) async-start(bf16[32,16,256]{2,1,0:T(8,128)(2,1)} %bitcast.23), calls=%async_computation | async-start | bytes 524288 | tf_op jit(solution)/shard_map/all_to_all | solution.py:410
  37.1 14.2 %collective-permute-start.13 = (bf16[4,128,256]{2,1,0:T(8,128)(2,1)}, bf16[4,128,256]{2,1,0:T(8,128)(2,1)S(1)}, u32[]{:S(2)}, u32[]{:S(2)}) collective-permute-start(bf16[4,128,256]{2,1,0:T(8,128)(2,1)} %get-tuple-element.55), channel_id=1, source_target_pairs={{0,1},{1,0},{2,3},{3,2},{4,5},{5,4},{6,7},{7,6},{8,9},{9,8},{10,11... | collective-permute-start | bytes 786440 | tf_op jit(solution)/shard_map/ppermute | solution.py:375
  39.0 1.9 %collective-permute-start.10 = (bf16[64,256]{1,0:T(8,128)(2,1)}, bf16[64,256]{1,0:T(8,128)(2,1)S(1)}, u32[]{:S(2)}, u32[]{:S(2)}) collective-permute-start(bf16[64,256]{1,0:T(8,128)(2,1)} %get-tuple-element.44), channel_id=1, source_target_pairs={{0,8},{8,0},{16,24},{24,16},{1,9},{9,1},{17,25},{25,17},{2,10},{10... | collective-permute-start | bytes 98312 | tf_op jit(solution)/shard_map/ppermute | solution.py:375
  39.0 4.3 %collective-permute-start.11 = (bf16[64,256]{1,0:T(8,128)(2,1)}, bf16[64,256]{1,0:T(8,128)(2,1)S(1)}, u32[]{:S(2)}, u32[]{:S(2)}) collective-permute-start(bf16[64,256]{1,0:T(8,128)(2,1)} %get-tuple-element.45), channel_id=1, source_target_pairs={{0,16},{8,24},{16,0},{24,8},{1,17},{9,25},{17,1},{25,9},{2,18},{10... | collective-permute-start | bytes 98312 | tf_op jit(solution)/shard_map/ppermute | solution.py:375
  40.4 3.8 %collective-permute-start.12 = (bf16[64,256]{1,0:T(8,128)(2,1)}, bf16[64,256]{1,0:T(8,128)(2,1)S(1)}, u32[]{:S(2)}, u32[]{:S(2)}) collective-permute-start(bf16[64,256]{1,0:T(8,128)(2,1)} %get-tuple-element.46), channel_id=1, source_target_pairs={{0,24},{8,16},{16,8},{24,0},{1,25},{9,17},{17,9},{25,1},{2,26},{10... | collective-permute-start | bytes 98312 | tf_op jit(solution)/shard_map/ppermute | solution.py:375
  40.8 16.0 %copy-start.5 = (bf16[64,256]{1,0:T(8,128)(2,1)}, bf16[64,256]{1,0:T(8,128)(2,1)S(1)}, u32[]{:S(2)}) copy-start(bf16[64,256]{1,0:T(8,128)(2,1)S(1)} %collective-permute-done.10.refs_7_) | copy-start | bytes 98308
  43.3 13.6 %copy-start.6 = (bf16[64,256]{1,0:T(8,128)(2,1)}, bf16[64,256]{1,0:T(8,128)(2,1)S(1)}, u32[]{:S(2)}) copy-start(bf16[64,256]{1,0:T(8,128)(2,1)S(1)} %collective-permute-done.11.refs_8_) | copy-start | bytes 98308
  44.2 12.7 %copy-start.7 = (bf16[64,256]{1,0:T(8,128)(2,1)}, bf16[64,256]{1,0:T(8,128)(2,1)S(1)}, u32[]{:S(2)}) copy-start(bf16[64,256]{1,0:T(8,128)(2,1)S(1)} %collective-permute-done.12.refs_9_) | copy-start | bytes 98308
  48.5 17.6 %all-to-all-start.1 = ((bf16[32,16,256]{2,1,0:T(8,128)(2,1)}), bf16[32,16,256]{2,1,0:T(8,128)(2,1)S(1)}, u32[]{:S(2)}, u32[]{:S(2)}) async-start(bf16[32,16,256]{2,1,0:T(8,128)(2,1)} %broadcast_in_dim.2), calls=%async_computation.1 | async-start | bytes 524288 | tf_op jit(solution)/shard_map/all_to_all | solution.py:420
  51.3 14.8 %copy-start.1 = (bf16[4,128,256]{2,1,0:T(8,128)(2,1)}, bf16[4,128,256]{2,1,0:T(8,128)(2,1)S(1)}, u32[]{:S(2)}) copy-start(bf16[4,128,256]{2,1,0:T(8,128)(2,1)S(1)} %collective-permute-done.13.side_ref) | copy-start | bytes 786436
  52.4 10.6 %collective-permute-start.16 = (bf16[128,256]{1,0:T(8,128)(2,1)S(1)}, bf16[128,256]{1,0:T(8,128)(2,1)S(1)}, u32[]{:S(2)}, u32[]{:S(2)}) collective-permute-start(bf16[128,256]{1,0:T(8,128)(2,1)S(1)} %get-tuple-element.62), channel_id=1, source_target_pairs={{0,6},{1,7},{2,4},{3,5},{4,2},{5,3},{6,0},{7,1},{8,14},{9,15},{10,... | collective-permute-start | bytes 196616 | tf_op jit(solution)/shard_map/ppermute | solution.py:375
  55.9 10.2 %collective-permute-start.15 = (bf16[128,256]{1,0:T(8,128)(2,1)S(1)}, bf16[128,256]{1,0:T(8,128)(2,1)S(1)}, u32[]{:S(2)}, u32[]{:S(2)}) collective-permute-start(bf16[128,256]{1,0:T(8,128)(2,1)S(1)} %get-tuple-element.63), channel_id=1, source_target_pairs={{0,4},{1,5},{2,6},{3,7},{4,0},{5,1},{6,2},{7,3},{8,12},{9,13},{10,... | collective-permute-start | bytes 196616 | tf_op jit(solution)/shard_map/ppermute | solution.py:375
  55.9 10.2 %collective-permute-start.14 = (bf16[128,256]{1,0:T(8,128)(2,1)S(1)}, bf16[128,256]{1,0:T(8,128)(2,1)S(1)}, u32[]{:S(2)}, u32[]{:S(2)}) collective-permute-start(bf16[128,256]{1,0:T(8,128)(2,1)S(1)} %get-tuple-element.64), channel_id=1, source_target_pairs={{0,2},{1,3},{2,0},{3,1},{4,6},{5,7},{6,4},{7,5},{8,10},{9,11},{10,... | collective-permute-start | bytes 196616 | tf_op jit(solution)/shard_map/ppermute | solution.py:375
  63.0 3.1 %copy-start.2 = (bf16[128,256]{1,0:T(8,128)(2,1)}, bf16[128,256]{1,0:T(8,128)(2,1)S(1)}, u32[]{:S(2)}) copy-start(bf16[128,256]{1,0:T(8,128)(2,1)S(1)} %collective-permute-done.16.refs_2_) | copy-start | bytes 196612
  66.1 0.6 copy-start.3
  66.1 0.6 copy-start.4
  66.1 0.7 %copy-start = (bf16[32,16,256]{2,1,0:T(8,128)(2,1)}, bf16[32,16,256]{2,1,0:T(8,128)(2,1)S(1)}, u32[]{:S(2)}) copy-start(bf16[32,16,256]{2,1,0:T(8,128)(2,1)S(1)} %all-to-all-done.1) | copy-start | bytes 786436

commit v6 on v5

--- a/solution.py
+++ b/solution.py
@@ -66,14 +66,16 @@
     return [slice(i, i + step) for i in range(0, count, step)]
 
 
-def pick_kernel(rows_ref, features_ref, head_ref, *rest):
-    out_refs, (features, picked, sems) = rest[:-3], rest[-3:]
+def pick_kernel(far_rows_ref, features_ref, *rest):
+    out_refs, (rows_ref, features, picked, sems) = rest[:-4], rest[-4:]
     groups, cut = rows_ref.shape[1:]
     count = features_ref.shape[0]
     group = lax.axis_index("grp")
     mover = Mover(sems)
     parts = split(count, CHUNK)
+    lines = mover.get(far_rows_ref, rows_ref)
     coming = [mover.get(features_ref.at[part], features.at[part]) for part in parts]
+    lines.wait()
     across = lax.broadcasted_iota(jnp.int32, (cut, cut), 0)
     along = lax.broadcasted_iota(jnp.int32, (cut, cut), 1)
     columns = []
@@ -84,7 +86,6 @@
     where = lax.broadcasted_iota(jnp.int32, (groups * cut, count), 1)
     table = jnp.where(where == column, 1.0, 0.0).astype(BF16)
     wait(coming)
-    mover.put(features.at[:HUB], head_ref)
     picked[...] = dot(table, features[...]).astype(BF16)
     odd_ref, even_refs = out_refs[0], out_refs[1:]
     for k in range(groups):
@@ -100,11 +101,12 @@
         pick_kernel,
         "pick_rows",
         (rows, features),
-        [((HUB, width), BF16), ((groups // 2, cut, width), BF16)]
+        [((groups // 2, cut, width), BF16)]
         + [((cut, width), BF16)] * (groups // 2),
-        [NEAR, ANY],
-        [ANY] * (2 + groups // 2),
+        [ANY, ANY],
+        [ANY] * (1 + groups // 2),
         [
+            pltpu.VMEM(rows.shape, jnp.int32),
             pltpu.VMEM((count, width), BF16),
             pltpu.VMEM((groups * cut, width), BF16),
             pltpu.SemaphoreType.DMA((1 + groups + count // CHUNK,)),
@@ -123,13 +125,14 @@
 
 
 def block_kernel(row_count, groups, *refs):
-    index_ref, owner_ref, degrees_ref, self_ref, neighbor_ref = refs[:5]
+    far_index_ref, far_owner_ref, far_degrees_ref, self_ref, neighbor_ref = refs[:5]
     features_ref, values_ref, hub_ref, cut_ref, cotangent_ref = refs[5:10]
     head_refs = refs[10 : 9 + row_count]
     piece_refs = refs[9 + row_count : 9 + row_count + groups]
-    outs = refs[9 + row_count + groups : -15]
+    outs = refs[9 + row_count + groups : -18]
     hidden_ref, grad_ref, aggregate_ref, weights_ref, odd_ref = outs[:5]
     even_refs, back_refs = outs[5 : 5 + row_count // 2], outs[5 + row_count // 2 :]
+    index_ref, owner_ref, degrees_ref = refs[-18:-15]
     pair, stack, values, edges, cotangent, heads, panels = refs[-15:-8]
     total, hidden, grad, aggregate, weights, sums, back, sems = refs[-8:]
     count, width = features_ref.shape
@@ -141,7 +144,9 @@
     mover = Mover(sems)
     parts = split(count, CHUNK)
     steps = split(values_ref.shape[0], TILE_STEP)
-    rows = [mover.get(features_ref, pair.at[:, :width])]
+    rows = [mover.get(far_index_ref, index_ref), mover.get(far_owner_ref, owner_ref)]
+    rows += [mover.get(far_degrees_ref, degrees_ref)]
+    rows += [mover.get(features_ref, pair.at[:, :width])]
     tiles = [mover.get(values_ref.at[part], values.at[part]) for part in steps]
     first = [mover.get(ref, heads.at[k + 1]) for k, ref in enumerate(head_refs)]
     for k in range(groups):
@@ -229,9 +234,12 @@
         + [((2 * width, width), BF16), ((half, HUB, width), BF16)]
         + [((HUB, width), BF16)] * half
         + [((piece, width), BF16)] * groups,
-        [SCALARS, SCALARS, NEAR] + [ANY] * (7 + len(heads) + groups),
+        [ANY] * (10 + len(heads) + groups),
         [ANY] * (5 + half + groups),
         [
+            pltpu.SMEM(index.shape, jnp.int32),
+            pltpu.SMEM(owners.shape, jnp.int32),
+            pltpu.VMEM(degrees.shape, jnp.int32),
             pltpu.VMEM((count, 2 * width), BF16),
             pltpu.VMEM((2 * width, width), BF16),
             pltpu.VMEM(values.shape, BF16),
@@ -247,7 +255,7 @@
             pltpu.VMEM((row_count, HUB, width), F32),
             pltpu.VMEM((cut.shape[1], width), BF16),
             pltpu.SemaphoreType.DMA(
-                (7 * count // CHUNK + tiles // TILE_STEP + 2 * row_count + 2 * groups + 2,)
+                (7 * count // CHUNK + tiles // TILE_STEP + 2 * row_count + 2 * groups + 5,)
             ),
         ],
         flops + 2 * tiles * TILE * TILE * width,
@@ -258,25 +266,28 @@
 
 
 def local_back_kernel(groups, *refs):
-    index_ref, self_ref, rows_ref, values_ref, aggregate_ref, grad_ref = refs[:6]
+    far_index_ref, far_self_ref, far_rows_ref, values_ref, aggregate_ref, grad_ref = refs[:6]
     piece_refs = refs[6 : 6 + groups]
-    out_ref, head_ref, values, aggregate, grad, returned, total, result, sems = refs[6 + groups :]
+    out_ref, head_ref, index_ref, self_ref, rows_ref, values, aggregate, grad = refs[6 + groups : -4]
+    returned, total, result, sems = refs[-4:]
     size = piece_refs[0].shape[0]
     picks = returned.shape[0]
     group = lax.axis_index("grp")
 
     mover = Mover(sems)
     parts = split(grad_ref.shape[0], CHUNK)
+    back = [mover.get(far_rows_ref, rows_ref), mover.get(far_self_ref, self_ref)]
+    back += [mover.get(far_index_ref, index_ref)]
     first = [mover.get(grad_ref.at[part], grad.at[part]) for part in parts]
-    back = [
+    back += [
         mover.get(ref, returned.at[aligned((group ^ k) * size, size)])
         for k, ref in enumerate(piece_refs)
     ]
     coming = [mover.get(aggregate_ref.at[part], aggregate.at[part]) for part in parts]
     steps = split(values_ref.shape[0], TILE_STEP)
     tiles = [mover.get(values_ref.at[part], values.at[part]) for part in steps]
+    wait(back)
     rows = jnp.concatenate([rows_ref[0, j : j + 1, :] for j in range(groups)], axis=1)
-    wait(back)
     for part, copy in zip(parts, first):
         where = lax.broadcasted_iota(jnp.int32, (CHUNK, picks), 0) + part.start
         table = jnp.where(where == rows, 1.0, 0.0).astype(BF16)
@@ -311,16 +322,19 @@
         "local_backward",
         (index, self_weight, rows, values, aggregate, grad, *pieces),
         [((count, width), BF16), ((HUB, width), F32)],
-        [SCALARS, NEAR, NEAR] + [ANY] * (3 + groups),
+        [ANY] * (6 + groups),
         [ANY, ANY],
         [
+            pltpu.SMEM(index.shape, jnp.int32),
+            pltpu.VMEM(self_weight.shape, BF16),
+            pltpu.VMEM(rows.shape, jnp.int32),
             pltpu.VMEM(values.shape, BF16),
             near,
             near,
             pltpu.VMEM((picks, width), BF16),
             pltpu.VMEM((count, width), F32),
             near,
-            pltpu.SemaphoreType.DMA((3 * count // CHUNK + groups + tiles // TILE_STEP + 1,)),
+            pltpu.SemaphoreType.DMA((3 * count // CHUNK + groups + tiles // TILE_STEP + 4,)),
         ],
         2 * tiles * TILE * TILE * width + 2 * count * width * (width + picks),
         2 * values.size + 8 * grad.size,
@@ -396,19 +410,22 @@
     index = tile_index.transpose(0, 2, 1)
     degrees = degrees.reshape(count // TILE, TILE)
 
-    head, odds, *pieces = pick_rows(send_rows, features)
+    head = features[:HUB]
     evens = [head] + [trade(head, "row", k) for k in range(2, row_count, 2)]
-    odds, evens[-1] = lax.optimization_barrier((trade(odds, "grp", 1), evens[-1]))
+    rows, evens[1] = lax.optimization_barrier((send_rows, evens[1]))
+    odds, *pieces = pick_rows(rows, features)
+    pieces = [pieces[0]] + [trade(pieces[k], "grp", 2 * k) for k in range(1, groups // 2)]
+    odds = trade(odds, "grp", 1)
+    odds, pieces = lax.optimization_barrier((odds, pieces))
     heads = [x for even in evens for x in (even, trade(even, "row", 1))][1:]
-    pieces = [pieces[0]] + [trade(pieces[k], "grp", 2 * k) for k in range(1, groups // 2)]
     passed = [odds] + [trade(odds, "grp", 2 * k) for k in range(1, groups // 2)]
     hidden, grad, aggregate, weights, odds, evens, pieces = block(
         index, hub_owner, degrees, self_weight, neighbor_weight, features, values,
         hub_adjacency, cut_adjacency, cotangent, heads, pieces, passed,
     )
+    odds = trade(odds, "row", 1)
     parts = weights.reshape(groups * row_count, -1, width)
     parts = lax.all_to_all(parts, everyone, split_axis=0, concat_axis=0, tiled=True)
-    odds = trade(odds, "row", 1)
     heads = [
         trade((even.astype(F32) + odds[j + 1].astype(F32)).astype(BF16), "row", 2 * j + 2)
         for j, even in enumerate(evens[1:])

time: 69.6 us -> 68.6 us (0.986)
  Pallas kernels: 22.6 us -> 20.9 us
  local copies, waits for them, and re-layouts: 2.04 us -> 2.92 us
    pallas_call x3, Pallas kernels: 20.5 us -> 18.8 us  [call(): pl.pallas_call(kernel, in_specs=in_specs, out_specs=out_specs, out_shape=...]
    slice x0 -> x1, local copies, waits for them, and re-layouts: none -> 0.85 us  [on_device(): head = features[:HUB]]
  transfers between devices with their start and end apart: 19 -> 19, of which waited for: 8 -> 7; matrix products, arithmetic and copies ran while one was open for 3% -> 3% of each run, Pallas kernels for 9% -> 12%
where the time goes in v6:
time: 68.6 us; the launch traced here: 68.2 us
  starting transfers between devices  28.6 us (42%)
  Pallas kernels  20.9 us (30%)
  waiting for transfers between devices  13.6 us (20%)
  local copies, waits for them, and re-layouts  2.92 us (4%)
  other arithmetic  1.1 us (2%)
  between operations  1 us (1%)
    ppermute x17, starting transfers between devices, trade(): lax.ppermute(value, axis, [(r, r ^ k) for r in range(lax.axis_size(axis))])  21.1 us
    pallas_call x3, Pallas kernels, call(): pl.pallas_call(kernel, in_specs=in_specs, out_specs=out_specs, out_shape=...  18.8 us
    ppermute x17, waiting for transfers between devices, trade(): lax.ppermute(value, axis, [(r, r ^ k) for r in range(lax.axis_size(axis))])  10 us
    all_to_all x1, starting transfers between devices, on_device(): lax.all_to_all(parts, everyone, split_axis=0, concat_axis=0, tiled=True)  4.8 us
    all_to_all x1, waiting for transfers between devices, on_device(): lax.all_to_all(parts, everyone, split_axis=0, concat_axis=0, tiled=True)  3.58 us
    all_to_all x1, starting transfers between devices, on_device(): lax.all_to_all(sums, everyone, split_axis=0, concat_axis=0, tiled=True)  2.77 us
    pallas_call x1, Pallas kernels, finish(): pl.pallas_call(finish_kernel, in_specs=[ANY] * (5 + len(heads)), out_spec...  2.1 us
  transfers between devices with their start and end apart: 19, of which 7 were waited for; matrix products, arithmetic and copies ran while one was open for 3% of the time, Pallas kernels for 12%

profile of v6, /device:TPU:0, one launch (start us, length us, event | category | flops | bytes accessed | tf_op | source)
XLA Modules:
  0.0 68.2 jit_solution(5915513214844897374)
XLA Ops:
  0.6 0.8 %slice.12 = bf16[128,256]{1,0:T(8,128)(2,1)S(1)} slice(bf16[2048,256]{1,0:T(8,128)(2,1)} %refs_5_.1), slice={[0:128], [0:256]} | slice | bytes 131072 | tf_op jit(solution)/shard_map/slice | solution.py:413
  1.5 3.0 %collective-permute-start.1 = (bf16[128,256]{1,0:T(8,128)(2,1)S(1)}, bf16[128,256]{1,0:T(8,128)(2,1)S(1)}, u32[]{:S(2)}, u32[]{:S(2)}) collective-permute-start(bf16[128,256]{1,0:T(8,128)(2,1)S(1)} %slice.12), channel_id=1, source_target_pairs={{0,2},{1,3},{2,0},{3,1},{4,6},{5,7},{6,4},{7,5},{8,10},{9,11},{10,... | collective-permute-start | bytes 196616 | tf_op jit(solution)/shard_map/ppermute | solution.py:389
  4.5 2.5 %collective-permute-start.5 = (bf16[128,256]{1,0:T(8,128)(2,1)S(1)}, bf16[128,256]{1,0:T(8,128)(2,1)S(1)}, u32[]{:S(2)}, u32[]{:S(2)}) collective-permute-start(bf16[128,256]{1,0:T(8,128)(2,1)S(1)} %slice.12), channel_id=1, source_target_pairs={{0,6},{1,7},{2,4},{3,5},{4,2},{5,3},{6,0},{7,1},{8,14},{9,15},{10,... | collective-permute-start | bytes 196616 | tf_op jit(solution)/shard_map/ppermute | solution.py:389
  7.0 0.1 collective-permute-start.3
  7.1 0.0 collective-permute-done.1.refs_11_
  7.1 2.4 %pick_rows.1 = (bf16[2,64,256]{2,1,0:T(8,128)(2,1)}, bf16[64,256]{1,0:T(8,128)(2,1)}, bf16[64,256]{1,0:T(8,128)(2,1)}) custom-call(s32[1,4,64]{2,1,0:T(4,128)} %refs_2_.1, bf16[2048,256]{1,0:T(8,128)(2,1)} %refs_5_.1), custom_call_target="tpu_custom_call" | custom-call | flops 268435456 | bytes 1048576 | tf_op jit(solution)/shard_map/pick_rows/pallas_call | solution.py:23
  9.5 0.1 collective-permute-start.7
  9.6 1.7 %collective-permute-start.8 = (bf16[64,256]{1,0:T(8,128)(2,1)}, bf16[64,256]{1,0:T(8,128)(2,1)S(1)}, u32[]{:S(2)}, u32[]{:S(2)}) collective-permute-start(bf16[64,256]{1,0:T(8,128)(2,1)} %get-tuple-element.39), channel_id=1, source_target_pairs={{0,16},{8,24},{16,0},{24,8},{1,17},{9,25},{17,1},{25,9},{2,18},{10... | collective-permute-start | bytes 98312 | tf_op jit(solution)/shard_map/ppermute | solution.py:389
  11.3 1.5 %collective-permute-start = (bf16[128,256]{1,0:T(8,128)(2,1)S(1)}, bf16[128,256]{1,0:T(8,128)(2,1)S(1)}, u32[]{:S(2)}, u32[]{:S(2)}) collective-permute-start(bf16[128,256]{1,0:T(8,128)(2,1)S(1)} %slice.12), channel_id=1, source_target_pairs={{0,1},{1,0},{2,3},{3,2},{4,5},{5,4},{6,7},{7,6},{8,9},{9,8},{10,11... | collective-permute-start | bytes 196616 | tf_op jit(solution)/shard_map/ppermute | solution.py:389
  12.7 0.0 collective-permute-done.5.refs_15_
  12.7 0.5 collective-permute-start.2
  13.3 0.1 collective-permute-done.3.refs_13_
  13.4 1.5 %collective-permute-start.6 = (bf16[128,256]{1,0:T(8,128)(2,1)S(1)}, bf16[128,256]{1,0:T(8,128)(2,1)S(1)}, u32[]{:S(2)}, u32[]{:S(2)}) collective-permute-start(bf16[128,256]{1,0:T(8,128)(2,1)S(1)} %collective-permute-done.5.refs_15_), channel_id=1, source_target_pairs={{0,1},{1,0},{2,3},{3,2},{4,5},{5,4},{6,7},{7,6},{8,9},{9,8},{10,11... | collective-permute-start | bytes 196616 | tf_op jit(solution)/shard_map/ppermute | solution.py:389
  14.9 0.0 collective-permute-done.8.refs_18_
  14.9 0.5 collective-permute-start.4
  15.5 0.0 collective-permute-done.7.refs_19_
  15.5 1.5 %collective-permute-start.9 = (bf16[2,64,256]{2,1,0:T(8,128)(2,1)S(1)}, bf16[2,64,256]{2,1,0:T(8,128)(2,1)S(1)}, u32[]{:S(2)}, u32[]{:S(2)}) collective-permute-start(bf16[2,64,256]{2,1,0:T(8,128)(2,1)S(1)} %collective-permute-done.7.refs_19_), channel_id=1, source_target_pairs={{0,16},{8,24},{16,0},{24,8},{1,17},{9,25},{17,1},{25,9},{2,18},{10... | collective-permute-start | bytes 196616 | tf_op jit(solution)/shard_map/ppermute | solution.py:389
  17.0 0.0 collective-permute-done.refs_10_
  17.0 2.0 %collective-permute-done.6.refs_16_ = bf16[128,256]{1,0:T(8,128)(2,1)S(1)} collective-permute-done((bf16[128,256]{1,0:T(8,128)(2,1)S(1)}, bf16[128,256]{1,0:T(8,128)(2,1)S(1)}, u32[]{:S(2)}, u32[]{:S(2)}) %collective-permute-start.6) | collective-permute-done | bytes 65568 | tf_op jit(solution)/shard_map/ppermute | solution.py:389
  19.0 0.7 %collective-permute-done.4.refs_14_ = bf16[128,256]{1,0:T(8,128)(2,1)S(1)} collective-permute-done((bf16[128,256]{1,0:T(8,128)(2,1)S(1)}, bf16[128,256]{1,0:T(8,128)(2,1)S(1)}, u32[]{:S(2)}, u32[]{:S(2)}) %collective-permute-start.4) | collective-permute-done | bytes 65568 | tf_op jit(solution)/shard_map/ppermute | solution.py:389
  19.7 0.0 collective-permute-done.2.refs_12_
  19.7 0.0 collective-permute-done.9.refs_20_
  19.8 0.5 copy-done.15
  20.4 0.0 copy-done.13
  20.4 0.0 copy-done.16
  20.4 11.0 %block.1 = (bf16[2048,256]{1,0:T(8,128)(2,1)}, bf16[2048,256]{1,0:T(8,128)(2,1)}, bf16[2048,256]{1,0:T(8,128)(2,1)}, bf16[512,256]{1,0:T(8,128)(2,1)}, bf16[4,12...) custom-call(s32[1,2,64]{2,1,0:T(2,128)} %bitcast.24, ...), custom_call_target="tpu_custom_call" | custom-call | flops 4563402752 | bytes 14680064 | tf_op jit(solution)/shard_map/block/pallas_call | solution.py:23
  31.4 4.8 %all-to-all-start = ((bf16[32,16,256]{2,1,0:T(8,128)(2,1)}), bf16[32,16,256]{2,1,0:T(8,128)(2,1)S(1)}, u32[]{:S(2)}, u32[]{:S(2)}) async-start(bf16[32,16,256]{2,1,0:T(8,128)(2,1)} %bitcast.23), calls=%async_computation | async-start | bytes 524288 | tf_op jit(solution)/shard_map/all_to_all | solution.py:428
  36.2 1.8 %collective-permute-start.13 = (bf16[4,128,256]{2,1,0:T(8,128)(2,1)}, bf16[4,128,256]{2,1,0:T(8,128)(2,1)S(1)}, u32[]{:S(2)}, u32[]{:S(2)}) collective-permute-start(bf16[4,128,256]{2,1,0:T(8,128)(2,1)} %get-tuple-element.59), channel_id=1, source_target_pairs={{0,1},{1,0},{2,3},{3,2},{4,5},{5,4},{6,7},{7,6},{8,9},{9,8},{10,11... | collective-permute-start | bytes 786440 | tf_op jit(solution)/shard_map/ppermute | solution.py:389
  38.0 0.0 collective-permute-start.10
  38.0 1.5 %collective-permute-start.11 = (bf16[64,256]{1,0:T(8,128)(2,1)}, bf16[64,256]{1,0:T(8,128)(2,1)S(1)}, u32[]{:S(2)}, u32[]{:S(2)}) collective-permute-start(bf16[64,256]{1,0:T(8,128)(2,1)} %get-tuple-element.49), channel_id=1, source_target_pairs={{0,16},{8,24},{16,0},{24,8},{1,17},{9,25},{17,1},{25,9},{2,18},{10... | collective-permute-start | bytes 98312 | tf_op jit(solution)/shard_map/ppermute | solution.py:389
  39.5 0.4 collective-permute-start.12
  39.9 2.5 %collective-permute-done.11.refs_8_ = bf16[64,256]{1,0:T(8,128)(2,1)S(1)} collective-permute-done((bf16[64,256]{1,0:T(8,128)(2,1)}, bf16[64,256]{1,0:T(8,128)(2,1)S(1)}, u32[]{:S(2)}, u32[]{:S(2)}) %collective-permute-start.11) | collective-permute-done | bytes 32800 | tf_op jit(solution)/shard_map/ppermute | solution.py:389
  42.4 0.9 %collective-permute-done.12.refs_9_ = bf16[64,256]{1,0:T(8,128)(2,1)S(1)} collective-permute-done((bf16[64,256]{1,0:T(8,128)(2,1)}, bf16[64,256]{1,0:T(8,128)(2,1)S(1)}, u32[]{:S(2)}, u32[]{:S(2)}) %collective-permute-start.12) | collective-permute-done | bytes 32800 | tf_op jit(solution)/shard_map/ppermute | solution.py:389
  43.2 3.6 %all-to-all-done = bf16[32,16,256]{2,1,0:T(8,128)(2,1)S(1)} async-done(((bf16[32,16,256]{2,1,0:T(8,128)(2,1)}), bf16[32,16,256]{2,1,0:T(8,128)(2,1)S(1)}, u32[]{:S(2)}, u32[]{:S(2)}) %all-to-all-start) | async-done | bytes 262176 | tf_op jit(solution)/shard_map/all_to_all | solution.py:428
  46.8 0.1 reduce_sum.12
  46.9 0.7 %broadcast_in_dim.2 = bf16[32,16,256]{2,1,0:T(8,128)(2,1)} broadcast(bf16[16,256]{1,0:T(8,128)(2,1)S(1)} %reduce_sum.12), dimensions={1,2} | broadcast | bytes 270336 | tf_op jit(solution)/shard_map/broadcast_in_dim | solution.py:436
  47.6 2.8 %all-to-all-start.1 = ((bf16[32,16,256]{2,1,0:T(8,128)(2,1)}), bf16[32,16,256]{2,1,0:T(8,128)(2,1)S(1)}, u32[]{:S(2)}, u32[]{:S(2)}) async-start(bf16[32,16,256]{2,1,0:T(8,128)(2,1)} %broadcast_in_dim.2), calls=%async_computation.1 | async-start | bytes 524288 | tf_op jit(solution)/shard_map/all_to_all | solution.py:437
  50.4 0.0 collective-permute-done.13.side_ref
  50.4 1.0 %fusion = (bf16[128,256]{1,0:T(8,128)(2,1)S(1)}, bf16[128,256]{1,0:T(8,128)(2,1)S(1)}, bf16[128,256]{1,0:T(8,128)(2,1)S(1)}) fusion(bf16[128,256]{1,0:T(8,128)(2,1)} %get-tuple-element.62, bf16[4,128,256]{2,1,0:T(8,128)(2,1)S(1)} %collective-permute-done.13.side_ref, bf16[128,256]{1,0:T(8,128)(2,1)} %get-tuple-element.61, bf16[128,256]{1,0:T(8,128)(2,1)} %get-tuple-element.60), kind=kLoop, calls=%fused_computation.1 | loop fusion | flops 393216 | bytes 589824 | tf_op jit(solution)/shard_map/convert_element_type | solution.py:430
  51.4 3.5 %collective-permute-start.16 = (bf16[128,256]{1,0:T(8,128)(2,1)S(1)}, bf16[128,256]{1,0:T(8,128)(2,1)S(1)}, u32[]{:S(2)}, u32[]{:S(2)}) collective-permute-start(bf16[128,256]{1,0:T(8,128)(2,1)S(1)} %get-tuple-element.66), channel_id=1, source_target_pairs={{0,6},{1,7},{2,4},{3,5},{4,2},{5,3},{6,0},{7,1},{8,14},{9,15},{10,... | collective-permute-start | bytes 196616 | tf_op jit(solution)/shard_map/ppermute | solution.py:389
  55.0 0.0 collective-permute-start.15
  55.0 0.9 %collective-permute-start.14 = (bf16[128,256]{1,0:T(8,128)(2,1)S(1)}, bf16[128,256]{1,0:T(8,128)(2,1)S(1)}, u32[]{:S(2)}, u32[]{:S(2)}) collective-permute-start(bf16[128,256]{1,0:T(8,128)(2,1)S(1)} %get-tuple-element.68), channel_id=1, source_target_pairs={{0,2},{1,3},{2,0},{3,1},{4,6},{5,7},{6,4},{7,5},{8,10},{9,11},{10,... | collective-permute-start | bytes 196616 | tf_op jit(solution)/shard_map/ppermute | solution.py:389
  55.9 5.5 %local_backward.1 = (bf16[2048,256]{1,0:T(8,128)(2,1)}, f32[128,256]{1,0:T(8,128)}) custom-call(s32[1,2,64]{2,1,0:T(2,128)} %bitcast.25, bf16[256,256]{1,0:T(8,128)(2,1)} %refs_1_.3, s32[1,4,64]{2,1,0:T(4,128)} %refs_2_.1, bf16[64,128,128]{2,1,0:T(8,128)(2,1)} %bitcast.21, bf16[2048,256]{1,0:T(8,128)(2,1)} %get-tuple-element.44.refs_4_, ...), custom_call_target="tpu_custom_call" | custom-call | flops 1073741824 | bytes 6291456 | tf_op jit(solution)/shard_map/local_backward/pallas_call | solution.py:23
  61.4 3.8 %collective-permute-done.15.refs_1_ = bf16[128,256]{1,0:T(8,128)(2,1)S(1)} collective-permute-done((bf16[128,256]{1,0:T(8,128)(2,1)S(1)}, bf16[128,256]{1,0:T(8,128)(2,1)S(1)}, u32[]{:S(2)}, u32[]{:S(2)}) %collective-permute-start.15) | collective-permute-done | bytes 65568 | tf_op jit(solution)/shard_map/ppermute | solution.py:389
  65.2 0.6 copy-done.3
  65.8 0.0 copy-done.4
  65.8 0.1 copy-done
  65.9 2.1 %finish.1 = (bf16[2048,256]{1,0:T(8,128)(2,1)}, f32[256,256]{1,0:T(8,128)}, f32[256,256]{1,0:T(8,128)}) custom-call(bf16[2048,256]{1,0:T(8,128)(2,1)} %get-tuple-element.55.grad_ref, f32[128,256]{1,0:T(8,128)} %get-tuple-element.56.local_ref, bf16[512,256]{1,0:T(8,128)(2,1)} %bitcast.22, ...), custom_call_target="tpu_custom_call", output_to_operand_aliasing={{0}: (0, {})} | custom-call | flops 131072 | bytes 1048576 | tf_op jit(solution)/shard_map/finish/pallas_call | solution.py:365
  (34 shorter events, 0.1 us)
Async XLA Ops:
  1.5 5.6 %collective-permute-start.1 = (bf16[128,256]{1,0:T(8,128)(2,1)S(1)}, bf16[128,256]{1,0:T(8,128)(2,1)S(1)}, u32[]{:S(2)}, u32[]{:S(2)}) collective-permute-start(bf16[128,256]{1,0:T(8,128)(2,1)S(1)} %slice.12), channel_id=1, source_target_pairs={{0,2},{1,3},{2,0},{3,1},{4,6},{5,7},{6,4},{7,5},{8,10},{9,11},{10,... | collective-permute-start | bytes 196616 | tf_op jit(solution)/shard_map/ppermute | solution.py:389
  4.5 8.2 %collective-permute-start.5 = (bf16[128,256]{1,0:T(8,128)(2,1)S(1)}, bf16[128,256]{1,0:T(8,128)(2,1)S(1)}, u32[]{:S(2)}, u32[]{:S(2)}) collective-permute-start(bf16[128,256]{1,0:T(8,128)(2,1)S(1)} %slice.12), channel_id=1, source_target_pairs={{0,6},{1,7},{2,4},{3,5},{4,2},{5,3},{6,0},{7,1},{8,14},{9,15},{10,... | collective-permute-start | bytes 196616 | tf_op jit(solution)/shard_map/ppermute | solution.py:389
  7.0 6.4 %collective-permute-start.3 = (bf16[128,256]{1,0:T(8,128)(2,1)S(1)}, bf16[128,256]{1,0:T(8,128)(2,1)S(1)}, u32[]{:S(2)}, u32[]{:S(2)}) collective-permute-start(bf16[128,256]{1,0:T(8,128)(2,1)S(1)} %slice.12), channel_id=1, source_target_pairs={{0,4},{1,5},{2,6},{3,7},{4,0},{5,1},{6,2},{7,3},{8,12},{9,13},{10,... | collective-permute-start | bytes 196616 | tf_op jit(solution)/shard_map/ppermute | solution.py:389
  7.1 12.7 %copy-start.8 = (bf16[128,256]{1,0:T(8,128)(2,1)}, bf16[128,256]{1,0:T(8,128)(2,1)S(1)}, u32[]{:S(2)}) copy-start(bf16[128,256]{1,0:T(8,128)(2,1)S(1)} %collective-permute-done.1.refs_11_) | copy-start | bytes 196612
  9.5 6.0 %collective-permute-start.7 = (bf16[2,64,256]{2,1,0:T(8,128)(2,1)}, bf16[2,64,256]{2,1,0:T(8,128)(2,1)S(1)}, u32[]{:S(2)}, u32[]{:S(2)}) collective-permute-start(bf16[2,64,256]{2,1,0:T(8,128)(2,1)} %get-tuple-element.37), channel_id=1, source_target_pairs={{0,8},{8,0},{16,24},{24,16},{1,9},{9,1},{17,25},{25,17},{2,10},{10... | collective-permute-start | bytes 196616 | tf_op jit(solution)/shard_map/ppermute | solution.py:389
  9.6 5.3 %collective-permute-start.8 = (bf16[64,256]{1,0:T(8,128)(2,1)}, bf16[64,256]{1,0:T(8,128)(2,1)S(1)}, u32[]{:S(2)}, u32[]{:S(2)}) collective-permute-start(bf16[64,256]{1,0:T(8,128)(2,1)} %get-tuple-element.39), channel_id=1, source_target_pairs={{0,16},{8,24},{16,0},{24,8},{1,17},{9,25},{17,1},{25,9},{2,18},{10... | collective-permute-start | bytes 98312 | tf_op jit(solution)/shard_map/ppermute | solution.py:389
  11.3 5.7 %collective-permute-start = (bf16[128,256]{1,0:T(8,128)(2,1)S(1)}, bf16[128,256]{1,0:T(8,128)(2,1)S(1)}, u32[]{:S(2)}, u32[]{:S(2)}) collective-permute-start(bf16[128,256]{1,0:T(8,128)(2,1)S(1)} %slice.12), channel_id=1, source_target_pairs={{0,1},{1,0},{2,3},{3,2},{4,5},{5,4},{6,7},{7,6},{8,9},{9,8},{10,11... | collective-permute-start | bytes 196616 | tf_op jit(solution)/shard_map/ppermute | solution.py:389
  12.7 7.0 %copy-start.9 = (bf16[128,256]{1,0:T(8,128)(2,1)}, bf16[128,256]{1,0:T(8,128)(2,1)S(1)}, u32[]{:S(2)}) copy-start(bf16[128,256]{1,0:T(8,128)(2,1)S(1)} %collective-permute-done.5.refs_15_) | copy-start | bytes 196612
  12.7 7.0 %collective-permute-start.2 = (bf16[128,256]{1,0:T(8,128)(2,1)S(1)}, bf16[128,256]{1,0:T(8,128)(2,1)S(1)}, u32[]{:S(2)}, u32[]{:S(2)}) collective-permute-start(bf16[128,256]{1,0:T(8,128)(2,1)S(1)} %collective-permute-done.1.refs_11_), channel_id=1, source_target_pairs={{0,1},{1,0},{2,3},{3,2},{4,5},{5,4},{6,7},{7,6},{8,9},{9,8},{10,11... | collective-permute-start | bytes 196616 | tf_op jit(solution)/shard_map/ppermute | solution.py:389
  13.4 6.4 %copy-start.10 = (bf16[128,256]{1,0:T(8,128)(2,1)}, bf16[128,256]{1,0:T(8,128)(2,1)S(1)}, u32[]{:S(2)}) copy-start(bf16[128,256]{1,0:T(8,128)(2,1)S(1)} %collective-permute-done.3.refs_13_) | copy-start | bytes 196612
  13.4 5.6 %collective-permute-start.6 = (bf16[128,256]{1,0:T(8,128)(2,1)S(1)}, bf16[128,256]{1,0:T(8,128)(2,1)S(1)}, u32[]{:S(2)}, u32[]{:S(2)}) collective-permute-start(bf16[128,256]{1,0:T(8,128)(2,1)S(1)} %collective-permute-done.5.refs_15_), channel_id=1, source_target_pairs={{0,1},{1,0},{2,3},{3,2},{4,5},{5,4},{6,7},{7,6},{8,9},{9,8},{10,11... | collective-permute-start | bytes 196616 | tf_op jit(solution)/shard_map/ppermute | solution.py:389
  14.9 4.9 %copy-start.17 = (bf16[64,256]{1,0:T(8,128)(2,1)}, bf16[64,256]{1,0:T(8,128)(2,1)S(1)}, u32[]{:S(2)}) copy-start(bf16[64,256]{1,0:T(8,128)(2,1)S(1)} %collective-permute-done.8.refs_18_) | copy-start | bytes 98308
  14.9 4.8 %collective-permute-start.4 = (bf16[128,256]{1,0:T(8,128)(2,1)S(1)}, bf16[128,256]{1,0:T(8,128)(2,1)S(1)}, u32[]{:S(2)}, u32[]{:S(2)}) collective-permute-start(bf16[128,256]{1,0:T(8,128)(2,1)S(1)} %collective-permute-done.3.refs_13_), channel_id=1, source_target_pairs={{0,1},{1,0},{2,3},{3,2},{4,5},{5,4},{6,7},{7,6},{8,9},{9,8},{10,11... | collective-permute-start | bytes 196616 | tf_op jit(solution)/shard_map/ppermute | solution.py:389
  15.5 4.3 %copy-start.11 = (bf16[2,64,256]{2,1,0:T(8,128)(2,1)}, bf16[2,64,256]{2,1,0:T(8,128)(2,1)S(1)}, u32[]{:S(2)}) copy-start(bf16[2,64,256]{2,1,0:T(8,128)(2,1)S(1)} %collective-permute-done.7.refs_19_) | copy-start | bytes 196612
  15.5 4.3 %collective-permute-start.9 = (bf16[2,64,256]{2,1,0:T(8,128)(2,1)S(1)}, bf16[2,64,256]{2,1,0:T(8,128)(2,1)S(1)}, u32[]{:S(2)}, u32[]{:S(2)}) collective-permute-start(bf16[2,64,256]{2,1,0:T(8,128)(2,1)S(1)} %collective-permute-done.7.refs_19_), channel_id=1, source_target_pairs={{0,16},{8,24},{16,0},{24,8},{1,17},{9,25},{17,1},{25,9},{2,18},{10... | collective-permute-start | bytes 196616 | tf_op jit(solution)/shard_map/ppermute | solution.py:389
  17.0 2.8 %copy-start.12 = (bf16[128,256]{1,0:T(8,128)(2,1)}, bf16[128,256]{1,0:T(8,128)(2,1)S(1)}, u32[]{:S(2)}) copy-start(bf16[128,256]{1,0:T(8,128)(2,1)S(1)} %collective-permute-done.refs_10_) | copy-start | bytes 196612
  19.0 0.8 %copy-start.14 = (bf16[128,256]{1,0:T(8,128)(2,1)}, bf16[128,256]{1,0:T(8,128)(2,1)S(1)}, u32[]{:S(2)}) copy-start(bf16[128,256]{1,0:T(8,128)(2,1)S(1)} %collective-permute-done.6.refs_16_) | copy-start | bytes 196612
  19.7 0.6 copy-start.15
  19.7 0.6 copy-start.13
  19.7 0.7 copy-start.16
  31.4 15.5 %all-to-all-start = ((bf16[32,16,256]{2,1,0:T(8,128)(2,1)}), bf16[32,16,256]{2,1,0:T(8,128)(2,1)S(1)}, u32[]{:S(2)}, u32[]{:S(2)}) async-start(bf16[32,16,256]{2,1,0:T(8,128)(2,1)} %bitcast.23), calls=%async_computation | async-start | bytes 524288 | tf_op jit(solution)/shard_map/all_to_all | solution.py:428
  36.2 14.2 %collective-permute-start.13 = (bf16[4,128,256]{2,1,0:T(8,128)(2,1)}, bf16[4,128,256]{2,1,0:T(8,128)(2,1)S(1)}, u32[]{:S(2)}, u32[]{:S(2)}) collective-permute-start(bf16[4,128,256]{2,1,0:T(8,128)(2,1)} %get-tuple-element.59), channel_id=1, source_target_pairs={{0,1},{1,0},{2,3},{3,2},{4,5},{5,4},{6,7},{7,6},{8,9},{9,8},{10,11... | collective-permute-start | bytes 786440 | tf_op jit(solution)/shard_map/ppermute | solution.py:389
  38.0 1.9 %collective-permute-start.10 = (bf16[64,256]{1,0:T(8,128)(2,1)}, bf16[64,256]{1,0:T(8,128)(2,1)S(1)}, u32[]{:S(2)}, u32[]{:S(2)}) collective-permute-start(bf16[64,256]{1,0:T(8,128)(2,1)} %get-tuple-element.48), channel_id=1, source_target_pairs={{0,8},{8,0},{16,24},{24,16},{1,9},{9,1},{17,25},{25,17},{2,10},{10... | collective-permute-start | bytes 98312 | tf_op jit(solution)/shard_map/ppermute | solution.py:389
  38.0 4.3 %collective-permute-start.11 = (bf16[64,256]{1,0:T(8,128)(2,1)}, bf16[64,256]{1,0:T(8,128)(2,1)S(1)}, u32[]{:S(2)}, u32[]{:S(2)}) collective-permute-start(bf16[64,256]{1,0:T(8,128)(2,1)} %get-tuple-element.49), channel_id=1, source_target_pairs={{0,16},{8,24},{16,0},{24,8},{1,17},{9,25},{17,1},{25,9},{2,18},{10... | collective-permute-start | bytes 98312 | tf_op jit(solution)/shard_map/ppermute | solution.py:389
  39.5 3.8 %collective-permute-start.12 = (bf16[64,256]{1,0:T(8,128)(2,1)}, bf16[64,256]{1,0:T(8,128)(2,1)S(1)}, u32[]{:S(2)}, u32[]{:S(2)}) collective-permute-start(bf16[64,256]{1,0:T(8,128)(2,1)} %get-tuple-element.50), channel_id=1, source_target_pairs={{0,24},{8,16},{16,8},{24,0},{1,25},{9,17},{17,9},{25,1},{2,26},{10... | collective-permute-start | bytes 98312 | tf_op jit(solution)/shard_map/ppermute | solution.py:389
  39.9 16.0 %copy-start.5 = (bf16[64,256]{1,0:T(8,128)(2,1)}, bf16[64,256]{1,0:T(8,128)(2,1)S(1)}, u32[]{:S(2)}) copy-start(bf16[64,256]{1,0:T(8,128)(2,1)S(1)} %collective-permute-done.10.refs_7_) | copy-start | bytes 98308
  42.4 13.6 %copy-start.6 = (bf16[64,256]{1,0:T(8,128)(2,1)}, bf16[64,256]{1,0:T(8,128)(2,1)S(1)}, u32[]{:S(2)}) copy-start(bf16[64,256]{1,0:T(8,128)(2,1)S(1)} %collective-permute-done.11.refs_8_) | copy-start | bytes 98308
  43.2 12.7 %copy-start.7 = (bf16[64,256]{1,0:T(8,128)(2,1)}, bf16[64,256]{1,0:T(8,128)(2,1)S(1)}, u32[]{:S(2)}) copy-start(bf16[64,256]{1,0:T(8,128)(2,1)S(1)} %collective-permute-done.12.refs_9_) | copy-start | bytes 98308
  47.6 17.6 %all-to-all-start.1 = ((bf16[32,16,256]{2,1,0:T(8,128)(2,1)}), bf16[32,16,256]{2,1,0:T(8,128)(2,1)S(1)}, u32[]{:S(2)}, u32[]{:S(2)}) async-start(bf16[32,16,256]{2,1,0:T(8,128)(2,1)} %broadcast_in_dim.2), calls=%async_computation.1 | async-start | bytes 524288 | tf_op jit(solution)/shard_map/all_to_all | solution.py:437
  50.4 14.8 %copy-start.1 = (bf16[4,128,256]{2,1,0:T(8,128)(2,1)}, bf16[4,128,256]{2,1,0:T(8,128)(2,1)S(1)}, u32[]{:S(2)}) copy-start(bf16[4,128,256]{2,1,0:T(8,128)(2,1)S(1)} %collective-permute-done.13.side_ref) | copy-start | bytes 786436
  51.4 9.9 %collective-permute-start.16 = (bf16[128,256]{1,0:T(8,128)(2,1)S(1)}, bf16[128,256]{1,0:T(8,128)(2,1)S(1)}, u32[]{:S(2)}, u32[]{:S(2)}) collective-permute-start(bf16[128,256]{1,0:T(8,128)(2,1)S(1)} %get-tuple-element.66), channel_id=1, source_target_pairs={{0,6},{1,7},{2,4},{3,5},{4,2},{5,3},{6,0},{7,1},{8,14},{9,15},{10,... | collective-permute-start | bytes 196616 | tf_op jit(solution)/shard_map/ppermute | solution.py:389
  55.0 10.2 %collective-permute-start.15 = (bf16[128,256]{1,0:T(8,128)(2,1)S(1)}, bf16[128,256]{1,0:T(8,128)(2,1)S(1)}, u32[]{:S(2)}, u32[]{:S(2)}) collective-permute-start(bf16[128,256]{1,0:T(8,128)(2,1)S(1)} %get-tuple-element.67), channel_id=1, source_target_pairs={{0,4},{1,5},{2,6},{3,7},{4,0},{5,1},{6,2},{7,3},{8,12},{9,13},{10,... | collective-permute-start | bytes 196616 | tf_op jit(solution)/shard_map/ppermute | solution.py:389
  55.0 10.2 %collective-permute-start.14 = (bf16[128,256]{1,0:T(8,128)(2,1)S(1)}, bf16[128,256]{1,0:T(8,128)(2,1)S(1)}, u32[]{:S(2)}, u32[]{:S(2)}) collective-permute-start(bf16[128,256]{1,0:T(8,128)(2,1)S(1)} %get-tuple-element.68), channel_id=1, source_target_pairs={{0,2},{1,3},{2,0},{3,1},{4,6},{5,7},{6,4},{7,5},{8,10},{9,11},{10,... | collective-permute-start | bytes 196616 | tf_op jit(solution)/shard_map/ppermute | solution.py:389
  61.4 3.8 %copy-start.2 = (bf16[128,256]{1,0:T(8,128)(2,1)}, bf16[128,256]{1,0:T(8,128)(2,1)S(1)}, u32[]{:S(2)}) copy-start(bf16[128,256]{1,0:T(8,128)(2,1)S(1)} %collective-permute-done.16.refs_2_) | copy-start | bytes 196612
  65.2 0.6 copy-start.3
  65.2 0.6 copy-start.4
  65.2 0.7 %copy-start = (bf16[32,16,256]{2,1,0:T(8,128)(2,1)}, bf16[32,16,256]{2,1,0:T(8,128)(2,1)S(1)}, u32[]{:S(2)}) copy-start(bf16[32,16,256]{2,1,0:T(8,128)(2,1)S(1)} %all-to-all-done.1) | copy-start | bytes 786436

commit v7 on v6

--- a/solution.py
+++ b/solution.py
@@ -142,7 +142,8 @@
     group, place = lax.axis_index("grp"), lax.axis_index("row")
 
     mover = Mover(sems)
-    parts = split(count, CHUNK)
+    early = count * 3 // 8
+    parts = [slice(0, early), slice(early, count)]
     steps = split(values_ref.shape[0], TILE_STEP)
     rows = [mover.get(far_index_ref, index_ref), mover.get(far_owner_ref, owner_ref)]
     rows += [mover.get(far_degrees_ref, degrees_ref)]
@@ -255,7 +256,7 @@
             pltpu.VMEM((row_count, HUB, width), F32),
             pltpu.VMEM((cut.shape[1], width), BF16),
             pltpu.SemaphoreType.DMA(
-                (7 * count // CHUNK + tiles // TILE_STEP + 2 * row_count + 2 * groups + 5,)
+                (14 + tiles // TILE_STEP + 2 * row_count + 2 * groups + 5,)
             ),
         ],
         flops + 2 * tiles * TILE * TILE * width,
@@ -379,7 +380,7 @@
             pltpu.SemaphoreType.DMA((len(heads) + 7,)),
         ],
         input_output_aliases={0: 0},
-        compiler_params=pltpu.CompilerParams(vmem_limit_bytes=VMEM_LIMIT),
+        compiler_params=pltpu.CompilerParams(vmem_limit_bytes=8 * 2**20),
         cost_estimate=pl.CostEstimate(flops=weights.size, bytes_accessed=8 * weights.size, transcendentals=0),
         name="finish",
     )(grad, local, weights, mine, side, *heads)

time: 68.6 us -> 67.9 us (0.990)
  Pallas kernels: 20.9 us -> 20 us
    unnamed x36 -> x30, local copies, waits for them, and re-layouts: 1.35 us -> 1.54 us
where the time goes in v7:
time: 67.9 us; the launch traced here: 67.5 us
  starting transfers between devices  28.6 us (42%)
  Pallas kernels  20 us (29%)
  waiting for transfers between devices  13.8 us (20%)
  local copies, waits for them, and re-layouts  3.11 us (5%)
  other arithmetic  1 us (1%)
  between operations  0.97 us (1%)
    ppermute x17, starting transfers between devices, trade(): lax.ppermute(value, axis, [(r, r ^ k) for r in range(lax.axis_size(axis))])  21.1 us
    pallas_call x3, Pallas kernels, call(): pl.pallas_call(kernel, in_specs=in_specs, out_specs=out_specs, out_shape=...  18.5 us
    ppermute x17, waiting for transfers between devices, trade(): lax.ppermute(value, axis, [(r, r ^ k) for r in range(lax.axis_size(axis))])  10.2 us
    all_to_all x1, starting transfers between devices, on_device(): lax.all_to_all(parts, everyone, split_axis=0, concat_axis=0, tiled=True)  4.8 us
    all_to_all x1, waiting for transfers between devices, on_device(): lax.all_to_all(parts, everyone, split_axis=0, concat_axis=0, tiled=True)  3.58 us
    all_to_all x1, starting transfers between devices, on_device(): lax.all_to_all(sums, everyone, split_axis=0, concat_axis=0, tiled=True)  2.77 us
    unnamed x30, local copies, waits for them, and re-layouts  1.54 us
    pallas_call x1, Pallas kernels, finish(): pl.pallas_call(finish_kernel, in_specs=[ANY] * (5 + len(heads)), out_spec...  1.5 us
  transfers between devices with their start and end apart: 19, of which 7 were waited for; matrix products, arithmetic and copies ran while one was open for 3% of the time, Pallas kernels for 12%

profile of v7, /device:TPU:0, one launch (start us, length us, event | category | flops | bytes accessed | tf_op | source)
XLA Modules:
  0.0 67.5 jit_solution(8063048323471163415)
XLA Ops:
  0.6 0.8 %slice.12 = bf16[128,256]{1,0:T(8,128)(2,1)S(1)} slice(bf16[2048,256]{1,0:T(8,128)(2,1)} %refs_5_.1), slice={[0:128], [0:256]} | slice | bytes 131072 | tf_op jit(solution)/shard_map/slice | solution.py:414
  1.5 3.0 %collective-permute-start.1 = (bf16[128,256]{1,0:T(8,128)(2,1)S(1)}, bf16[128,256]{1,0:T(8,128)(2,1)S(1)}, u32[]{:S(2)}, u32[]{:S(2)}) collective-permute-start(bf16[128,256]{1,0:T(8,128)(2,1)S(1)} %slice.12), channel_id=1, source_target_pairs={{0,2},{1,3},{2,0},{3,1},{4,6},{5,7},{6,4},{7,5},{8,10},{9,11},{10,... | collective-permute-start | bytes 196616 | tf_op jit(solution)/shard_map/ppermute | solution.py:390
  4.5 2.5 %collective-permute-start.5 = (bf16[128,256]{1,0:T(8,128)(2,1)S(1)}, bf16[128,256]{1,0:T(8,128)(2,1)S(1)}, u32[]{:S(2)}, u32[]{:S(2)}) collective-permute-start(bf16[128,256]{1,0:T(8,128)(2,1)S(1)} %slice.12), channel_id=1, source_target_pairs={{0,6},{1,7},{2,4},{3,5},{4,2},{5,3},{6,0},{7,1},{8,14},{9,15},{10,... | collective-permute-start | bytes 196616 | tf_op jit(solution)/shard_map/ppermute | solution.py:390
  7.0 0.1 collective-permute-start.3
  7.1 0.0 collective-permute-done.1.refs_11_
  7.1 2.4 %pick_rows.1 = (bf16[2,64,256]{2,1,0:T(8,128)(2,1)}, bf16[64,256]{1,0:T(8,128)(2,1)}, bf16[64,256]{1,0:T(8,128)(2,1)}) custom-call(s32[1,4,64]{2,1,0:T(4,128)} %refs_2_.1, bf16[2048,256]{1,0:T(8,128)(2,1)} %refs_5_.1), custom_call_target="tpu_custom_call" | custom-call | flops 268435456 | bytes 1048576 | tf_op jit(solution)/shard_map/pick_rows/pallas_call | solution.py:23
  9.5 0.1 collective-permute-start.7
  9.6 1.7 %collective-permute-start.8 = (bf16[64,256]{1,0:T(8,128)(2,1)}, bf16[64,256]{1,0:T(8,128)(2,1)S(1)}, u32[]{:S(2)}, u32[]{:S(2)}) collective-permute-start(bf16[64,256]{1,0:T(8,128)(2,1)} %get-tuple-element.39), channel_id=1, source_target_pairs={{0,16},{8,24},{16,0},{24,8},{1,17},{9,25},{17,1},{25,9},{2,18},{10... | collective-permute-start | bytes 98312 | tf_op jit(solution)/shard_map/ppermute | solution.py:390
  11.3 1.5 %collective-permute-start = (bf16[128,256]{1,0:T(8,128)(2,1)S(1)}, bf16[128,256]{1,0:T(8,128)(2,1)S(1)}, u32[]{:S(2)}, u32[]{:S(2)}) collective-permute-start(bf16[128,256]{1,0:T(8,128)(2,1)S(1)} %slice.12), channel_id=1, source_target_pairs={{0,1},{1,0},{2,3},{3,2},{4,5},{5,4},{6,7},{7,6},{8,9},{9,8},{10,11... | collective-permute-start | bytes 196616 | tf_op jit(solution)/shard_map/ppermute | solution.py:390
  12.7 0.0 collective-permute-done.5.refs_15_
  12.7 0.5 collective-permute-start.2
  13.3 0.1 collective-permute-done.3.refs_13_
  13.4 1.5 %collective-permute-start.6 = (bf16[128,256]{1,0:T(8,128)(2,1)S(1)}, bf16[128,256]{1,0:T(8,128)(2,1)S(1)}, u32[]{:S(2)}, u32[]{:S(2)}) collective-permute-start(bf16[128,256]{1,0:T(8,128)(2,1)S(1)} %collective-permute-done.5.refs_15_), channel_id=1, source_target_pairs={{0,1},{1,0},{2,3},{3,2},{4,5},{5,4},{6,7},{7,6},{8,9},{9,8},{10,11... | collective-permute-start | bytes 196616 | tf_op jit(solution)/shard_map/ppermute | solution.py:390
  14.9 0.0 collective-permute-done.8.refs_18_
  14.9 0.5 collective-permute-start.4
  15.5 0.0 collective-permute-done.7.refs_19_
  15.5 1.5 %collective-permute-start.9 = (bf16[2,64,256]{2,1,0:T(8,128)(2,1)S(1)}, bf16[2,64,256]{2,1,0:T(8,128)(2,1)S(1)}, u32[]{:S(2)}, u32[]{:S(2)}) collective-permute-start(bf16[2,64,256]{2,1,0:T(8,128)(2,1)S(1)} %collective-permute-done.7.refs_19_), channel_id=1, source_target_pairs={{0,16},{8,24},{16,0},{24,8},{1,17},{9,25},{17,1},{25,9},{2,18},{10... | collective-permute-start | bytes 196616 | tf_op jit(solution)/shard_map/ppermute | solution.py:390
  17.0 0.0 collective-permute-done.refs_10_
  17.0 2.0 %collective-permute-done.6.refs_16_ = bf16[128,256]{1,0:T(8,128)(2,1)S(1)} collective-permute-done((bf16[128,256]{1,0:T(8,128)(2,1)S(1)}, bf16[128,256]{1,0:T(8,128)(2,1)S(1)}, u32[]{:S(2)}, u32[]{:S(2)}) %collective-permute-start.6) | collective-permute-done | bytes 65568 | tf_op jit(solution)/shard_map/ppermute | solution.py:390
  19.0 0.7 %collective-permute-done.4.refs_14_ = bf16[128,256]{1,0:T(8,128)(2,1)S(1)} collective-permute-done((bf16[128,256]{1,0:T(8,128)(2,1)S(1)}, bf16[128,256]{1,0:T(8,128)(2,1)S(1)}, u32[]{:S(2)}, u32[]{:S(2)}) %collective-permute-start.4) | collective-permute-done | bytes 65568 | tf_op jit(solution)/shard_map/ppermute | solution.py:390
  19.8 0.5 copy-done.12
  20.4 0.0 copy-done.10
  20.4 0.0 copy-done.13
  20.4 10.7 %block.1 = (bf16[2048,256]{1,0:T(8,128)(2,1)}, bf16[2048,256]{1,0:T(8,128)(2,1)}, bf16[2048,256]{1,0:T(8,128)(2,1)}, bf16[512,256]{1,0:T(8,128)(2,1)}, bf16[4,12...) custom-call(s32[1,2,64]{2,1,0:T(2,128)} %bitcast.24, ...), custom_call_target="tpu_custom_call" | custom-call | flops 4563402752 | bytes 14680064 | tf_op jit(solution)/shard_map/block/pallas_call | solution.py:23
  31.1 4.8 %all-to-all-start = ((bf16[32,16,256]{2,1,0:T(8,128)(2,1)}), bf16[32,16,256]{2,1,0:T(8,128)(2,1)S(1)}, u32[]{:S(2)}, u32[]{:S(2)}) async-start(bf16[32,16,256]{2,1,0:T(8,128)(2,1)} %bitcast.23), calls=%async_computation | async-start | bytes 524288 | tf_op jit(solution)/shard_map/all_to_all | solution.py:429
  35.9 1.8 %collective-permute-start.13 = (bf16[4,128,256]{2,1,0:T(8,128)(2,1)}, bf16[4,128,256]{2,1,0:T(8,128)(2,1)S(1)}, u32[]{:S(2)}, u32[]{:S(2)}) collective-permute-start(bf16[4,128,256]{2,1,0:T(8,128)(2,1)} %get-tuple-element.59), channel_id=1, source_target_pairs={{0,1},{1,0},{2,3},{3,2},{4,5},{5,4},{6,7},{7,6},{8,9},{9,8},{10,11... | collective-permute-start | bytes 786440 | tf_op jit(solution)/shard_map/ppermute | solution.py:390
  37.8 0.0 collective-permute-start.10
  37.8 1.5 %collective-permute-start.11 = (bf16[64,256]{1,0:T(8,128)(2,1)}, bf16[64,256]{1,0:T(8,128)(2,1)S(1)}, u32[]{:S(2)}, u32[]{:S(2)}) collective-permute-start(bf16[64,256]{1,0:T(8,128)(2,1)} %get-tuple-element.49), channel_id=1, source_target_pairs={{0,16},{8,24},{16,0},{24,8},{1,17},{9,25},{17,1},{25,9},{2,18},{10... | collective-permute-start | bytes 98312 | tf_op jit(solution)/shard_map/ppermute | solution.py:390
  39.2 0.4 collective-permute-start.12
  39.6 2.5 %collective-permute-done.11.refs_8_ = bf16[64,256]{1,0:T(8,128)(2,1)S(1)} collective-permute-done((bf16[64,256]{1,0:T(8,128)(2,1)}, bf16[64,256]{1,0:T(8,128)(2,1)S(1)}, u32[]{:S(2)}, u32[]{:S(2)}) %collective-permute-start.11) | collective-permute-done | bytes 32800 | tf_op jit(solution)/shard_map/ppermute | solution.py:390
  42.1 0.9 %collective-permute-done.12.refs_9_ = bf16[64,256]{1,0:T(8,128)(2,1)S(1)} collective-permute-done((bf16[64,256]{1,0:T(8,128)(2,1)}, bf16[64,256]{1,0:T(8,128)(2,1)S(1)}, u32[]{:S(2)}, u32[]{:S(2)}) %collective-permute-start.12) | collective-permute-done | bytes 32800 | tf_op jit(solution)/shard_map/ppermute | solution.py:390
  43.0 3.6 %all-to-all-done = bf16[32,16,256]{2,1,0:T(8,128)(2,1)S(1)} async-done(((bf16[32,16,256]{2,1,0:T(8,128)(2,1)}), bf16[32,16,256]{2,1,0:T(8,128)(2,1)S(1)}, u32[]{:S(2)}, u32[]{:S(2)}) %all-to-all-start) | async-done | bytes 262176 | tf_op jit(solution)/shard_map/all_to_all | solution.py:429
  46.6 0.1 reduce_sum.12
  46.6 0.7 %broadcast_in_dim.2 = bf16[32,16,256]{2,1,0:T(8,128)(2,1)} broadcast(bf16[16,256]{1,0:T(8,128)(2,1)S(1)} %reduce_sum.12), dimensions={1,2} | broadcast | bytes 270336 | tf_op jit(solution)/shard_map/broadcast_in_dim | solution.py:437
  47.4 2.8 %all-to-all-start.1 = ((bf16[32,16,256]{2,1,0:T(8,128)(2,1)}), bf16[32,16,256]{2,1,0:T(8,128)(2,1)S(1)}, u32[]{:S(2)}, u32[]{:S(2)}) async-start(bf16[32,16,256]{2,1,0:T(8,128)(2,1)} %broadcast_in_dim.2), calls=%async_computation.1 | async-start | bytes 524288 | tf_op jit(solution)/shard_map/all_to_all | solution.py:438
  50.1 0.0 collective-permute-done.13.side_ref
  50.1 1.0 %fusion = (bf16[128,256]{1,0:T(8,128)(2,1)S(1)}, bf16[128,256]{1,0:T(8,128)(2,1)S(1)}, bf16[128,256]{1,0:T(8,128)(2,1)S(1)}) fusion(bf16[128,256]{1,0:T(8,128)(2,1)} %get-tuple-element.62, bf16[4,128,256]{2,1,0:T(8,128)(2,1)S(1)} %collective-permute-done.13.side_ref, bf16[128,256]{1,0:T(8,128)(2,1)} %get-tuple-element.61, bf16[128,256]{1,0:T(8,128)(2,1)} %get-tuple-element.60), kind=kLoop, calls=%fused_computation.1 | loop fusion | flops 393216 | bytes 589824 | tf_op jit(solution)/shard_map/convert_element_type | solution.py:431
  51.1 3.5 %collective-permute-start.16 = (bf16[128,256]{1,0:T(8,128)(2,1)S(1)}, bf16[128,256]{1,0:T(8,128)(2,1)S(1)}, u32[]{:S(2)}, u32[]{:S(2)}) collective-permute-start(bf16[128,256]{1,0:T(8,128)(2,1)S(1)} %get-tuple-element.66), channel_id=1, source_target_pairs={{0,6},{1,7},{2,4},{3,5},{4,2},{5,3},{6,0},{7,1},{8,14},{9,15},{10,... | collective-permute-start | bytes 196616 | tf_op jit(solution)/shard_map/ppermute | solution.py:390
  54.6 0.0 collective-permute-start.15
  54.6 0.9 %collective-permute-start.14 = (bf16[128,256]{1,0:T(8,128)(2,1)S(1)}, bf16[128,256]{1,0:T(8,128)(2,1)S(1)}, u32[]{:S(2)}, u32[]{:S(2)}) collective-permute-start(bf16[128,256]{1,0:T(8,128)(2,1)S(1)} %get-tuple-element.68), channel_id=1, source_target_pairs={{0,2},{1,3},{2,0},{3,1},{4,6},{5,7},{6,4},{7,5},{8,10},{9,11},{10,... | collective-permute-start | bytes 196616 | tf_op jit(solution)/shard_map/ppermute | solution.py:390
  55.6 5.5 %local_backward.1 = (bf16[2048,256]{1,0:T(8,128)(2,1)}, f32[128,256]{1,0:T(8,128)}) custom-call(s32[1,2,64]{2,1,0:T(2,128)} %bitcast.25, bf16[256,256]{1,0:T(8,128)(2,1)} %refs_1_.3, s32[1,4,64]{2,1,0:T(4,128)} %refs_2_.1, bf16[64,128,128]{2,1,0:T(8,128)(2,1)} %bitcast.22, bf16[2048,256]{1,0:T(8,128)(2,1)} %get-tuple-element.44.refs_4_, ...), custom_call_target="tpu_custom_call" | custom-call | flops 1073741824 | bytes 6291456 | tf_op jit(solution)/shard_map/local_backward/pallas_call | solution.py:23
  61.0 0.0 collective-permute-done.16.refs_2_
  61.0 3.9 %collective-permute-done.15.refs_1_ = bf16[128,256]{1,0:T(8,128)(2,1)S(1)} collective-permute-done((bf16[128,256]{1,0:T(8,128)(2,1)S(1)}, bf16[128,256]{1,0:T(8,128)(2,1)S(1)}, u32[]{:S(2)}, u32[]{:S(2)}) %collective-permute-start.15) | collective-permute-done | bytes 65568 | tf_op jit(solution)/shard_map/ppermute | solution.py:390
  64.9 0.0 collective-permute-done.14.refs_0_
  64.9 0.0 all-to-all-done.1
  64.9 0.0 copy-start
  65.0 0.9 %copy-done = f32[128,256]{1,0:T(8,128)S(1)} copy-done((f32[128,256]{1,0:T(8,128)S(1)}, f32[128,256]{1,0:T(8,128)}, u32[]{:S(2)}) %copy-start) | copy-done | bytes 131096
  65.8 1.5 %finish.1 = (bf16[2048,256]{1,0:T(8,128)(2,1)}, f32[256,256]{1,0:T(8,128)}, f32[256,256]{1,0:T(8,128)}) custom-call(bf16[2048,256]{1,0:T(8,128)(2,1)} %get-tuple-element.55.grad_ref, f32[128,256]{1,0:T(8,128)S(1)} %copy-done, bf16[512,256]{1,0:T(8,128)(2,1)S(1)} %bitcast.20, bf16[128,256]{1,0:T(8,128)(2,1)S(1)} %copy-done.1, ...), custom_call_target="tpu_custom_call", output_to_operand_aliasing={{0}: (0, {})} | custom-call | flops 131072 | bytes 1048576 | tf_op jit(solution)/shard_map/finish/pallas_call | solution.py:366
  (28 shorter events, 0.1 us)
Async XLA Ops:
  1.5 5.6 %collective-permute-start.1 = (bf16[128,256]{1,0:T(8,128)(2,1)S(1)}, bf16[128,256]{1,0:T(8,128)(2,1)S(1)}, u32[]{:S(2)}, u32[]{:S(2)}) collective-permute-start(bf16[128,256]{1,0:T(8,128)(2,1)S(1)} %slice.12), channel_id=1, source_target_pairs={{0,2},{1,3},{2,0},{3,1},{4,6},{5,7},{6,4},{7,5},{8,10},{9,11},{10,... | collective-permute-start | bytes 196616 | tf_op jit(solution)/shard_map/ppermute | solution.py:390
  4.5 8.2 %collective-permute-start.5 = (bf16[128,256]{1,0:T(8,128)(2,1)S(1)}, bf16[128,256]{1,0:T(8,128)(2,1)S(1)}, u32[]{:S(2)}, u32[]{:S(2)}) collective-permute-start(bf16[128,256]{1,0:T(8,128)(2,1)S(1)} %slice.12), channel_id=1, source_target_pairs={{0,6},{1,7},{2,4},{3,5},{4,2},{5,3},{6,0},{7,1},{8,14},{9,15},{10,... | collective-permute-start | bytes 196616 | tf_op jit(solution)/shard_map/ppermute | solution.py:390
  7.0 6.4 %collective-permute-start.3 = (bf16[128,256]{1,0:T(8,128)(2,1)S(1)}, bf16[128,256]{1,0:T(8,128)(2,1)S(1)}, u32[]{:S(2)}, u32[]{:S(2)}) collective-permute-start(bf16[128,256]{1,0:T(8,128)(2,1)S(1)} %slice.12), channel_id=1, source_target_pairs={{0,4},{1,5},{2,6},{3,7},{4,0},{5,1},{6,2},{7,3},{8,12},{9,13},{10,... | collective-permute-start | bytes 196616 | tf_op jit(solution)/shard_map/ppermute | solution.py:390
  7.1 12.7 %copy-start.5 = (bf16[128,256]{1,0:T(8,128)(2,1)}, bf16[128,256]{1,0:T(8,128)(2,1)S(1)}, u32[]{:S(2)}) copy-start(bf16[128,256]{1,0:T(8,128)(2,1)S(1)} %collective-permute-done.1.refs_11_) | copy-start | bytes 196612
  9.5 6.0 %collective-permute-start.7 = (bf16[2,64,256]{2,1,0:T(8,128)(2,1)}, bf16[2,64,256]{2,1,0:T(8,128)(2,1)S(1)}, u32[]{:S(2)}, u32[]{:S(2)}) collective-permute-start(bf16[2,64,256]{2,1,0:T(8,128)(2,1)} %get-tuple-element.37), channel_id=1, source_target_pairs={{0,8},{8,0},{16,24},{24,16},{1,9},{9,1},{17,25},{25,17},{2,10},{10... | collective-permute-start | bytes 196616 | tf_op jit(solution)/shard_map/ppermute | solution.py:390
  9.6 5.3 %collective-permute-start.8 = (bf16[64,256]{1,0:T(8,128)(2,1)}, bf16[64,256]{1,0:T(8,128)(2,1)S(1)}, u32[]{:S(2)}, u32[]{:S(2)}) collective-permute-start(bf16[64,256]{1,0:T(8,128)(2,1)} %get-tuple-element.39), channel_id=1, source_target_pairs={{0,16},{8,24},{16,0},{24,8},{1,17},{9,25},{17,1},{25,9},{2,18},{10... | collective-permute-start | bytes 98312 | tf_op jit(solution)/shard_map/ppermute | solution.py:390
  11.3 5.7 %collective-permute-start = (bf16[128,256]{1,0:T(8,128)(2,1)S(1)}, bf16[128,256]{1,0:T(8,128)(2,1)S(1)}, u32[]{:S(2)}, u32[]{:S(2)}) collective-permute-start(bf16[128,256]{1,0:T(8,128)(2,1)S(1)} %slice.12), channel_id=1, source_target_pairs={{0,1},{1,0},{2,3},{3,2},{4,5},{5,4},{6,7},{7,6},{8,9},{9,8},{10,11... | collective-permute-start | bytes 196616 | tf_op jit(solution)/shard_map/ppermute | solution.py:390
  12.7 7.0 %copy-start.6 = (bf16[128,256]{1,0:T(8,128)(2,1)}, bf16[128,256]{1,0:T(8,128)(2,1)S(1)}, u32[]{:S(2)}) copy-start(bf16[128,256]{1,0:T(8,128)(2,1)S(1)} %collective-permute-done.5.refs_15_) | copy-start | bytes 196612
  12.7 7.0 %collective-permute-start.2 = (bf16[128,256]{1,0:T(8,128)(2,1)S(1)}, bf16[128,256]{1,0:T(8,128)(2,1)S(1)}, u32[]{:S(2)}, u32[]{:S(2)}) collective-permute-start(bf16[128,256]{1,0:T(8,128)(2,1)S(1)} %collective-permute-done.1.refs_11_), channel_id=1, source_target_pairs={{0,1},{1,0},{2,3},{3,2},{4,5},{5,4},{6,7},{7,6},{8,9},{9,8},{10,11... | collective-permute-start | bytes 196616 | tf_op jit(solution)/shard_map/ppermute | solution.py:390
  13.4 6.4 %copy-start.7 = (bf16[128,256]{1,0:T(8,128)(2,1)}, bf16[128,256]{1,0:T(8,128)(2,1)S(1)}, u32[]{:S(2)}) copy-start(bf16[128,256]{1,0:T(8,128)(2,1)S(1)} %collective-permute-done.3.refs_13_) | copy-start | bytes 196612
  13.4 5.6 %collective-permute-start.6 = (bf16[128,256]{1,0:T(8,128)(2,1)S(1)}, bf16[128,256]{1,0:T(8,128)(2,1)S(1)}, u32[]{:S(2)}, u32[]{:S(2)}) collective-permute-start(bf16[128,256]{1,0:T(8,128)(2,1)S(1)} %collective-permute-done.5.refs_15_), channel_id=1, source_target_pairs={{0,1},{1,0},{2,3},{3,2},{4,5},{5,4},{6,7},{7,6},{8,9},{9,8},{10,11... | collective-permute-start | bytes 196616 | tf_op jit(solution)/shard_map/ppermute | solution.py:390
  14.9 4.9 %copy-start.14 = (bf16[64,256]{1,0:T(8,128)(2,1)}, bf16[64,256]{1,0:T(8,128)(2,1)S(1)}, u32[]{:S(2)}) copy-start(bf16[64,256]{1,0:T(8,128)(2,1)S(1)} %collective-permute-done.8.refs_18_) | copy-start | bytes 98308
  14.9 4.8 %collective-permute-start.4 = (bf16[128,256]{1,0:T(8,128)(2,1)S(1)}, bf16[128,256]{1,0:T(8,128)(2,1)S(1)}, u32[]{:S(2)}, u32[]{:S(2)}) collective-permute-start(bf16[128,256]{1,0:T(8,128)(2,1)S(1)} %collective-permute-done.3.refs_13_), channel_id=1, source_target_pairs={{0,1},{1,0},{2,3},{3,2},{4,5},{5,4},{6,7},{7,6},{8,9},{9,8},{10,11... | collective-permute-start | bytes 196616 | tf_op jit(solution)/shard_map/ppermute | solution.py:390
  15.5 4.3 %copy-start.8 = (bf16[2,64,256]{2,1,0:T(8,128)(2,1)}, bf16[2,64,256]{2,1,0:T(8,128)(2,1)S(1)}, u32[]{:S(2)}) copy-start(bf16[2,64,256]{2,1,0:T(8,128)(2,1)S(1)} %collective-permute-done.7.refs_19_) | copy-start | bytes 196612
  15.5 4.3 %collective-permute-start.9 = (bf16[2,64,256]{2,1,0:T(8,128)(2,1)S(1)}, bf16[2,64,256]{2,1,0:T(8,128)(2,1)S(1)}, u32[]{:S(2)}, u32[]{:S(2)}) collective-permute-start(bf16[2,64,256]{2,1,0:T(8,128)(2,1)S(1)} %collective-permute-done.7.refs_19_), channel_id=1, source_target_pairs={{0,16},{8,24},{16,0},{24,8},{1,17},{9,25},{17,1},{25,9},{2,18},{10... | collective-permute-start | bytes 196616 | tf_op jit(solution)/shard_map/ppermute | solution.py:390
  17.0 2.8 %copy-start.9 = (bf16[128,256]{1,0:T(8,128)(2,1)}, bf16[128,256]{1,0:T(8,128)(2,1)S(1)}, u32[]{:S(2)}) copy-start(bf16[128,256]{1,0:T(8,128)(2,1)S(1)} %collective-permute-done.refs_10_) | copy-start | bytes 196612
  19.0 0.8 %copy-start.11 = (bf16[128,256]{1,0:T(8,128)(2,1)}, bf16[128,256]{1,0:T(8,128)(2,1)S(1)}, u32[]{:S(2)}) copy-start(bf16[128,256]{1,0:T(8,128)(2,1)S(1)} %collective-permute-done.6.refs_16_) | copy-start | bytes 196612
  19.7 0.6 copy-start.12
  19.7 0.6 copy-start.10
  19.7 0.7 %copy-start.13 = (bf16[2,64,256]{2,1,0:T(8,128)(2,1)}, bf16[2,64,256]{2,1,0:T(8,128)(2,1)S(1)}, u32[]{:S(2)}) copy-start(bf16[2,64,256]{2,1,0:T(8,128)(2,1)S(1)} %collective-permute-done.9.refs_20_) | copy-start | bytes 196612
  31.1 33.8 %copy-start.1 = (bf16[128,256]{1,0:T(8,128)(2,1)S(1)}, bf16[128,256]{1,0:T(8,128)(2,1)}, u32[]{:S(2)}) copy-start(bf16[128,256]{1,0:T(8,128)(2,1)} %get-tuple-element.58.mine_ref) | copy-start | bytes 196612
  31.1 15.5 %all-to-all-start = ((bf16[32,16,256]{2,1,0:T(8,128)(2,1)}), bf16[32,16,256]{2,1,0:T(8,128)(2,1)S(1)}, u32[]{:S(2)}, u32[]{:S(2)}) async-start(bf16[32,16,256]{2,1,0:T(8,128)(2,1)} %bitcast.23), calls=%async_computation | async-start | bytes 524288 | tf_op jit(solution)/shard_map/all_to_all | solution.py:429
  35.9 14.2 %collective-permute-start.13 = (bf16[4,128,256]{2,1,0:T(8,128)(2,1)}, bf16[4,128,256]{2,1,0:T(8,128)(2,1)S(1)}, u32[]{:S(2)}, u32[]{:S(2)}) collective-permute-start(bf16[4,128,256]{2,1,0:T(8,128)(2,1)} %get-tuple-element.59), channel_id=1, source_target_pairs={{0,1},{1,0},{2,3},{3,2},{4,5},{5,4},{6,7},{7,6},{8,9},{9,8},{10,11... | collective-permute-start | bytes 786440 | tf_op jit(solution)/shard_map/ppermute | solution.py:390
  37.8 1.9 %collective-permute-start.10 = (bf16[64,256]{1,0:T(8,128)(2,1)}, bf16[64,256]{1,0:T(8,128)(2,1)S(1)}, u32[]{:S(2)}, u32[]{:S(2)}) collective-permute-start(bf16[64,256]{1,0:T(8,128)(2,1)} %get-tuple-element.48), channel_id=1, source_target_pairs={{0,8},{8,0},{16,24},{24,16},{1,9},{9,1},{17,25},{25,17},{2,10},{10... | collective-permute-start | bytes 98312 | tf_op jit(solution)/shard_map/ppermute | solution.py:390
  37.8 4.3 %collective-permute-start.11 = (bf16[64,256]{1,0:T(8,128)(2,1)}, bf16[64,256]{1,0:T(8,128)(2,1)S(1)}, u32[]{:S(2)}, u32[]{:S(2)}) collective-permute-start(bf16[64,256]{1,0:T(8,128)(2,1)} %get-tuple-element.49), channel_id=1, source_target_pairs={{0,16},{8,24},{16,0},{24,8},{1,17},{9,25},{17,1},{25,9},{2,18},{10... | collective-permute-start | bytes 98312 | tf_op jit(solution)/shard_map/ppermute | solution.py:390
  39.2 3.8 %collective-permute-start.12 = (bf16[64,256]{1,0:T(8,128)(2,1)}, bf16[64,256]{1,0:T(8,128)(2,1)S(1)}, u32[]{:S(2)}, u32[]{:S(2)}) collective-permute-start(bf16[64,256]{1,0:T(8,128)(2,1)} %get-tuple-element.50), channel_id=1, source_target_pairs={{0,24},{8,16},{16,8},{24,0},{1,25},{9,17},{17,9},{25,1},{2,26},{10... | collective-permute-start | bytes 98312 | tf_op jit(solution)/shard_map/ppermute | solution.py:390
  39.6 15.9 %copy-start.2 = (bf16[64,256]{1,0:T(8,128)(2,1)}, bf16[64,256]{1,0:T(8,128)(2,1)S(1)}, u32[]{:S(2)}) copy-start(bf16[64,256]{1,0:T(8,128)(2,1)S(1)} %collective-permute-done.10.refs_7_) | copy-start | bytes 98308
  42.1 13.4 %copy-start.3 = (bf16[64,256]{1,0:T(8,128)(2,1)}, bf16[64,256]{1,0:T(8,128)(2,1)S(1)}, u32[]{:S(2)}) copy-start(bf16[64,256]{1,0:T(8,128)(2,1)S(1)} %collective-permute-done.11.refs_8_) | copy-start | bytes 98308
  43.0 12.6 %copy-start.4 = (bf16[64,256]{1,0:T(8,128)(2,1)}, bf16[64,256]{1,0:T(8,128)(2,1)S(1)}, u32[]{:S(2)}) copy-start(bf16[64,256]{1,0:T(8,128)(2,1)S(1)} %collective-permute-done.12.refs_9_) | copy-start | bytes 98308
  47.4 17.6 %all-to-all-start.1 = ((bf16[32,16,256]{2,1,0:T(8,128)(2,1)}), bf16[32,16,256]{2,1,0:T(8,128)(2,1)S(1)}, u32[]{:S(2)}, u32[]{:S(2)}) async-start(bf16[32,16,256]{2,1,0:T(8,128)(2,1)} %broadcast_in_dim.2), calls=%async_computation.1 | async-start | bytes 524288 | tf_op jit(solution)/shard_map/all_to_all | solution.py:438
  51.1 9.9 %collective-permute-start.16 = (bf16[128,256]{1,0:T(8,128)(2,1)S(1)}, bf16[128,256]{1,0:T(8,128)(2,1)S(1)}, u32[]{:S(2)}, u32[]{:S(2)}) collective-permute-start(bf16[128,256]{1,0:T(8,128)(2,1)S(1)} %get-tuple-element.66), channel_id=1, source_target_pairs={{0,6},{1,7},{2,4},{3,5},{4,2},{5,3},{6,0},{7,1},{8,14},{9,15},{10,... | collective-permute-start | bytes 196616 | tf_op jit(solution)/shard_map/ppermute | solution.py:390
  54.6 10.3 %collective-permute-start.15 = (bf16[128,256]{1,0:T(8,128)(2,1)S(1)}, bf16[128,256]{1,0:T(8,128)(2,1)S(1)}, u32[]{:S(2)}, u32[]{:S(2)}) collective-permute-start(bf16[128,256]{1,0:T(8,128)(2,1)S(1)} %get-tuple-element.67), channel_id=1, source_target_pairs={{0,4},{1,5},{2,6},{3,7},{4,0},{5,1},{6,2},{7,3},{8,12},{9,13},{10,... | collective-permute-start | bytes 196616 | tf_op jit(solution)/shard_map/ppermute | solution.py:390
  54.6 10.3 %collective-permute-start.14 = (bf16[128,256]{1,0:T(8,128)(2,1)S(1)}, bf16[128,256]{1,0:T(8,128)(2,1)S(1)}, u32[]{:S(2)}, u32[]{:S(2)}) collective-permute-start(bf16[128,256]{1,0:T(8,128)(2,1)S(1)} %get-tuple-element.68), channel_id=1, source_target_pairs={{0,2},{1,3},{2,0},{3,1},{4,6},{5,7},{6,4},{7,5},{8,10},{9,11},{10,... | collective-permute-start | bytes 196616 | tf_op jit(solution)/shard_map/ppermute | solution.py:390
  64.9 0.9 %copy-start = (f32[128,256]{1,0:T(8,128)S(1)}, f32[128,256]{1,0:T(8,128)}, u32[]{:S(2)}) copy-start(f32[128,256]{1,0:T(8,128)} %get-tuple-element.56.local_ref) | copy-start | bytes 393220
